TPU v7x, 32 devices: a whole 2x2x4 slice. The times are simulated.
32 devices in a mesh: fsdp: 8 (over y, x, core), dp: 4 (over z).
Axes of the slice: x: 2, y: 2, z: 4, core: 2. Of those that a mesh axis runs over, the one named last changes fastest.
Arguments:
- hidden_in: bfloat16 [16384, 768], P(('fsdp', 'dp')), may hold values from -6 to 6
- norm_gain_attn: bfloat16 [768], P('fsdp'), may hold values from 0.5 to 1.5
- w_query: bfloat16 [768, 768], P('fsdp'), may hold values from -0.02734375 to 0.02734375
- w_key: bfloat16 [768, 768], P('fsdp'), may hold values from -0.21875 to 0.21875
- w_value: bfloat16 [768, 768], P('fsdp'), may hold values from -0.21875 to 0.21875
- w_out: bfloat16 [768, 768], P('fsdp'), may hold values from -1.75 to 1.75
- rel_bias: bfloat16 [32, 12], P('fsdp'), may hold values from -6 to 6
- norm_gain_ffn: bfloat16 [768], P('fsdp'), may hold values from 0.5 to 1.5
- w_in: bfloat16 [768, 3072], P('fsdp'), may hold values from -0.21875 to 0.21875
- w_ffout: bfloat16 [3072, 768], P('fsdp'), may hold values from -0.109375 to 0.109375
- bucket_index: int32 [1023], replicated, may hold values from 0 to 31
- row_lengths: int32 [32], P(('fsdp', 'dp')), may hold values from 80 to 512, as said below
- prefix_lengths: int32 [32], P(('fsdp', 'dp')), may hold values from 5 to 40
- out_cotangent: bfloat16 [16384, 768], P(('fsdp', 'dp')), may hold values from -12 to 12
- pool_cotangent: float32 [32, 768], P(('fsdp', 'dp')), may hold values from -768 to 768
Outputs:
- hidden_out: bfloat16 [16384, 768], P(('fsdp', 'dp'))
- pooled: float32 [32, 768], P(('fsdp', 'dp'))
- grad_hidden: float32 [16384, 768], P(('fsdp', 'dp'))
- grad_gain_attn: float32 [768], P('fsdp')
- grad_query: float32 [768, 768], P('fsdp')
- grad_key: float32 [768, 768], P('fsdp')
- grad_value: float32 [768, 768], P('fsdp')
- grad_out: float32 [768, 768], P('fsdp')
- grad_rel: float32 [32, 12], P('fsdp')
- grad_gain_ffn: float32 [768], P('fsdp')
- grad_in: float32 [768, 3072], P('fsdp')
- grad_ffout: float32 [3072, 768], P('fsdp')
- token_root_mean_square: float32 [32, 3], P(('fsdp', 'dp'))
Inputs may be any that keep to these rules, and one draw needn't show every extreme that they name: `row_lengths`: some sequence has exactly 512 live tokens.
All inputs are finite; a program needn't handle non-finite values.
Results may differ from a plain program's by a relative error of at most 0.019.
Values may be sent and summed in bfloat16 or wider, within the bound.
No kernel may reach another device: no remote copies, remote signals or barrier semaphores. Data moves between devices by JAX's collectives and lax.ppermute only.
A program may use at most 128 MiB of HBM per device.

v0:
```python
import jax
import jax.numpy as jnp
from jax import lax
from jax.sharding import PartitionSpec as P

epsilon = 1e-06
masked_score = -1e30


def rms_norm(values, gain_vec):
    inv_rms = lax.rsqrt(jnp.mean(values * values, axis=-1, keepdims=True) + epsilon)
    return values * inv_rms * gain_vec


def trans_right(left, right):
    return lax.dot_general(
        left, right, (((1,), (1,)), ((), ())), preferred_element_type=jnp.float32
    )


def trans_left(left, right):
    return lax.dot_general(
        left, right, (((0,), (0,)), ((), ())), preferred_element_type=jnp.float32
    )


def bucket_onehot(bucket_index, sequence_length, bucket_count):
    padded = jnp.concatenate([bucket_index, jnp.zeros((1,), jnp.int32)])
    tiled = jnp.broadcast_to(padded[None, :], (sequence_length, 2 * sequence_length)).reshape(-1)
    span = 2 * sequence_length - 1
    skewed = lax.slice(
        tiled, (sequence_length - 1,), (sequence_length - 1 + sequence_length * span,)
    )
    chosen = skewed.reshape(sequence_length, span)[:, :sequence_length]
    levels = lax.broadcasted_iota(jnp.int32, (bucket_count, sequence_length, sequence_length), 0)
    return (chosen[None, :, :] == levels).astype(jnp.bfloat16)


def masked_scores(queries, key_rows, length, pos_bias):
    scores = (
        jnp.einsum("ihd,jhd->hij", queries, key_rows, preferred_element_type=jnp.float32) + pos_bias
    )
    allowed = lax.broadcasted_iota(jnp.int32, scores.shape, 2) < length
    return jnp.where(allowed, scores, masked_score)


def attend_forward(queries, key_rows, value_rows, length, pos_bias):
    scores = masked_scores(queries, key_rows, length, pos_bias)
    row_max = jnp.max(scores, axis=-1, keepdims=True)
    powers = jnp.exp(scores - row_max)
    row_sum = jnp.sum(powers, axis=-1, keepdims=True)
    attn_probs = powers / row_sum
    attended = jnp.einsum(
        "hij,jhd->ihd",
        attn_probs.astype(jnp.bfloat16),
        value_rows,
        preferred_element_type=jnp.float32,
    )
    return (attended, row_max[..., 0] + jnp.log(row_sum[..., 0]))


def attend_backward(queries, key_rows, value_rows, grad_mix, length, log_sum, pos_bias, onehot):
    scores = masked_scores(queries, key_rows, length, pos_bias)
    attn_probs = jnp.exp(scores - log_sum[..., None])
    grad_probs = jnp.einsum(
        "ihd,jhd->hij", grad_mix, value_rows, preferred_element_type=jnp.float32
    )
    grad_values = jnp.einsum(
        "hij,ihd->jhd",
        attn_probs.astype(jnp.bfloat16),
        grad_mix,
        preferred_element_type=jnp.float32,
    )
    inner = jnp.sum(attn_probs * grad_probs, axis=-1, keepdims=True)
    grad_scores = (attn_probs * (grad_probs - inner)).astype(jnp.bfloat16)
    grad_queries = jnp.einsum(
        "hij,jhd->ihd", grad_scores, key_rows, preferred_element_type=jnp.float32
    )
    grad_keys = jnp.einsum("hij,ihd->jhd", grad_scores, queries, preferred_element_type=jnp.float32)
    grad_table = jnp.einsum("hij,bij->bh", grad_scores, onehot, preferred_element_type=jnp.float32)
    return (
        grad_queries.astype(jnp.bfloat16),
        grad_keys.astype(jnp.bfloat16),
        grad_values.astype(jnp.bfloat16),
        grad_table,
    )


def body(
    hidden_in,
    norm_gain_attn,
    w_query,
    w_key,
    w_value,
    w_out,
    rel_bias,
    norm_gain_ffn,
    w_in,
    w_ffout,
    bucket_index,
    row_lengths,
    prefix_lengths,
    out_cotangent,
    pool_cotangent,
):
    sequence_count = row_lengths.shape[0]
    sequence_length = (bucket_index.shape[0] + 1) // 2
    tok_count = sequence_count * sequence_length
    embedding_width = hidden_in.shape[1]
    gain_attn, query_full, key_full, value_full, out_full, table_full = (
        lax.all_gather(norm_gain_attn, "fsdp", axis=0, tiled=True),
        lax.all_gather(w_query, "fsdp", axis=0, tiled=True),
        lax.all_gather(w_key, "fsdp", axis=0, tiled=True),
        lax.all_gather(w_value, "fsdp", axis=0, tiled=True),
        lax.all_gather(w_out, "fsdp", axis=0, tiled=True),
        lax.all_gather(rel_bias, "fsdp", axis=0, tiled=True),
    )
    head_count = table_full.shape[1]
    head_dim = query_full.shape[1] // head_count
    onehot = bucket_onehot(bucket_index, sequence_length, table_full.shape[0])
    pos_bias = jnp.einsum("bij,bh->hij", onehot, table_full, preferred_element_type=jnp.float32)
    inputs = hidden_in.astype(jnp.float32)
    gain_one = gain_attn.astype(jnp.float32)
    normed_attn = rms_norm(inputs, gain_one).astype(jnp.bfloat16)
    queries = jnp.dot(normed_attn, query_full, preferred_element_type=jnp.float32).astype(
        jnp.bfloat16
    )
    key_rows = jnp.dot(normed_attn, key_full, preferred_element_type=jnp.float32).astype(
        jnp.bfloat16
    )
    value_rows = jnp.dot(normed_attn, value_full, preferred_element_type=jnp.float32).astype(
        jnp.bfloat16
    )

    def by_heads(tensor):
        return tensor.reshape(sequence_count, sequence_length, head_count, head_dim)

    def forward_one(seq_items):
        return attend_forward(seq_items[0], seq_items[1], seq_items[2], seq_items[3], pos_bias)

    attended, log_sums = lax.map(
        forward_one, (by_heads(queries), by_heads(key_rows), by_heads(value_rows), row_lengths)
    )
    attended = attended.reshape(tok_count, head_count * head_dim).astype(jnp.bfloat16)
    branch_attn = jnp.dot(attended, out_full, preferred_element_type=jnp.float32)
    residual = inputs + branch_attn
    gain_ffn, in_full, ffout_full = (
        lax.all_gather(norm_gain_ffn, "fsdp", axis=0, tiled=True),
        lax.all_gather(w_in, "fsdp", axis=0, tiled=True),
        lax.all_gather(w_ffout, "fsdp", axis=0, tiled=True),
    )
    gain_two = gain_ffn.astype(jnp.float32)
    normed_ffn = rms_norm(residual, gain_two).astype(jnp.bfloat16)
    pre_act = jnp.dot(normed_ffn, in_full, preferred_element_type=jnp.float32)
    activated = jax.nn.gelu(pre_act).astype(jnp.bfloat16)
    branch_ffn = jnp.dot(activated, ffout_full, preferred_element_type=jnp.float32)
    layer_output = residual + branch_ffn
    positions = lax.broadcasted_iota(jnp.int32, (sequence_count, sequence_length), 1)
    pool_mask = (
        (positions >= prefix_lengths[:, None]) & (positions < row_lengths[:, None])
    ).astype(jnp.float32)
    pooling_weight_rows = pool_mask / jnp.sum(pool_mask, axis=1, keepdims=True)
    pooled = jnp.einsum(
        "jb,jbx->jx",
        pooling_weight_rows,
        layer_output.reshape(sequence_count, sequence_length, embedding_width),
    )
    valid_mask = (positions < row_lengths[:, None]).astype(jnp.float32)
    denominators = row_lengths.astype(jnp.float32) * embedding_width

    def row_measure(tensor):
        squares = jnp.sum(
            (tensor * tensor).reshape(sequence_count, sequence_length, embedding_width), axis=-1
        )
        return jnp.sqrt(jnp.sum(valid_mask * squares, axis=1) / denominators)

    row_stats = jnp.stack(
        [row_measure(inputs), row_measure(branch_attn), row_measure(branch_ffn)], axis=-1
    )
    gain_ffn, in_full, ffout_full = (
        lax.all_gather(norm_gain_ffn, "fsdp", axis=0, tiled=True),
        lax.all_gather(w_in, "fsdp", axis=0, tiled=True),
        lax.all_gather(w_ffout, "fsdp", axis=0, tiled=True),
    )
    gain_attn, query_full, key_full, value_full, out_full, table_full = (
        lax.all_gather(norm_gain_attn, "fsdp", axis=0, tiled=True),
        lax.all_gather(w_query, "fsdp", axis=0, tiled=True),
        lax.all_gather(w_key, "fsdp", axis=0, tiled=True),
        lax.all_gather(w_value, "fsdp", axis=0, tiled=True),
        lax.all_gather(w_out, "fsdp", axis=0, tiled=True),
        lax.all_gather(rel_bias, "fsdp", axis=0, tiled=True),
    )
    gain_two = gain_ffn.astype(jnp.float32)
    gain_one = gain_attn.astype(jnp.float32)
    pos_bias = jnp.einsum("bij,bh->hij", onehot, table_full, preferred_element_type=jnp.float32)
    pool_terms = pooling_weight_rows[:, :, None] * pool_cotangent[:, None, :]
    output_gradient = out_cotangent.astype(jnp.float32) + pool_terms.reshape(
        tok_count, embedding_width
    )
    low_output = output_gradient.astype(jnp.bfloat16)
    grad_activated = trans_right(low_output, ffout_full)
    grad_ffout_local = trans_left(activated, low_output)
    gelu_pull = jax.vjp(jax.nn.gelu, pre_act)[1]
    grad_pre = gelu_pull(grad_activated)[0].astype(jnp.bfloat16)
    grad_in_local = trans_left(normed_ffn, grad_pre)
    grad_normed_ffn = trans_right(grad_pre, in_full)
    norm_two_pull = jax.vjp(rms_norm, residual, gain_two)[1]
    resid_extra, grad_gain_two = norm_two_pull(grad_normed_ffn)
    grad_residual = output_gradient + resid_extra
    ffn_gain_share, ffn_in_share, ffn_out_share = (
        lax.psum_scatter(
            grad_gain_two.astype(jnp.bfloat16), "fsdp", scatter_dimension=0, tiled=True
        ).astype(jnp.float32),
        lax.psum_scatter(
            grad_in_local.astype(jnp.bfloat16), "fsdp", scatter_dimension=0, tiled=True
        ).astype(jnp.float32),
        lax.psum_scatter(
            grad_ffout_local.astype(jnp.bfloat16), "fsdp", scatter_dimension=0, tiled=True
        ).astype(jnp.float32),
    )
    grad_gain_ffn, grad_in, grad_ffout = (
        lax.psum(ffn_gain_share.astype(jnp.bfloat16), "dp").astype(jnp.float32),
        lax.psum(ffn_in_share.astype(jnp.bfloat16), "dp").astype(jnp.float32),
        lax.psum(ffn_out_share.astype(jnp.bfloat16), "dp").astype(jnp.float32),
    )
    low_residual = grad_residual.astype(jnp.bfloat16)
    grad_out_local = trans_left(attended, low_residual)
    grad_attended = trans_right(low_residual, out_full).astype(jnp.bfloat16)

    def backward_one(seq_items):
        return attend_backward(
            seq_items[0],
            seq_items[1],
            seq_items[2],
            seq_items[3],
            seq_items[4],
            seq_items[5],
            pos_bias,
            onehot,
        )

    grad_queries, grad_keys, grad_values, grad_tables = lax.map(
        backward_one,
        (
            by_heads(queries),
            by_heads(key_rows),
            by_heads(value_rows),
            by_heads(grad_attended),
            row_lengths,
            log_sums,
        ),
    )
    grad_queries = grad_queries.reshape(tok_count, head_count * head_dim)
    grad_keys = grad_keys.reshape(tok_count, head_count * head_dim)
    grad_values = grad_values.reshape(tok_count, head_count * head_dim)
    grad_table_local = jnp.sum(grad_tables, axis=0)
    grad_query_local = trans_left(normed_attn, grad_queries)
    grad_key_local = trans_left(normed_attn, grad_keys)
    grad_value_local = trans_left(normed_attn, grad_values)
    grad_normed_attn = (
        trans_right(grad_queries, query_full)
        + trans_right(grad_keys, key_full)
        + trans_right(grad_values, value_full)
    )
    norm_one_pull = jax.vjp(rms_norm, inputs, gain_one)[1]
    input_extra, grad_gain_one = norm_one_pull(grad_normed_attn)
    grad_hidden = grad_residual + input_extra
    gain_share, query_share, key_share, value_share, out_share, table_share = (
        lax.psum_scatter(
            grad_gain_one.astype(jnp.bfloat16), "fsdp", scatter_dimension=0, tiled=True
        ).astype(jnp.float32),
        lax.psum_scatter(
            grad_query_local.astype(jnp.bfloat16), "fsdp", scatter_dimension=0, tiled=True
        ).astype(jnp.float32),
        lax.psum_scatter(
            grad_key_local.astype(jnp.bfloat16), "fsdp", scatter_dimension=0, tiled=True
        ).astype(jnp.float32),
        lax.psum_scatter(
            grad_value_local.astype(jnp.bfloat16), "fsdp", scatter_dimension=0, tiled=True
        ).astype(jnp.float32),
        lax.psum_scatter(
            grad_out_local.astype(jnp.bfloat16), "fsdp", scatter_dimension=0, tiled=True
        ).astype(jnp.float32),
        lax.psum_scatter(
            grad_table_local.astype(jnp.bfloat16), "fsdp", scatter_dimension=0, tiled=True
        ).astype(jnp.float32),
    )
    grad_gain_attn, grad_query, grad_key, grad_value, grad_out, grad_rel = (
        lax.psum(gain_share.astype(jnp.bfloat16), "dp").astype(jnp.float32),
        lax.psum(query_share.astype(jnp.bfloat16), "dp").astype(jnp.float32),
        lax.psum(key_share.astype(jnp.bfloat16), "dp").astype(jnp.float32),
        lax.psum(value_share.astype(jnp.bfloat16), "dp").astype(jnp.float32),
        lax.psum(out_share.astype(jnp.bfloat16), "dp").astype(jnp.float32),
        lax.psum(table_share.astype(jnp.bfloat16), "dp").astype(jnp.float32),
    )
    return (
        layer_output.astype(jnp.bfloat16),
        pooled,
        grad_hidden,
        grad_gain_attn,
        grad_query,
        grad_key,
        grad_value,
        grad_out,
        grad_rel,
        grad_gain_ffn,
        grad_in,
        grad_ffout,
        row_stats,
    )


def solution(mesh):
    return jax.shard_map(
        body,
        mesh=mesh,
        in_specs=(
            P(("fsdp", "dp"), None),
            P("fsdp"),
            P("fsdp", None),
            P("fsdp", None),
            P("fsdp", None),
            P("fsdp", None),
            P("fsdp", None),
            P("fsdp"),
            P("fsdp", None),
            P("fsdp", None),
            P(),
            P(("fsdp", "dp")),
            P(("fsdp", "dp")),
            P(("fsdp", "dp"), None),
            P(("fsdp", "dp"), None),
        ),
        out_specs=(
            P(("fsdp", "dp"), None),
            P(("fsdp", "dp"), None),
            P(("fsdp", "dp"), None),
            P("fsdp"),
            P("fsdp", None),
            P("fsdp", None),
            P("fsdp", None),
            P("fsdp", None),
            P("fsdp", None),
            P("fsdp"),
            P("fsdp", None),
            P("fsdp", None),
            P(("fsdp", "dp"), None),
        ),
        check_vma=False,
    )
```

profile of v0, /device:TPU:0, one launch (start us, length us, event | category | flops | bytes accessed | tf_op | source)
XLA Modules:
  0.0 593.3 jit_solution(16502491710129506685)
XLA Ops:
  14.3 15.2 %all-reduce.6 = (bf16[768]{0:T(1024)(128)(2,1)S(1)}, bf16[768]{0:T(1024)(128)(2,1)S(1)}) all-reduce(bf16[768]{0:T(1024)(128)(2,1)S(1)} %dynamic-update-slice, bf16[768]{0:T(1024)(128)(2,1)S(1)} %dynamic-update-slice.1), channel_id=1, replica_groups=mesh['fsdp'=8,'dp'=4] {'fsdp'}, use_global_device_ids=true, to_apply=%add | all-reduce | flops 1536 | bytes 6144
  35.0 8.1 %all-gather = bf16[8,4,12]{2,1,0:T(4,128)(2,1)S(1)} all-gather(bf16[1,4,12]{2,1,0:T(4,128)(2,1)S(1)} %bitcast.104), channel_id=1, replica_groups=mesh['fsdp'=8,'dp'=4] {'fsdp'}, dimensions={0}, use_global_device_ids=true | all-gather | bytes 864 | tf_op jit(solution)/shard_map/all_gather | solution.py:116
  43.1 9.2 %fusion.1 = f32[512,512,12]{1,2,0:T(8,128)} fusion(bf16[32,12,1]{1,0,2:T(8,128)(2,1)S(1)} %bitcast.102, s32[512,512]{1,0:T(8,128)S(1)} %slice.9), kind=kOutput, calls=%fused_computation.2 | convolution fusion | flops 209715200 | bytes 13632256 | tf_op jit(solution)/shard_map/bij,bh->hij/dot_general | solution.py:121
  52.4 17.9 %copy.69 = f32[512,512,12]{0,1,2:T(8,128)} copy(f32[512,512,12]{1,2,0:T(8,128)} %fusion.1) | data formatting | bytes 25165824 | tf_op jit(solution)/shard_map/bij,bh->hij/dot_general | solution.py:121
  76.8 11.9 %all-gather.8.cloned.1.call-done = bf16[768,768]{1,0:T(8,128)(2,1)} async-done(((bf16[96,768]{1,0:T(8,128)(2,1)}), bf16[768,768]{1,0:T(8,128)(2,1)}) %all-gather.8.cloned.1.call-update) | async-done | bytes 1179664 | tf_op jit(solution)/shard_map/all_gather | solution.py:114
  107.7 6.9 %all-gather.14.cloned.1.call-done = bf16[768,768]{1,0:T(8,128)(2,1)} async-done(((bf16[96,768]{1,0:T(8,128)(2,1)}), bf16[768,768]{1,0:T(8,128)(2,1)}) %all-gather.14.cloned.1.call-update) | async-done | bytes 1179664 | tf_op jit(solution)/shard_map/all_gather | solution.py:115
  118.2 37.1 %all-gather.16.cloned.1.call-done = bf16[768,3072]{1,0:T(8,128)(2,1)} async-done(((bf16[96,3072]{1,0:T(8,128)(2,1)}), bf16[768,3072]{1,0:T(8,128)(2,1)}) %all-gather.16.cloned.1.call-update) | async-done | bytes 4718608 | tf_op jit(solution)/shard_map/all_gather | solution.py:149
  155.2 8.2 %fusion.47 = f32[512,3072]{1,0:T(8,128)} fusion(bf16[768,3072]{1,0:T(8,128)(2,1)} %all-gather.16.cloned.1.call-done, f32[512,768]{1,0:T(8,128)} %get-tuple-element.95, f32[768]{0:T(1024)S(1)} %convert_element_type.187, f32[512]{0:T(512)S(1)} %fusion.46), kind=kOutput, calls=%fused_computation.93 | convolution fusion | flops 2417098752 | bytes 12588032 | tf_op jit(solution)/shard_map/dot_general | solution.py:154
  163.4 32.5 %all-gather.18.cloned.1.call-done = bf16[3072,768]{1,0:T(8,128)(2,1)} async-done(((bf16[384,768]{1,0:T(8,128)(2,1)}), bf16[3072,768]{1,0:T(8,128)(2,1)}) %all-gather.18.cloned.1.call-update) | async-done | bytes 4718608 | tf_op jit(solution)/shard_map/all_gather | solution.py:150
  195.9 8.8 %fusion.13 = bf16[512,3072]{1,0:T(8,128)(2,1)S(1)} fusion(f32[512,3072]{1,0:T(8,128)} %fusion.47, bf16[3072,768]{1,0:T(8,128)(2,1)} %all-gather.18.cloned.1.call-done, bf16[512,768]{1,0:T(8,128)(2,1)} %param.28, f32[768]{0:T(1024)S(1)} %reduce.13, f32[512]{0:T(512)S(1)} %fusion.44), kind=kOutput, calls=%fused_computation.22 | convolution fusion | flops 2448949248 | bytes 14947328 | tf_op jit(solution)/shard_map/dot_general | solution.py:16
  224.0 6.6 %fusion.27 = bf16[12,64,512]{2,1,0:T(8,128)(2,1)S(1)} fusion(bf16[512,12,64]{0,2,1:T(8,128)(2,1)S(1)} %bitcast.88, f32[12,512,512]{1,2,0:T(8,128)} %copy-done, f32[12,512]{1,0:T(8,128)S(1)} %log_add_fusion), kind=kOutput, calls=%fused_computation.61 | convolution fusion | flops 409337856 | bytes 14180352 | tf_op jit(solution)/shard_map/while/body/eval_jaxpr/hij,ihd->jhd/dot_general | solution.py:68
  233.5 9.1 %multiply_reduce_fusion = (f32[12,512]{1,0:T(8,128)S(1)}, f32[12,512,512]{1,2,0:T(8,128)}) fusion(f32[12,512,512]{1,2,0:T(8,128)} %copy-done, f32[12,512]{1,0:T(8,128)S(1)} %log_add_fusion, bf16[512,12,64]{0,2,1:T(8,128)(2,1)S(1)} %bitcast.89, bf16[512,12,64]{0,2,1:T(8,128)(2,1)} %bitcast.93), kind=kOutput, calls=%fused_computation.8 | convolution fusion | flops 412084224 | bytes 26787840 | tf_op jit(solution)/shard_map/while/body/eval_jaxpr/ihd,jhd->hij/dot_general | solution.py:65
  242.7 10.0 %multiply_convert_fusion = bf16[12,512,512]{1,2,0:T(8,128)(2,1)S(1)} fusion(f32[12,512,512]{1,2,0:T(8,128)} %get-tuple-element.109, f32[12,512,512]{1,2,0:T(8,128)} %copy-done, f32[12,512]{1,0:T(8,128)S(1)} %get-tuple-element.108, f32[12,512]{1,0:T(8,128)S(1)} %log_add_fusion), kind=kLoop, calls=%fused_computation.7 | loop fusion | flops 12582912 | bytes 31506432 | tf_op jit(solution)/shard_map/while/body/eval_jaxpr/convert_element_type | solution.py:75
  265.4 8.3 %convolution_convert_fusion = bf16[3072,768]{1,0:T(8,128)(2,1)} fusion(bf16[512,768]{1,0:T(8,128)(2,1)S(1)} %copy-done.30, f32[768]{0:T(1024)S(1)} %reduce.13, f32[512]{0:T(512)S(1)} %fusion.44, f32[512,3072]{1,0:T(8,128)} %fusion.47), kind=kOutput, calls=%fused_computation.27 | convolution fusion | flops 2434007040 | bytes 11801600 | tf_op jit(solution)/shard_map/dot_general | solution.py:22
  291.0 9.7 %reduce-scatter.11.cloned.1.call-done = bf16[96,768]{1,0:T(8,128)(2,1)} async-done(((bf16[768,768]{1,0:T(8,128)(2,1)}), bf16[96,768]{1,0:T(8,128)(2,1)}) %reduce-scatter.11.cloned.1.call-update) | async-done | bytes 147472 | tf_op jit(solution)/shard_map/reduce_scatter | solution.py:278
  300.8 40.6 %reduce-scatter.7.cloned.1.call-done = bf16[96,768]{1,0:T(8,128)(2,1)} async-done(((bf16[768,768]{1,0:T(8,128)(2,1)}), bf16[96,768]{1,0:T(8,128)(2,1)}) %reduce-scatter.7.cloned.1.call-update) | async-done | bytes 147472 | tf_op jit(solution)/shard_map/reduce_scatter | solution.py:272
  341.4 40.8 %reduce-scatter.9.cloned.1.call-done = bf16[96,768]{1,0:T(8,128)(2,1)} async-done(((bf16[768,768]{1,0:T(8,128)(2,1)}), bf16[96,768]{1,0:T(8,128)(2,1)}) %reduce-scatter.9.cloned.1.call-update) | async-done | bytes 147472 | tf_op jit(solution)/shard_map/reduce_scatter | solution.py:275
  382.2 57.4 %reduce-scatter.17.cloned.1.call-done = bf16[384,768]{1,0:T(8,128)(2,1)} async-done(((bf16[3072,768]{1,0:T(8,128)(2,1)}), bf16[384,768]{1,0:T(8,128)(2,1)}) %reduce-scatter.17.cloned.1.call-update) | async-done | bytes 589840 | tf_op jit(solution)/shard_map/reduce_scatter | solution.py:217
  439.6 57.6 %reduce-scatter.15.cloned.1.call-done = bf16[96,3072]{1,0:T(8,128)(2,1)} async-done(((bf16[768,3072]{1,0:T(8,128)(2,1)}), bf16[96,3072]{1,0:T(8,128)(2,1)}) %reduce-scatter.15.cloned.1.call-update) | async-done | bytes 589840 | tf_op jit(solution)/shard_map/reduce_scatter | solution.py:214
  497.8 14.6 %copy.75 = bf16[12,512,512]{2,0,1:T(8,128)(2,1)} copy(bf16[12,512,512]{1,2,0:T(8,128)(2,1)} %copy-done.1) | data formatting | bytes 12582912 | tf_op jit(solution)/shard_map/while/body/eval_jaxpr/convert_element_type | solution.py:75
  513.8 6.8 %fusion.32 = bf16[32,12]{1,0:T(8,128)(2,1)S(1)} fusion(bf16[12,512,512]{2,0,1:T(8,128)(2,1)} %copy.75, s32[512,512]{1,0:T(8,128)S(1)} %copy-done.4), kind=kOutput, calls=%fused_computation.66 | convolution fusion | flops 209715584 | bytes 7340800 | tf_op jit(solution)/shard_map/while/body/eval_jaxpr/hij,bij->bh/dot_general | solution.py:80
  520.7 24.3 %all-reduce.5 = (bf16[768]{0:T(1024)(128)(2,1)S(1)}, bf16[32,12]{1,0:T(8,128)(2,1)S(1)}, bf16[768]{0:T(1024)(128)(2,1)S(1)}) all-reduce(bf16[768]{0:T(1024)(128)(2,1)S(1)} %get-tuple-element.65, bf16[32,12]{1,0:T(8,128)(2,1)S(1)} %fusion.32, bf16[768]{0:T(1024)(128)(2,1)S(1)} %get-tuple-element.63), channel_id=2, replica_groups=mesh['fsdp'=8,'dp'=4] {'fsdp'}, use_global_device_ids=true, to_apply=%region_9.10.clone | all-reduce | flops 1920 | bytes 7680
  545.1 11.7 %all-reduce.7 = (bf16[96]{0:T(256)(128)(2,1)S(1)}, bf16[4,12]{1,0:T(4,128)(2,1)S(1)}, bf16[96]{0:T(256)(128)(2,1)S(1)}) all-reduce(bf16[96]{0:T(256)(128)(2,1)S(1)} %dynamic-slice.4, bf16[4,12]{1,0:T(4,128)(2,1)S(1)} %constant_dynamic-slice_fusion, bf16[96]{0:T(256)(128)(2,1)S(1)} %dynamic-slice.8), channel_id=1, replica_groups=mesh['fsdp'=8,'dp'=4] {'dp'}, use_global_device_ids=true, to_apply=%region_10.11 | all-reduce | flops 240 | bytes 960 | tf_op jit(solution)/shard_map/psum | solution.py:289
  563.4 14.3 %all-reduce.11.cloned.1.call-done = (bf16[96,768]{1,0:T(8,128)(2,1)}, bf16[96,768]{1,0:T(8,128)(2,1)}, bf16[96,768]{1,0:T(8,128)(2,1)}, bf16[96,768]{1,0:T(8,128...) async-done(((bf16[96,768]{1,0:T(8,128)(2,1)}, bf16[96,768]{1,0:T(8,128)(2,1)}, bf16[96,768]{1,0:T(8,128)(2,1)}, bf16[96,768]{1,0:T(8,128)(2,1)}, ...) | async-done | bytes 1769488 | tf_op jit(solution)/shard_map/psum | solution.py:290
  (161 shorter events, 104.9 us)
Async XLA Ops:
  7.2 6.6 %copy-start.31 = (bf16[96]{0:T(256)(128)(2,1)S(1)}, bf16[96]{0:T(256)(128)(2,1)}, u32[]{:S(2)}) copy-start(bf16[96]{0:T(256)(128)(2,1)} %param.16) | copy-start | bytes 580
  7.2 6.8 %copy-start.32 = (bf16[96]{0:T(256)(128)(2,1)S(1)}, bf16[96]{0:T(256)(128)(2,1)}, u32[]{:S(2)}) copy-start(bf16[96]{0:T(256)(128)(2,1)} %param.22) | copy-start | bytes 580
  7.2 22.3 %copy-start.23 = (s32[1023]{0:T(1024)S(1)}, s32[1023]{0:T(1024)}, u32[]{:S(2)}) copy-start(s32[1023]{0:T(1024)} %param.25) | copy-start | bytes 12280
  7.2 64.7 %all-gather.10.cloned.1.call-start = ((), (), s32[]{:S(2)}) async-start(), calls=%async_computation.7 | async-start | bytes 1327104 | tf_op jit(solution)/shard_map/all_gather | solution.py:112
  8.0 66.4 %all-gather.12.cloned.1.call-start = ((), (), s32[]{:S(2)}) async-start(), calls=%async_computation.8 | async-start | bytes 1327104 | tf_op jit(solution)/shard_map/all_gather | solution.py:113
  8.7 80.0 %all-gather.8.cloned.1.call-start = ((), (), s32[]{:S(2)}) async-start(), calls=%async_computation.6 | async-start | bytes 1327104 | tf_op jit(solution)/shard_map/all_gather | solution.py:114
  9.4 105.1 %all-gather.14.cloned.1.call-start = ((), (), s32[]{:S(2)}) async-start(), calls=%async_computation.9 | async-start | bytes 1327104 | tf_op jit(solution)/shard_map/all_gather | solution.py:115
  10.0 145.2 %all-gather.16.cloned.1.call-start = ((), (), s32[]{:S(2)}) async-start(), calls=%async_computation.10 | async-start | bytes 5308416 | tf_op jit(solution)/shard_map/all_gather | solution.py:149
  10.6 185.3 %all-gather.18.cloned.1.call-start = ((), (), s32[]{:S(2)}) async-start(), calls=%async_computation.11 | async-start | bytes 5308416 | tf_op jit(solution)/shard_map/all_gather | solution.py:150
  11.2 279.9 %reduce-scatter.13.cloned.1.call-start = ((), (), s32[]{:S(2)}) async-start(), calls=%async_computation.15 | async-start | bytes 1327104 | tf_op jit(solution)/shard_map/reduce_scatter | solution.py:281
  35.0 8.1 %copy-start.3 = (s32[512,512]{1,0:T(8,128)}, s32[512,512]{1,0:T(8,128)S(1)}, u32[]{:S(2)}) copy-start(s32[512,512]{1,0:T(8,128)S(1)} %slice.9) | copy-start | bytes 3145732
  52.4 19.2 %copy-start.24 = (f32[1,768]{1,0:T(1,128)S(1)}, f32[1,768]{1,0:T(1,128)}, u32[]{:S(2)}) copy-start(f32[1,768]{1,0:T(1,128)} %param.29) | copy-start | bytes 9220
  52.4 19.3 %copy-start.2 = (bf16[512,768]{1,0:T(8,128)(2,1)S(1)}, bf16[512,768]{1,0:T(8,128)(2,1)}, u32[]{:S(2)}) copy-start(bf16[512,768]{1,0:T(8,128)(2,1)} %param.15) | copy-start | bytes 2359300
  93.1 8.4 %copy-start.12 = (bf16[512,768]{0,1:T(8,128)(2,1)}, bf16[512,768]{0,1:T(8,128)(2,1)S(1)}, u32[]{:S(2)}) copy-start(bf16[512,768]{0,1:T(8,128)(2,1)S(1)} %copy.65) | copy-start | bytes 2359300
  195.9 8.8 %copy-start.9 = (f32[512,768]{1,0:T(8,128)S(1)}, f32[512,768]{1,0:T(8,128)}, u32[]{:S(2)}) copy-start(f32[512,768]{1,0:T(8,128)} %get-tuple-element.95) | copy-start | bytes 4718596
  195.9 8.8 %copy-start.11 = (bf16[768,3072]{1,0:T(8,128)(2,1)S(1)}, bf16[768,3072]{1,0:T(8,128)(2,1)}, u32[]{:S(2)}) copy-start(bf16[768,3072]{1,0:T(8,128)(2,1)} %all-gather.16.cloned.1.call-done) | copy-start | bytes 14155780
  223.4 77.3 %reduce-scatter.11.cloned.1.call-start = ((), (), s32[]{:S(2)}) async-start(), calls=%async_computation.14 | async-start | bytes 1327104 | tf_op jit(solution)/shard_map/reduce_scatter | solution.py:278
  242.6 98.8 %reduce-scatter.7.cloned.1.call-start = ((), (), s32[]{:S(2)}) async-start(), calls=%async_computation.12 | async-start | bytes 1327104 | tf_op jit(solution)/shard_map/reduce_scatter | solution.py:272
  257.4 124.8 %reduce-scatter.9.cloned.1.call-start = ((), (), s32[]{:S(2)}) async-start(), calls=%async_computation.13 | async-start | bytes 1327104 | tf_op jit(solution)/shard_map/reduce_scatter | solution.py:275
  265.1 174.4 %reduce-scatter.17.cloned.1.call-start = ((), (), s32[]{:S(2)}) async-start(), calls=%async_computation.17 | async-start | bytes 5308416 | tf_op jit(solution)/shard_map/reduce_scatter | solution.py:217
  273.7 223.4 %reduce-scatter.15.cloned.1.call-start = ((), (), s32[]{:S(2)}) async-start(), calls=%async_computation.16 | async-start | bytes 5308416 | tf_op jit(solution)/shard_map/reduce_scatter | solution.py:214
  281.6 296.1 %all-reduce.11.cloned.1.call-start = ((), (), s32[]{:S(2)}) async-start(), calls=%async_computation.18 | async-start | bytes 3538944 | tf_op jit(solution)/shard_map/psum | solution.py:290
  497.8 16.0 %copy-start.4 = (s32[512,512]{1,0:T(8,128)S(1)}, s32[512,512]{1,0:T(8,128)}, u32[]{:S(2)}) copy-start(s32[512,512]{1,0:T(8,128)} %copy-done.3) | copy-start | bytes 3145732
  577.7 6.7 %copy-start.22 = (bf16[96,3072]{1,0:T(8,128)(2,1)S(1)}, bf16[96,3072]{1,0:T(8,128)(2,1)}, u32[]{:S(2)}) copy-start(bf16[96,3072]{1,0:T(8,128)(2,1)} %get-tuple-element.92) | copy-start | bytes 1769476
  (23 other events, 68.3 us)
Sparse Core Ops, SparseCore 0:
  9.9 26.7 all-gather.9
  38.7 24.0 all-gather.11
  64.6 24.0 all-gather.7
  90.5 24.0 all-gather.13
  116.3 38.9 all-gather.15
  157.0 38.9 all-gather.17
  223.6 36.7 reduce-scatter.12
  263.9 36.7 reduce-scatter.10
  304.6 36.7 reduce-scatter.6
  345.4 36.7 reduce-scatter.8
  385.6 53.8 reduce-scatter.16
  443.2 53.8 reduce-scatter.14
  500.0 77.6 all-reduce.10
where the time goes:
time: 598 us; the launch traced here: 593 us
  waiting for transfers between devices  313 us (52%)
  matrix products  118 us (20%)
  blocking collectives  59.2 us (10%)
  local copies, waits for them, and re-layouts  54.4 us (9%)
  other arithmetic  27.3 us (5%)
  between operations  20.7 us (3%)
    reduce_scatter x1, waiting for transfers between devices, body(): lax.psum_scatter(grad_in_local.astype(jnp.bfloat16), 'fsdp', scatter_dime...  57.6 us
    reduce_scatter x1, waiting for transfers between devices, body(): lax.psum_scatter(grad_ffout_local.astype(jnp.bfloat16), 'fsdp', scatter_d...  57.4 us
    reduce_scatter x1, waiting for transfers between devices, body(): lax.psum_scatter(grad_key_local.astype(jnp.bfloat16), 'fsdp', scatter_dim...  40.8 us
    reduce_scatter x1, waiting for transfers between devices, body(): lax.psum_scatter(grad_query_local.astype(jnp.bfloat16), 'fsdp', scatter_d...  40.6 us
    unnamed x2, blocking collectives  39.5 us
    all_gather x1, waiting for transfers between devices, body(): lax.all_gather(w_in, 'fsdp', axis=0, tiled=True)  37.1 us
    all_gather x1, waiting for transfers between devices, body(): lax.all_gather(w_ffout, 'fsdp', axis=0, tiled=True)  32.5 us
    dot_general x6, matrix products, trans_left(): lax.dot_general(left, right, (((0,), (0,)), ((), ())), preferred_element_...  22.5 us
  transfers between devices with their start and end apart: 13, of which 10 were waited for; matrix products, arithmetic and copies ran while one was open for 26% of the time, Pallas kernels for 0%

commit v1 on v0

v1 whole, which is shorter than its diff:
```python
import functools

import jax
import jax.numpy as jnp
from jax import lax
from jax.experimental import pallas as pl
from jax.experimental.pallas import tpu as pltpu
from jax.sharding import PartitionSpec as P

EPS = 1e-06
F32 = jnp.float32
BF16 = jnp.bfloat16
VMEM_LIMIT = 44 * 2**20
GELU_A = 0.7978845608028654
GELU_B = 0.044715


def dot(a, b):
    return lax.dot_general(a, b, (((1,), (0,)), ((), ())), preferred_element_type=F32)


def dot_right(a, b):
    return lax.dot_general(a, b, (((1,), (1,)), ((), ())), preferred_element_type=F32)


def dot_left(a, b):
    return lax.dot_general(a, b, (((0,), (0,)), ((), ())), preferred_element_type=F32)


def iota(shape, dim):
    return lax.broadcasted_iota(jnp.int32, shape, dim)


def call(kernel, name, ins, outs, scratch=(), flops=0, nbytes=0, trans=0):
    spaces = {"v": pltpu.VMEM, "s": pltpu.SMEM, "h": pl.ANY}
    return pl.pallas_call(
        kernel,
        name=name,
        out_shape=[jax.ShapeDtypeStruct(s, d) for s, d, _ in outs],
        in_specs=[pl.BlockSpec(memory_space=spaces[m]) for _, m in ins],
        out_specs=[pl.BlockSpec(memory_space=spaces[m]) for _, _, m in outs],
        scratch_shapes=list(scratch),
        compiler_params=pltpu.CompilerParams(vmem_limit_bytes=VMEM_LIMIT),
        cost_estimate=pl.CostEstimate(flops=flops, bytes_accessed=nbytes, transcendentals=trans),
    )(*[a for a, _ in ins])


def place(meta, pieces, targets, copies, sems):
    handles = []
    for number, (src, row, rows, dst, base, column, unit, far, level) in enumerate(copies):
        start = base
        if unit:
            start = pl.multiple_of(base + unit * jnp.bitwise_xor(meta[level], far), 16)
        width = pieces[src].shape[1]
        handle = pltpu.make_async_copy(
            pieces[src].at[pl.ds(row, rows), :],
            targets[dst].at[pl.ds(start, rows), pl.ds(column, width)],
            sems.at[number],
        )
        handle.start()
        handles.append(handle)
    return handles


def wait_all(handles):
    for handle in handles:
        handle.wait()


def rows_loop(count, step, fn):
    def one(i, carry):
        fn(pl.ds(pl.multiple_of(i * step, step), step))
        return carry

    lax.fori_loop(0, count // step, one, 0)


def prepare_kernel(
    meta, hidden, gain, table, buckets, out_cot, pool_cot, normed, bias, low, table_rows
):
    size = hidden.shape[0]
    length, prefix = meta[4], meta[5]
    count = (length - prefix).astype(F32)

    def rows(ds):
        x = hidden[ds, :].astype(F32)
        inv = lax.rsqrt(jnp.mean(x * x, axis=-1, keepdims=True) + EPS)
        normed[ds, :] = (x * inv * gain[...]).astype(BF16)
        t = iota((128, 1), 0) + ds.start
        pool = jnp.where((t >= prefix) & (t < length), 1.0, 0.0) / count
        low[ds, :] = (out_cot[ds, :].astype(F32) + pool * pool_cot[...]).astype(BF16)

    rows_loop(size, 128, rows)
    span = 2 * size
    hot = (buckets[...] == iota((table.shape[1], span), 0)).astype(BF16)
    table_rows[...] = dot(table[...], hot)
    width = bias.shape[2]

    def head(h, carry):
        row = table_rows[pl.ds(h, 1), :]
        first = jnp.broadcast_to(pltpu.roll(row, span - 127, 1), (8, span))
        sub = iota((8, span), 0)
        block = first
        for k in range(1, 8):
            block = jnp.where(sub == k, pltpu.roll(first, k, 1), block)
        bias[h, 0:8, :] = block[:, :width]
        full = block
        have = 8
        while have < 128:
            more = pltpu.roll(full, have, 1)
            bias[h, have : 2 * have, :] = more[:, :width]
            full = jnp.concatenate([full, more], axis=0)
            have *= 2
        return carry

    lax.fori_loop(0, bias.shape[0], head, 0)


def attend_kernel(copies, n_pieces, *refs):
    meta, normed, bias = refs[:3]
    pieces = refs[3 : 3 + n_pieces]
    q, k, v, attended, powers, inv_sums, wq, wk, wv, scores, sems = refs[3 + n_pieces :]
    handles = place(meta, pieces, (wq, wk, wv), copies, sems)
    wait_all(handles)
    size = normed.shape[0]
    length = meta[4]

    def project(ds):
        x = normed[ds, :]
        q[ds, :] = dot(x, wq[...]).astype(BF16)
        k[ds, :] = dot(x, wk[...]).astype(BF16)
        v[ds, :] = dot(x, wv[...]).astype(BF16)

    rows_loop(size, 256, project)
    lane = iota((1, 128), 1)
    half = lane < 64
    masked = jnp.where(iota((size, 1), 0) < length, 0.0, -1e30).astype(F32)
    strips = size // 128
    inv_sums[...] = jnp.zeros_like(inv_sums)

    def pair(p, carry):
        cols = pl.ds(pl.multiple_of(p * 128, 128), 128)
        qp, kp, vp = q[:, cols].astype(F32), k[:, cols].astype(F32), v[:, cols].astype(F32)
        joined = None
        for side in range(2):
            head = 2 * p + side
            own = half if side == 0 else jnp.logical_not(half)
            spare = lane == (64 if side == 0 else 0)
            qa = jnp.where(own, qp, jnp.where(spare, 1.0, 0.0)).astype(BF16)
            ka = jnp.where(own, kp, jnp.where(spare, masked, 0.0)).astype(BF16)
            va = jnp.where(own, vp, jnp.where(spare, 1.0, 0.0)).astype(BF16)
            top = None
            for a in range(strips):
                rows = slice(128 * a, 128 * a + 128)
                off = 128 * (strips - 1 - a)
                s = dot_right(ka[rows], qa) + bias[head, :, off : off + size]
                scores[rows, :] = s
                peak = jnp.max(s, axis=0, keepdims=True)
                top = peak if top is None else jnp.maximum(top, peak)
            for a in range(strips):
                rows = slice(128 * a, 128 * a + 128)
                powers[head, rows, :] = jnp.exp(scores[rows, :] - top).astype(BF16)
            mixed = dot_left(va, powers[head]).T
            total = jnp.sum(jnp.where(spare, mixed, 0.0), axis=1, keepdims=True)
            inv = 1.0 / total
            inv_sums[...] = jnp.where(lane == head, inv, inv_sums[...])
            mixed = mixed * inv
            joined = mixed if side == 0 else jnp.where(half, joined, mixed)
        attended[:, cols] = joined.astype(BF16)
        return carry

    lax.fori_loop(0, q.shape[1] // 128, pair, 0)


def residual_kernel(copies, n_pieces, *refs):
    meta, hidden, attended, gain = refs[:4]
    pieces = refs[4 : 4 + n_pieces]
    residual, normed, sums, w_out, sems = refs[4 + n_pieces :]
    wait_all(place(meta, pieces, (w_out,), copies, sems))
    size = hidden.shape[0]
    length = meta[4]
    sums[...] = jnp.zeros_like(sums)

    def rows(ds):
        x = hidden[ds, :].astype(F32)
        branch = dot(attended[ds, :], w_out[...])
        live = (iota((256, 1), 0) + ds.start) < length
        sums[0:1, :] += jnp.sum(jnp.where(live, x * x, 0.0), axis=0, keepdims=True)
        sums[1:2, :] += jnp.sum(jnp.where(live, branch * branch, 0.0), axis=0, keepdims=True)
        r = x + branch
        residual[ds, :] = r
        inv = lax.rsqrt(jnp.mean(r * r, axis=-1, keepdims=True) + EPS)
        normed[ds, :] = (r * inv * gain[...]).astype(BF16)

    rows_loop(size, 256, rows)


def scatter_out(meta, scratch, outs, plan, sems):
    handles = []
    for number, (dst, row, rows, unit, far, offset) in enumerate(plan):
        start = offset
        if unit:
            start = pl.multiple_of(offset + unit * jnp.bitwise_xor(meta[1], far), 16)
        handle = pltpu.make_async_copy(
            scratch.at[pl.ds(start, rows), :], outs[dst].at[pl.ds(row, rows), :], sems.at[number]
        )
        handle.start()
        handles.append(handle)
    return handles


def expand_kernel(copies, n_pieces, plan, n_out, *refs):
    meta, x_own, x_peer, low_own, low_peer = refs[:5]
    pieces = refs[5 : 5 + n_pieces]
    activated, slope = refs[5 + n_pieces : 7 + n_pieces]
    outs = refs[7 + n_pieces : 7 + n_pieces + n_out]
    w_in, grads, sems, out_sems = refs[7 + n_pieces + n_out :]
    wait_all(place(meta, pieces, (w_in,), copies, sems))
    size = x_own.shape[0]
    chunk = 512 if w_in.shape[1] % 512 == 0 else 256

    for which, x_ref in enumerate((x_own, x_peer)):

        def rows(ds, which=which, x_ref=x_ref):
            x = x_ref[ds, :]
            for c in range(0, w_in.shape[1], chunk):
                t = dot(x, w_in[:, c : c + chunk])
                square = t * t
                th = jnp.tanh(GELU_A * t * (1.0 + GELU_B * square))
                phi = 0.5 + 0.5 * th
                activated[which, ds, c : c + chunk] = (t * phi).astype(BF16)
                inner = GELU_A + (3.0 * GELU_A * GELU_B) * square
                slope[which, ds, c : c + chunk] = (
                    phi + 0.5 * t * (1.0 - th * th) * inner
                ).astype(BF16)

        rows_loop(size, 256, rows)

    for c in range(0, w_in.shape[1], 256):
        part = dot_left(activated[0, :, c : c + 256], low_own[...])
        part += dot_left(activated[1, :, c : c + 256], low_peer[...])
        grads[c : c + 256, :] = part.astype(BF16)
    wait_all(scatter_out(meta, grads, outs, plan, out_sems))


def contract_kernel(copies, n_pieces, *refs):
    meta, slope, low_own, low_peer = refs[:4]
    pieces = refs[4 : 4 + n_pieces]
    grad_pre, part_own, part_peer, w_in, w_ffout, sems = refs[4 + n_pieces :]
    wait_all(place(meta, pieces, (w_in, w_ffout), copies, sems))
    size = low_own.shape[0]
    chunk = 512 if w_in.shape[1] % 512 == 0 else 256
    for which, (low, part) in ((1, (low_peer, part_peer)), (0, (low_own, part_own))):

        def rows(ds, which=which, low=low, part=part):
            y = low[ds, :]
            total = None
            for c in range(0, w_in.shape[1], chunk):
                g = dot_right(y, w_ffout[c : c + chunk, :])
                g = (slope[which, ds, c : c + chunk].astype(F32) * g).astype(BF16)
                grad_pre[which, ds, c : c + chunk] = g
                t = dot_right(g, w_in[:, c : c + chunk])
                total = t if total is None else total + t
            part[ds, :] = total.astype(part.dtype)

        rows_loop(size, 256, rows)


def outer_kernel(plan, n_out, *refs):
    meta, x_own, x_peer, grad_pre = refs[:4]
    outs = refs[4 : 4 + n_out]
    grads, out_sems = refs[4 + n_out :]
    for c in range(0, grads.shape[0], 256):
        part = dot_left(x_own[:, c : c + 256], grad_pre[0])
        part += dot_left(x_peer[:, c : c + 256], grad_pre[1])
        grads[c : c + 256, :] = part.astype(BF16)
    wait_all(scatter_out(meta, grads, outs, plan, out_sems))


def through_kernel(copies, n_pieces, *refs):
    meta, residual, part, other, out_cot, pool_cot, gain = refs[:7]
    pieces = refs[7 : 7 + n_pieces]
    grad_residual, low_residual, grad_attended, grad_gain, w_out, sems = refs[7 + n_pieces :]
    handles = place(meta, pieces, (w_out,), copies, sems)
    size = residual.shape[0]
    length, prefix = meta[4], meta[5]
    count = (length - prefix).astype(F32)
    grad_gain[...] = jnp.zeros_like(grad_gain)
    wait_all(handles)

    def rows(ds):
        x = residual[ds, :]
        gn = part[ds, :] + other[ds, :].astype(F32)
        inv = lax.rsqrt(jnp.mean(x * x, axis=-1, keepdims=True) + EPS)
        u = gain[...] * gn
        xr = x * inv
        t = iota((128, 1), 0) + ds.start
        pool = jnp.where((t >= prefix) & (t < length), 1.0, 0.0) / count
        go = out_cot[ds, :].astype(F32) + pool * pool_cot[...]
        g = go + inv * (u - xr * jnp.mean(xr * u, axis=-1, keepdims=True))
        grad_gain[...] += jnp.sum(xr * gn, axis=0, keepdims=True)
        grad_residual[ds, :] = g
        lr = g.astype(BF16)
        low_residual[ds, :] = lr
        grad_attended[ds, :] = dot_right(lr, w_out[...]).astype(BF16)

    rows_loop(size, 128, rows)


def attend_back_kernel(*refs):
    meta, q, k, v, powers, grad_att, attended, inv_sums, buckets = refs[:9]
    send, keep, grad_table, grads, slant, diag = refs[9:]
    size, width = q.shape
    pairs = width // 128
    group = pairs // 2
    strips = size // 128
    span = 2 * size
    lane = iota((1, 128), 1)
    half = lane < 64
    diag[...] = jnp.zeros_like(diag)

    def pair(p, slot, out):
        cols = pl.ds(pl.multiple_of(p * 128, 128), 128)
        qp, kp = q[:, cols], k[:, cols]
        vp = v[:, cols].astype(F32)
        do = grad_att[:, cols].astype(F32)
        prod = do * attended[:, cols].astype(F32)
        dq_all = None
        base = pl.multiple_of(slot * 128, 128)
        for side in range(2):
            head = 2 * p + side
            own = half if side == 0 else jnp.logical_not(half)
            one = 64 if side == 0 else 0
            inv = jnp.sum(jnp.where(lane == head, inv_sums[...], 0.0), axis=1, keepdims=True)
            inner = jnp.sum(jnp.where(own, prod, 0.0), axis=1, keepdims=True) * inv
            upper = inner.astype(BF16).astype(F32)
            dos = jnp.where(
                own,
                do * inv,
                jnp.where(lane == one, -upper, jnp.where(lane == one + 1, upper - inner, 0.0)),
            ).astype(BF16)
            ones = (lane == one) | (lane == one + 1)
            va = jnp.where(own, vp, jnp.where(ones, 1.0, 0.0)).astype(BF16)
            slant[...] = jnp.zeros_like(slant)
            for a in range(strips):
                rows = slice(128 * a, 128 * a + 128)
                off = 128 * (strips - 1 - a)
                e = powers[head, rows, :]
                ds = (e.astype(F32) * dot_right(va[rows], dos)).astype(BF16)
                grads[rows, :] = ds
                slant[:, off : off + size] += ds.astype(F32)
                dk = dot(ds, qp).astype(BF16)
                dv = dot(e, dos).astype(BF16)
                kcols = pl.ds(base + width // 2, 128)
                vcols = pl.ds(base + width, 128)
                if side == 1:
                    dk = jnp.where(half, out[rows, kcols].astype(F32), dk.astype(F32)).astype(BF16)
                    dv = jnp.where(half, out[rows, vcols].astype(F32), dv.astype(F32)).astype(BF16)
                out[rows, kcols] = dk
                out[rows, vcols] = dv
            dq = dot_left(kp, grads[...]).T
            dq_all = dq if side == 0 else jnp.where(half, dq_all, dq)
            y = slant[...]
            rest = 64
            while rest >= 1:
                y = y[:rest] + pltpu.roll(y[rest:], span - rest, 1)
                rest //= 2
            diag[pl.ds(head, 1), :] = pltpu.roll(y, 127, 1)
        out[:, pl.ds(base, 128)] = dq_all.astype(BF16)

    mine = meta[2]

    def first(t, carry):
        pair((1 - mine) * group + t, t, send)
        return carry

    def second(t, carry):
        pair(mine * group + t, t, keep)
        return carry

    lax.fori_loop(0, group, first, 0)
    lax.fori_loop(0, group, second, 0)
    hot = (buckets[...] == iota((grad_table.shape[1], span), 0)).astype(F32)
    grad_table[...] = lax.dot_general(
        diag[...],
        hot,
        (((1,), (1,)), ((), ())),
        preferred_element_type=F32,
        precision=lax.Precision.HIGHEST,
    )


def input_kernel(copies, n_pieces, *refs):
    meta, hidden, grad_residual, send, keep, gain = refs[:6]
    pieces = refs[6 : 6 + n_pieces]
    grad_hidden, grad_gain, wq, wk, wv, sems = refs[6 + n_pieces :]
    wait_all(place(meta, pieces, (wq, wk, wv), copies, sems))
    size, width = hidden.shape
    part = width // 2
    mine = meta[2]
    grad_gain[...] = jnp.zeros_like(grad_gain)

    def rows(ds):
        total = None
        for ref, which in ((send, 1 - mine), (keep, mine)):
            cols = pl.ds(pl.multiple_of(which * part, 128), part)
            for n, w in enumerate((wq, wk, wv)):
                t = dot_right(ref[ds, n * part : (n + 1) * part], w[:, cols])
                total = t if total is None else total + t
        x = hidden[ds, :].astype(F32)
        inv = lax.rsqrt(jnp.mean(x * x, axis=-1, keepdims=True) + EPS)
        u = gain[...] * total
        xr = x * inv
        grad_gain[...] += jnp.sum(xr * total, axis=0, keepdims=True)
        grad_hidden[ds, :] = grad_residual[ds, :] + inv * (
            u - xr * jnp.mean(xr * u, axis=-1, keepdims=True)
        )

    rows_loop(size, 256, rows)


def weights_kernel(plan, n_out, *refs):
    meta, x_own, x_peer, keep, got, att_own, att_peer, low_own, low_peer, extra = refs[:10]
    outs = refs[10 : 10 + n_out]
    grads, out_sems = refs[10 + n_out :]
    part = keep.shape[1]
    depth = x_own.shape[1]
    for c in range(0, depth, 256):
        cols = slice(c, c + 256)
        g = dot_left(x_own[:, cols], keep[...]) + dot_left(x_peer[:, cols], got[...])
        grads[cols, 0:part] = g.astype(BF16)
        g = dot_left(att_own[:, cols], low_own[...]) + dot_left(att_peer[:, cols], low_peer[...])
        grads[cols, part:] = g.astype(BF16)
    grads[depth:, :] = extra[...]
    wait_all(scatter_out(meta, grads, outs, plan, out_sems))


def output_kernel(copies, n_pieces, *refs):
    meta, activated = refs[:2]
    pieces = refs[2 : 2 + n_pieces]
    part_own, part_peer, w_ffout, sems = refs[2 + n_pieces :]
    wait_all(place(meta, pieces, (w_ffout,), copies, sems))
    size = part_own.shape[0]
    for which, part in ((1, part_peer), (0, part_own)):

        def rows(ds, which=which, part=part):
            part[ds, :] = dot(activated[which, ds, :], w_ffout[...]).astype(part.dtype)

        rows_loop(size, 256, rows)


def finish_kernel(meta, residual, part, other, sums, hidden_out, pooled, stats):
    size, width = residual.shape
    length, prefix = meta[4], meta[5]
    count = (length - prefix).astype(F32)
    pooled[...] = jnp.zeros_like(pooled)
    stats[...] = jnp.zeros_like(stats)

    def rows(ds):
        branch = part[ds, :] + other[ds, :].astype(F32)
        out = residual[ds, :] + branch
        hidden_out[ds, :] = out.astype(BF16)
        t = iota((128, 1), 0) + ds.start
        live = t < length
        stats[0:1, :] += jnp.sum(jnp.where(live, branch * branch, 0.0), axis=0, keepdims=True)
        pooled[...] += jnp.sum(jnp.where((t >= prefix) & live, out, 0.0), axis=0, keepdims=True)

    rows_loop(size, 128, rows)
    pooled[...] = pooled[...] / count
    total = jnp.sum(stats[0:1, :])
    first = jnp.sum(sums[0:1, :])
    second = jnp.sum(sums[1:2, :])
    denominator = length.astype(F32) * width
    column = iota(stats.shape, 1)
    values = jnp.where(column == 0, first, jnp.where(column == 1, second, total))
    stats[...] = jnp.sqrt(values / denominator)


def swap(v, axis, count, far):
    return lax.ppermute(v, axis, [(i, i ^ far) for i in range(count)])


def add(a, b):
    return (a.astype(F32) + b.astype(F32)).astype(BF16)


def chip_gather(v):
    h = v.shape[0] // 2
    by_x = swap(v, "fsdp", 8, 2)
    by_y = swap(v, "fsdp", 8, 4)
    upper = swap(by_x[:h], "fsdp", 8, 4)
    lower = swap(by_y[h:], "fsdp", 8, 2)
    return [(v, 0, 0), (by_x, 0, 1), (by_y, 0, 2), (upper, 0, 3), (lower, h, 3)]


def chip_scatter(to_x, to_y, keep_a, keep_b, extra=0):
    h = keep_a.shape[0] // 2
    if extra:
        h = (keep_a.shape[0] - extra) // 2
    got_x = swap(to_x, "fsdp", 8, 2)
    got_y = swap(to_y, "fsdp", 8, 4)
    on_y = add(keep_a[h:], got_x[h:])
    on_x = add(keep_b[h:], got_y[h:])
    last_y = swap(on_y, "fsdp", 8, 4)
    last_x = swap(on_x, "fsdp", 8, 2)
    own_a = add(keep_a[:h], got_x[:h])
    own_b = add(keep_b[:h], got_y[:h])
    upper = add(own_a, last_y[:h])
    lower = add(own_b, last_x)
    parts = [upper, lower]
    if extra:
        parts.append(add(on_y[h:], last_y[h:]))
    return jnp.concatenate(parts, axis=0)


def chain_sum(v, count, where):
    if count != 4:
        for bit in range(count.bit_length() - 1):
            v = add(v, swap(v, "dp", count, 1 << bit))
        return v
    v = add(v, lax.ppermute(v, "dp", [(0, 1), (3, 2)]))
    v = add(v, lax.ppermute(v, "dp", [(1, 2), (2, 1)]))
    back = lax.ppermute(v, "dp", [(1, 0), (2, 3)])
    return jnp.where((where == 1) | (where == 2), v, back)


def message_plan(unit):
    h = unit // 2
    plan = []
    for dst, (near, far) in enumerate(((1, 3), (2, 3), (0, 2), (0, 1))):
        offset = 0 if dst in (0, 2) else h
        plan.append((dst, 0, h, unit, near, offset))
        plan.append((dst, h, h, unit, far, offset))
    return plan


def body(
    nf,
    nz,
    hidden_in,
    norm_gain_attn,
    w_query,
    w_key,
    w_value,
    w_out,
    rel_bias,
    norm_gain_ffn,
    w_in,
    w_ffout,
    bucket_index,
    row_lengths,
    prefix_lengths,
    out_cotangent,
    pool_cotangent,
):
    fast = nf == 8 and nz & (nz - 1) == 0
    size, width = hidden_in.shape
    shard = w_query.shape[0]
    heads = rel_bias.shape[1]
    levels = rel_bias.shape[0] * nf
    full_ff = w_in.shape[1]
    part_ff = full_ff // 2
    block = w_ffout.shape[0]
    half = width // 2
    me = lax.axis_index("fsdp").astype(jnp.int32)
    where = lax.axis_index("dp").astype(jnp.int32)
    core = me & 1
    zero = jnp.zeros((), jnp.int32)
    meta = jnp.stack([me, me >> 1, core, where, row_lengths[0], prefix_lengths[0], zero, zero])

    def by_core(first, second):
        return jnp.where(core == 0, first, second)

    def peer(v):
        return swap(v, "fsdp", nf, 1)

    cols = w_in.reshape(shard, nf // 2, 2, block)
    kept = by_core(cols[:, :, 0], cols[:, :, 1]).reshape(shard, part_ff)
    given = by_core(cols[:, :, 1], cols[:, :, 0]).reshape(shard, part_ff)
    if fast:
        stage = chip_gather(jnp.concatenate([w_query, w_key, w_value], axis=0))
        qkv_pieces, qkv_copies = [], []

        def put(piece, first, far):
            number = len(qkv_pieces)
            qkv_pieces.append(piece)
            for n in range(3):
                low, high = max(first, n * shard), min(first + piece.shape[0], (n + 1) * shard)
                if low < high:
                    qkv_copies.append(
                        (number, low - first, high - low, n, low - n * shard, 0, shard, far, 0)
                    )

        for piece, first, far in stage:
            put(piece, first, 2 * far)
            put(peer(piece), first, 2 * far + 1)

        taken = peer(given)
        both = by_core(
            jnp.concatenate([kept, taken], axis=0), jnp.concatenate([taken, kept], axis=0)
        )
        second = jnp.concatenate([w_out, both[:, :width], both[:, width:]], axis=0)
        in_pieces, in_copies, out_pieces, out_copies = [], [], [], []
        for piece, first, far in chip_gather(second):
            number = len(in_pieces)
            in_pieces.append(piece)
            for n in range(2):
                start = shard + n * 2 * shard
                low, high = max(first, start), min(first + piece.shape[0], start + 2 * shard)
                if low < high:
                    in_copies.append(
                        (number, low - first, high - low, 0, low - start, n * width, 2 * shard, far, 1)
                    )
            if first == 0:
                rows = piece[:shard]
                for extra, arr in ((0, rows), (1, peer(rows))):
                    out_copies.append(
                        (len(out_pieces), 0, shard, 0, 0, 0, shard, 2 * far + extra, 0)
                    )
                    out_pieces.append(arr)
        ff_pieces, ff_copies = [], []
        for piece, first, far in chip_gather(w_ffout):
            ff_copies.append(
                (len(ff_pieces), 0, piece.shape[0], 0, first, 0, block, far, 1)
            )
            ff_pieces.append(piece)
    else:

        def whole(v):
            return lax.all_gather(v, "fsdp", axis=0, tiled=True)

        qkv_pieces = [whole(w) for w in (w_query, w_key, w_value)]
        qkv_copies = [(n, 0, width, n, 0, 0, 0, 0, 0) for n in range(3)]
        out_pieces, out_copies = [whole(w_out)], [(0, 0, width, 0, 0, 0, 0, 0, 0)]
        all_in = whole(w_in).reshape(width, nf // 2, 2, block)
        in_pieces = [by_core(all_in[:, :, 0], all_in[:, :, 1]).reshape(width, part_ff)]
        in_copies = [(0, 0, width, 0, 0, 0, 0, 0, 0)]
        all_ff = whole(w_ffout).reshape(nf // 2, 2, block, width)
        ff_pieces = [by_core(all_ff[:, 0], all_ff[:, 1]).reshape(part_ff, width)]
        ff_copies = [(0, 0, part_ff, 0, 0, 0, 0, 0, 0)]

    small = jnp.concatenate([norm_gain_attn, norm_gain_ffn, rel_bias.reshape(-1)])
    small = lax.all_gather(small, "fsdp").astype(F32)
    gain_one = small[:, :shard].reshape(1, width)
    gain_two = small[:, shard : 2 * shard].reshape(1, width)
    table = small[:, 2 * shard :].reshape(levels, heads).T
    head_rows = -(-heads // 16) * 16
    table = jnp.pad(table, ((0, head_rows - heads), (0, 0))).astype(BF16)
    buckets = jnp.concatenate([bucket_index[::-1], jnp.full((1,), -1, jnp.int32)])[None, :]

    def dma(n):
        return pltpu.SemaphoreType.DMA((n,))

    def ins(arrays):
        return [(a, "h") for a in arrays]

    meta_in = (meta, "s")
    dense = size * width * width
    normed, bias, low = call(
        prepare_kernel,
        "prepare",
        [meta_in] + [(a, "v") for a in (hidden_in, gain_one, table, buckets, out_cotangent, pool_cotangent)],
        [
            ((size, width), BF16, "v"),
            ((heads, 128, 2 * size - 128), F32, "v"),
            ((size, width), BF16, "v"),
        ],
        [pltpu.VMEM((head_rows, 2 * size), F32)],
        nbytes=12 * 2**20,
    )
    low_peer = peer(low)
    normed_peer = peer(normed)
    square = pltpu.VMEM((width, width), BF16)
    q, k, v, attended, powers, inv_sums = call(
        functools.partial(attend_kernel, qkv_copies, len(qkv_pieces)),
        "attend",
        [meta_in, (normed, "v"), (bias, "v")] + ins(qkv_pieces),
        [((size, width), BF16, "v")] * 4
        + [((heads, size, size), BF16, "v"), ((size, 128), F32, "v")],
        [square] * 3 + [pltpu.VMEM((size, size), F32), dma(len(qkv_copies))],
        flops=8 * dense,
        nbytes=20 * 2**20,
        trans=heads * size * size,
    )
    attended_peer = peer(attended)
    residual, normed_two, sums = call(
        functools.partial(residual_kernel, out_copies, len(out_pieces)),
        "residual",
        [meta_in, (hidden_in, "v"), (attended, "v"), (gain_two, "v")] + ins(out_pieces),
        [((size, width), F32, "v"), ((size, width), BF16, "v"), ((8, width), F32, "v")],
        [square, dma(len(out_copies))],
        flops=2 * dense,
        nbytes=6 * 2**20,
    )
    normed_two_peer = peer(normed_two)
    shape_in = pltpu.VMEM((width, part_ff), BF16)
    shape_ff = pltpu.VMEM((part_ff, width), BF16)
    if fast:
        ff_plan, in_plan = message_plan(block), message_plan(2 * shard)
        ff_outs = [((block, width), BF16, "h")] * 4
        in_outs = [((2 * shard, part_ff), BF16, "h")] * 4
    else:
        ff_plan = [(0, 0, part_ff, 0, 0, 0)]
        in_plan = [(0, 0, width, 0, 0, 0)]
        ff_outs = [((part_ff, width), BF16, "h")]
        in_outs = [((width, part_ff), BF16, "h")]
    activated, slope, *ff_parts = call(
        functools.partial(expand_kernel, in_copies, len(in_pieces), ff_plan, len(ff_outs)),
        "expand",
        [meta_in]
        + [(a, "v") for a in (normed_two, normed_two_peer, low, low_peer)]
        + ins(in_pieces),
        [((2, size, part_ff), BF16, "v")] * 2 + ff_outs,
        [shape_in, shape_ff, dma(len(in_copies)), dma(len(ff_plan))],
        flops=16 * dense,
        nbytes=16 * 2**20,
        trans=size * full_ff,
    )
    grad_pre, part_gn, send_gn = call(
        functools.partial(
            contract_kernel,
            in_copies + [(n + len(in_pieces), r, c, 1, b, o, u, f, l) for n, r, c, d, b, o, u, f, l in ff_copies],
            len(in_pieces) + len(ff_pieces),
        ),
        "contract",
        [meta_in] + [(a, "v") for a in (slope, low, low_peer)] + ins(in_pieces + ff_pieces),
        [
            ((2, size, part_ff), BF16, "v"),
            ((size, width), F32, "v"),
            ((size, width), BF16, "v"),
        ],
        [shape_in, shape_ff, dma(len(in_copies) + len(ff_copies))],
        flops=16 * dense,
        nbytes=16 * 2**20,
    )
    other_gn = peer(send_gn)
    in_parts = call(
        functools.partial(outer_kernel, in_plan, len(in_outs)),
        "outer",
        [meta_in] + [(a, "v") for a in (normed_two, normed_two_peer, grad_pre)],
        in_outs,
        [shape_in, dma(len(in_plan))],
        flops=8 * dense,
        nbytes=8 * 2**20,
    )
    grad_residual, low_residual, grad_attended, grad_gain_two = call(
        functools.partial(through_kernel, out_copies, len(out_pieces)),
        "through",
        [meta_in]
        + [(a, "v") for a in (residual, part_gn, other_gn, out_cotangent, pool_cotangent, gain_two)]
        + ins(out_pieces),
        [
            ((size, width), F32, "v"),
            ((size, width), BF16, "v"),
            ((size, width), BF16, "v"),
            ((1, width), F32, "v"),
        ],
        [square, dma(len(out_copies))],
        flops=2 * dense,
        nbytes=10 * 2**20,
    )
    low_mine = by_core(low_residual[:, :half], low_residual[:, half:])
    low_other = peer(by_core(low_residual[:, half:], low_residual[:, :half]))
    send, keep, grad_table = call(
        attend_back_kernel,
        "attend_back",
        [meta_in]
        + [(a, "v") for a in (q, k, v, powers, grad_attended, attended, inv_sums, buckets)],
        [
            ((size, 3 * half), BF16, "v"),
            ((size, 3 * half), BF16, "v"),
            ((head_rows, levels), F32, "v"),
        ],
        [
            pltpu.VMEM((size, size), BF16),
            pltpu.VMEM((128, 2 * size), F32),
            pltpu.VMEM((head_rows, 2 * size), F32),
        ],
        flops=10 * dense,
        nbytes=14 * 2**20,
    )
    got = peer(send)
    grad_hidden, grad_gain_one = call(
        functools.partial(input_kernel, qkv_copies, len(qkv_pieces)),
        "inputs",
        [meta_in]
        + [(a, "v") for a in (hidden_in, grad_residual, send, keep, gain_one)]
        + ins(qkv_pieces),
        [((size, width), F32, "v"), ((1, width), F32, "v")],
        [square] * 3 + [dma(len(qkv_copies))],
        flops=6 * dense,
        nbytes=12 * 2**20,
    )
    tail = jnp.concatenate([grad_gain_one, grad_gain_two, grad_table[:heads].T.reshape(1, -1)], axis=1)
    tail_size = tail.shape[1]
    tail = jnp.pad(tail, ((0, 0), (0, 4 * half * 2 - tail_size))).reshape(2, 4 * half)
    extra = jnp.pad(tail, ((0, 14), (0, 0))).astype(BF16)
    if fast:
        at_plan = message_plan(2 * shard)
        at_plan = at_plan + [
            (0, 2 * shard, 16, 0, 0, width),
            (2, 2 * shard, 16, 0, 0, width),
        ]
        at_outs = [((2 * shard + (16 if n in (0, 2) else 0), 4 * half), BF16, "h") for n in range(4)]
    else:
        at_plan = [(0, 0, width + 16, 0, 0, 0)]
        at_outs = [((width + 16, 4 * half), BF16, "h")]
    at_parts = call(
        functools.partial(weights_kernel, at_plan, len(at_outs)),
        "weights",
        [meta_in]
        + [
            (a, "v")
            for a in (normed, normed_peer, keep, got, attended, attended_peer, low_mine, low_other, extra)
        ],
        at_outs,
        [pltpu.VMEM((width + 16, 4 * half), BF16), dma(len(at_plan))],
        flops=8 * dense,
        nbytes=10 * 2**20,
    )
    part_branch, send_branch = call(
        functools.partial(output_kernel, ff_copies, len(ff_pieces)),
        "output",
        [meta_in, (activated, "v")] + ins(ff_pieces),
        [((size, width), F32, "v"), ((size, width), BF16, "v")],
        [shape_ff, dma(len(ff_copies))],
        flops=8 * dense,
        nbytes=8 * 2**20,
    )
    other_branch = peer(send_branch)
    hidden_out, pooled, stats = call(
        finish_kernel,
        "finish",
        [meta_in] + [(a, "v") for a in (residual, part_branch, other_branch, sums)],
        [((size, width), BF16, "v"), ((1, width), F32, "v"), ((1, width), F32, "v")],
        nbytes=6 * 2**20,
    )

    if fast:
        sum_ff = chip_scatter(*ff_parts)
        grad_ffout = chain_sum(sum_ff, nz, where).astype(F32)

        def trade(v):
            mine_rows = by_core(v[:shard], v[shard : 2 * shard])
            other_rows = by_core(v[shard : 2 * shard], v[:shard])
            return mine_rows, other_rows

        sum_in = chip_scatter(*in_parts)
        mine_in, other_in = trade(sum_in)
        sum_in = jnp.concatenate([mine_in, peer(other_in)], axis=0)
        sum_in = chain_sum(sum_in, nz, where)
        mine_in = sum_in[:shard].reshape(shard, nf // 2, 1, block)
        other_in = sum_in[shard:].reshape(shard, nf // 2, 1, block)
        grad_in = by_core(
            jnp.concatenate([mine_in, other_in], axis=2),
            jnp.concatenate([other_in, mine_in], axis=2),
        ).reshape(shard, full_ff).astype(F32)
        sum_at = chip_scatter(*at_parts, extra=16)
        mine_at, other_at = trade(sum_at)
        rest = sum_at[2 * shard :]
        got_at = peer(jnp.concatenate([other_at, rest], axis=0))
        sum_at = jnp.concatenate([mine_at, got_at[:shard], add(rest, got_at[shard:])], axis=0)
        sum_at = chain_sum(sum_at, nz, where)
        mine_at, other_at = sum_at[:shard], sum_at[shard : 2 * shard]
        rest = sum_at[2 * shard :].astype(F32)

        def joined(n):
            a, b = mine_at[:, n * half : (n + 1) * half], other_at[:, n * half : (n + 1) * half]
            return by_core(jnp.concatenate([a, b], axis=1), jnp.concatenate([b, a], axis=1)).astype(F32)

    else:

        def reduced(v):
            v = lax.psum_scatter(v, "fsdp", scatter_dimension=0, tiled=True)
            return lax.psum(v, "dp").astype(F32)

        def spread(v, axis):
            none = jnp.zeros_like(v)
            return by_core(jnp.stack([v, none], axis), jnp.stack([none, v], axis))

        grad_ffout = reduced(
            spread(ff_parts[0].reshape(nf // 2, block, width), 1).reshape(full_ff, width)
        )
        grad_in = reduced(
            spread(in_parts[0].reshape(width, nf // 2, block), 2).reshape(width, full_ff)
        )
        grads = spread(at_parts[0][:width].reshape(width, 4, half), 2).reshape(width, 4 * width)
        grads = reduced(grads)
        rest = lax.psum(at_parts[0][width:], ("fsdp", "dp")).astype(F32)

        def joined(n):
            return grads[:, n * width : (n + 1) * width]

    rest = rest[:2].reshape(-1)
    all_one, all_two = rest[:width], rest[width : 2 * width]
    all_table = rest[2 * width : 2 * width + levels * heads].reshape(levels, heads)

    def mine(v):
        count = v.shape[0] // nf
        return lax.dynamic_slice_in_dim(v, me * count, count, 0)

    return (
        hidden_out,
        pooled,
        grad_hidden,
        mine(all_one),
        joined(0),
        joined(1),
        joined(2),
        joined(3),
        mine(all_table),
        mine(all_two),
        grad_in,
        grad_ffout,
        stats[:, :3],
    )


def solution(mesh):
    token = P(("fsdp", "dp"), None)
    weight = P("fsdp", None)
    return jax.shard_map(
        functools.partial(body, mesh.shape["fsdp"], mesh.shape["dp"]),
        mesh=mesh,
        in_specs=(
            token,
            P("fsdp"),
            weight,
            weight,
            weight,
            weight,
            weight,
            P("fsdp"),
            weight,
            weight,
            P(),
            P(("fsdp", "dp")),
            P(("fsdp", "dp")),
            token,
            token,
        ),
        out_specs=(
            token,
            token,
            token,
            P("fsdp"),
            weight,
            weight,
            weight,
            weight,
            weight,
            P("fsdp"),
            weight,
            weight,
            token,
        ),
        check_vma=False,
    )
```

time: 598 us -> 352 us (0.59)
  waiting for transfers between devices: 313 us -> 114 us
  matrix products: 118 us -> 0 us
  Pallas kernels: 0 us -> 109 us
  starting transfers between devices: 1.15 us -> 49.5 us
  blocking collectives: 59.2 us -> 14.2 us
  between operations: 20.7 us -> 4.4 us
  other arithmetic: 27.3 us -> 12.9 us
  local copies, waits for them, and re-layouts: 54.4 us -> 43.6 us
    reduce_scatter x6 -> x0, waiting for transfers between devices: 206 us -> none  [the longest x1 57.6 us: body(): lax.psum_scatter(grad_in_local.astype(jnp.bfloat16), 'fsdp', scatter_dime...]
    dot_general x27 -> x0, matrix products: 118 us -> none  [the longest x6 22.5 us: trans_left(): lax.dot_general(left, right, (((0,), (0,)), ((), ())), preferred_element_...]
    ppermute x0 -> x53, waiting for transfers between devices: none -> 114 us  [the longest x44 70.6 us: swap(): return lax.ppermute(v, axis, [(i, i ^ far) for i in range(count)])]
    pallas_call x0 -> x12, Pallas kernels: none -> 109 us  [call(): pl.pallas_call(kernel, name=name, out_shape=[jax.ShapeDtypeStruct(s, d) f...]
    all_gather x6 -> x0, waiting for transfers between devices: 88.5 us -> none  [the longest x1 37.1 us: body(): lax.all_gather(w_in, 'fsdp', axis=0, tiled=True)]
    ppermute x0 -> x53, starting transfers between devices: none -> 49.5 us  [the longest x44 29.3 us: swap(): return lax.ppermute(v, axis, [(i, i ^ far) for i in range(count)])]
    unnamed x2 -> x1, blocking collectives: 39.5 us -> 14.2 us
    dot_general x1 -> x0, local copies, waits for them, and re-layouts: 17.9 us -> none  [body(): jnp.einsum('bij,bh->hij', onehot, table_full, preferred_element_type=jnp....]
  transfers between devices with their start and end apart: 13 -> 53, of which waited for: 10 -> 17; matrix products, arithmetic and copies ran while one was open for 26% -> 6% of each run, Pallas kernels for 0% -> 27%
where the time goes in v1:
time: 352 us; the launch traced here: 348 us
  waiting for transfers between devices  114 us (32%)
  Pallas kernels  109 us (31%)
  starting transfers between devices  49.5 us (14%)
  local copies, waits for them, and re-layouts  43.6 us (12%)
  blocking collectives  14.2 us (4%)
  other arithmetic  12.9 us (4%)
  between operations  4.4 us (1%)
    pallas_call x12, Pallas kernels, call(): pl.pallas_call(kernel, name=name, out_shape=[jax.ShapeDtypeStruct(s, d) f...  109 us
    ppermute x44, waiting for transfers between devices, swap(): return lax.ppermute(v, axis, [(i, i ^ far) for i in range(count)])  70.6 us
    ppermute x44, starting transfers between devices, swap(): return lax.ppermute(v, axis, [(i, i ^ far) for i in range(count)])  29.3 us
    unnamed x193, local copies, waits for them, and re-layouts  27.4 us
    ppermute x3, waiting for transfers between devices, chain_sum(): back = lax.ppermute(v, 'dp', [(1, 0), (2, 3)])  24.3 us
    ppermute x3, waiting for transfers between devices, chain_sum(): v = add(v, lax.ppermute(v, 'dp', [(0, 1), (3, 2)]))  19.4 us
    ppermute x3, starting transfers between devices, chain_sum(): v = add(v, lax.ppermute(v, 'dp', [(0, 1), (3, 2)]))  14.2 us
    unnamed x1, blocking collectives  14.2 us
  transfers between devices with their start and end apart: 53, of which 17 were waited for; matrix products, arithmetic and copies ran while one was open for 6% of the time, Pallas kernels for 27%

profile of v1, /device:TPU:0, one launch (start us, length us, event | category | flops | bytes accessed | tf_op | source)
XLA Modules:
  0.0 347.5 jit_solution(9823996172366328941)
XLA Ops:
  12.9 15.1 %collective-permute-done.11.refs_6_.refs_5_ = bf16[480,768]{1,0:T(8,128)(2,1)S(1)} collective-permute-done((bf16[480,768]{1,0:T(8,128)(2,1)}, bf16[480,768]{1,0:T(8,128)(2,1)S(1)}, u32[]{:S(2)}, u32[]{:S(2)}) %collective-permute-start.11) | collective-permute-done | bytes 737312 | tf_op jit(solution)/shard_map/ppermute | solution.py:480
  30.8 6.1 %collective-permute-done.1.refs_5_.refs_8_ = bf16[288,768]{1,0:T(8,128)(2,1)S(1)} collective-permute-done((bf16[288,768]{1,0:T(8,128)(2,1)S(1)}, bf16[288,768]{1,0:T(8,128)(2,1)S(1)}, u32[]{:S(2)}, u32[]{:S(2)}) %collective-permute-start.1) | collective-permute-done | bytes 442400 | tf_op jit(solution)/shard_map/ppermute | solution.py:480
  43.0 8.1 %collective-permute-done.5.refs_9_.refs_12_ = bf16[144,768]{1,0:T(8,128)(2,1)S(1)} collective-permute-done((bf16[144,768]{1,0:T(8,128)(2,1)}, bf16[144,768]{1,0:T(8,128)(2,1)S(1)}, u32[]{:S(2)}, u32[]{:S(2)}) %collective-permute-start.5) | collective-permute-done | bytes 221216 | tf_op jit(solution)/shard_map/ppermute | solution.py:480
  52.0 14.2 %all-reduce.3 = bf16[1920]{0:T(1024)(128)(2,1)S(1)} all-reduce(bf16[1920]{0:T(1024)(128)(2,1)S(1)} %dynamic-update-slice), channel_id=2, replica_groups=mesh['fsdp'=8,'dp'=4] {'fsdp'}, use_global_device_ids=true, to_apply=%add.3 | all-reduce | flops 1920 | bytes 7680
  69.0 8.1 %prepare.1 = (bf16[512,768]{1,0:T(8,128)(2,1)}, f32[12,128,896]{2,1,0:T(8,128)S(1)}, bf16[512,768]{1,0:T(8,128)(2,1)S(1)}) custom-call(s32[8]{0:T(128)S(1)} %stack.19.meta.refs_0_, bf16[512,768]{1,0:T(8,128)(2,1)S(1)} %copy-done, f32[1,768]{1,0:T(1,128)S(1)} %reshape.80.gain.refs_5_, bf16[16,32]{1,0:T(8,128)(2,1)S(1)} %pad.15.table, s32[1,1024]{1,0:T(1,128)S(1)} %bitcast.18, ...), custom_call_target="tpu_custom_call" | custom-call | bytes 12582912 | tf_op jit(solution)/shard_map/prepare/pallas_call | solution.py:36
  82.7 20.1 %attend.1 = (bf16[512,768]{1,0:T(8,128)(2,1)S(1)}, bf16[512,768]{1,0:T(8,128)(2,1)S(1)}, bf16[512,768]{1,0:T(8,128)(2,1)S(1)}, bf16[512,768]{1,0:T(8,128)(2,1)S(...) custom-call(s32[8]{0:T(128)S(1)} %stack.19.meta.refs_0_, bf16[512,768]{1,0:T(8,128)(2,1)} %get-tuple-element.56.refs_1_, ...), custom_call_target="tpu_custom_call" | custom-call | flops 2415919104 | bytes 20971520 | tf_op jit(solution)/shard_map/attend/pallas_call | solution.py:36
  112.4 12.6 %collective-permute-done.20.refs_3_.refs_10_ = bf16[384,768]{1,0:T(8,128)(2,1)S(1)} collective-permute-done((bf16[384,768]{1,0:T(8,128)(2,1)S(1)}, bf16[384,768]{1,0:T(8,128)(2,1)S(1)}, u32[]{:S(2)}, u32[]{:S(2)}) %collective-permute-start.20) | collective-permute-done | bytes 589856 | tf_op jit(solution)/shard_map/ppermute | solution.py:480
  126.0 6.9 %collective-permute-done.19.refs_9_.refs_8_ = bf16[240,768]{1,0:T(8,128)(2,1)S(1)} collective-permute-done((bf16[240,768]{1,0:T(8,128)(2,1)S(1)}, bf16[240,768]{1,0:T(8,128)(2,1)S(1)}, u32[]{:S(2)}, u32[]{:S(2)}) %collective-permute-start.19) | collective-permute-done | bytes 368672 | tf_op jit(solution)/shard_map/ppermute | solution.py:480
  132.9 13.5 %expand.1 = (bf16[2,512,1536]{2,1,0:T(8,128)(2,1)}, bf16[2,512,1536]{2,1,0:T(8,128)(2,1)}, bf16[384,768]{1,0:T(8,128)(2,1)S(1)}, bf16[384,768]{1,0:T(8,128)(2,1)...) custom-call(s32[8]{0:T(128)S(1)} %stack.19.meta.refs_0_, ...), custom_call_target="tpu_custom_call" | custom-call | flops 4831838208 | bytes 16777216 | tf_op jit(solution)/shard_map/expand/pallas_call | solution.py:36
  149.7 11.7 %contract.1 = (bf16[2,512,1536]{2,1,0:T(8,128)(2,1)}, f32[512,768]{1,0:T(8,128)S(1)}, bf16[512,768]{1,0:T(8,128)(2,1)}) custom-call(s32[8]{0:T(128)S(1)} %stack.19.meta.refs_0_, bf16[2,512,1536]{2,1,0:T(8,128)(2,1)} %get-tuple-element.68.refs_1_, bf16[512,768]{1,0:T(8,128)(2,1)S(1)} %get-tuple-element.61.refs_3_.refs_2_, ...), custom_call_target="tpu_custom_call" | custom-call | flops 4831838208 | bytes 16777216 | tf_op jit(solution)/shard_map/contract/pallas_call | solution.py:36
  164.5 4.1 %outer.1 = (bf16[192,1536]{1,0:T(8,128)(2,1)}, bf16[192,1536]{1,0:T(8,128)(2,1)S(1)}, bf16[192,1536]{1,0:T(8,128)(2,1)S(1)}, bf16[192,1536]{1,0:T(8,128)(2,1)S(1)}) custom-call(s32[8]{0:T(128)S(1)} %stack.19.meta.refs_0_, bf16[512,768]{1,0:T(8,128)(2,1)S(1)} %get-tuple-element.60.refs_1_, bf16[512,768]{1,0:T(8,128)(2,1)S(1)} %collective-permute-done.17.refs_2_, ...), custom_call_target="tpu_custom_call" | custom-call | flops 2415919104 | bytes 8388608 | tf_op jit(solution)/shard_map/outer/pallas_call | solution.py:36
  179.1 4.2 %output.1 = (f32[512,768]{1,0:T(8,128)S(1)}, bf16[512,768]{1,0:T(8,128)(2,1)S(1)}) custom-call(s32[8]{0:T(128)S(1)} %stack.19.meta.refs_0_, bf16[2,512,1536]{2,1,0:T(8,128)(2,1)S(1)} %copy-done.74, bf16[384,768]{1,0:T(8,128)(2,1)S(1)} %copy-done.62, bf16[384,768]{1,0:T(8,128)(2,1)S(1)} %copy-done.49, bf16[384,768]{1,0:T(8,128)(2,1)S(1)} %copy-done.51, ...), custom_call_target="tpu_custom_call" | custom-call | flops 2415919104 | bytes 8388608 | tf_op jit(solution)/shard_map/output/pallas_call | solution.py:36
  189.9 5.8 %through.1 = (f32[512,768]{1,0:T(8,128)S(1)}, bf16[512,768]{1,0:T(8,128)(2,1)S(1)}, bf16[512,768]{1,0:T(8,128)(2,1)S(1)}, f32[1,768]{1,0:T(1,128)S(1)}) custom-call(s32[8]{0:T(128)S(1)} %stack.19.meta.refs_0_, f32[512,768]{1,0:T(8,128)S(1)} %get-tuple-element.59.residual.refs_1_, f32[512,768]{1,0:T(8,128)S(1)} %copy-done.12, ...), custom_call_target="tpu_custom_call" | custom-call | flops 603979776 | bytes 10485760 | tf_op jit(solution)/shard_map/through/pallas_call | solution.py:36
  195.8 20.3 %attend_back.1 = (bf16[512,1152]{1,0:T(8,128)(2,1)}, bf16[512,1152]{1,0:T(8,128)(2,1)S(1)}, f32[16,32]{1,0:T(8,128)S(1)}) custom-call(s32[8]{0:T(128)S(1)} %stack.19.meta.refs_0_, bf16[512,768]{1,0:T(8,128)(2,1)S(1)} %copy-done.56, bf16[512,768]{1,0:T(8,128)(2,1)S(1)} %copy-done.58, bf16[512,768]{1,0:T(8,128)(2,1)S(1)} %copy-done.60, ...), custom_call_target="tpu_custom_call" | custom-call | flops 3019898880 | bytes 14680064 | tf_op jit(solution)/shard_map/attend_back/pallas_call | solution.py:36
  222.7 9.2 %inputs.1 = (f32[512,768]{1,0:T(8,128)}, f32[1,768]{1,0:T(1,128)S(1)}) custom-call(s32[8]{0:T(128)S(1)} %stack.19.meta.refs_0_, bf16[512,768]{1,0:T(8,128)(2,1)S(1)} %copy-done, f32[512,768]{1,0:T(8,128)S(1)} %get-tuple-element.71.refs_2_, bf16[512,1152]{1,0:T(8,128)(2,1)} %get-tuple-element.78.refs_3_, ...), custom_call_target="tpu_custom_call" | custom-call | flops 1811939328 | bytes 12582912 | tf_op jit(solution)/shard_map/inputs/pallas_call | solution.py:36
  241.9 6.0 %weights.1 = (bf16[208,1536]{1,0:T(8,128)(2,1)S(1)}, bf16[192,1536]{1,0:T(8,128)(2,1)S(1)}, bf16[208,1536]{1,0:T(8,128)(2,1)S(1)}, bf16[192,1536]{1,0:T(8,128)(2,1)S(1)}) custom-call(s32[8]{0:T(128)S(1)} %stack.19.meta.refs_0_, bf16[512,768]{1,0:T(8,128)(2,1)} %get-tuple-element.56.refs_1_, bf16[512,768]{1,0:T(8,128)(2,1)} %collective-permute-done.26.refs_2_, ...), custom_call_target="tpu_custom_call" | custom-call | flops 2415919104 | bytes 10485760 | tf_op jit(solution)/shard_map/weights/pallas_call | solution.py:36
  250.8 11.8 %collective-permute-done.32 = bf16[192,1536]{1,0:T(8,128)(2,1)S(1)} collective-permute-done((bf16[192,1536]{1,0:T(8,128)(2,1)S(1)}, bf16[192,1536]{1,0:T(8,128)(2,1)S(1)}, u32[]{:S(2)}, u32[]{:S(2)}) %collective-permute-start.32) | collective-permute-done | bytes 589856 | tf_op jit(solution)/shard_map/ppermute | solution.py:480
  263.1 4.3 %collective-permute-done.30 = bf16[208,1536]{1,0:T(8,128)(2,1)S(1)} collective-permute-done((bf16[208,1536]{1,0:T(8,128)(2,1)S(1)}, bf16[208,1536]{1,0:T(8,128)(2,1)S(1)}, u32[]{:S(2)}, u32[]{:S(2)}) %collective-permute-start.30) | collective-permute-done | bytes 639008 | tf_op jit(solution)/shard_map/ppermute | solution.py:480
  280.7 5.8 %collective-permute-done.50 = bf16[384,768]{1,0:T(8,128)(2,1)S(1)} collective-permute-done((bf16[384,768]{1,0:T(8,128)(2,1)S(1)}, bf16[384,768]{1,0:T(8,128)(2,1)S(1)}, u32[]{:S(2)}, u32[]{:S(2)}) %collective-permute-start.50) | collective-permute-done | bytes 589856 | tf_op jit(solution)/shard_map/ppermute | solution.py:521
  287.4 7.2 %collective-permute-start.35 = (bf16[208,1536]{1,0:T(8,128)(2,1)S(1)}, bf16[208,1536]{1,0:T(8,128)(2,1)S(1)}, u32[]{:S(2)}, u32[]{:S(2)}) collective-permute-start(bf16[208,1536]{1,0:T(8,128)(2,1)S(1)} %pad_maximum_fusion.1), channel_id=1, source_target_pairs={{0,1},{3,2},{4,5},{7,6},{8,9},{11,10},{12,13},{15,14},{16,17},{19,... | collective-permute-start | bytes 1916936 | tf_op jit(solution)/shard_map/ppermute | solution.py:521
  294.7 4.4 %collective-permute-done.43 = bf16[192,1536]{1,0:T(8,128)(2,1)S(1)} collective-permute-done((bf16[192,1536]{1,0:T(8,128)(2,1)S(1)}, bf16[192,1536]{1,0:T(8,128)(2,1)S(1)}, u32[]{:S(2)}, u32[]{:S(2)}) %collective-permute-start.43) | collective-permute-done | bytes 589856 | tf_op jit(solution)/shard_map/ppermute | solution.py:521
  301.4 9.2 %collective-permute-done.35 = bf16[208,1536]{1,0:T(8,128)(2,1)S(1)} collective-permute-done((bf16[208,1536]{1,0:T(8,128)(2,1)S(1)}, bf16[208,1536]{1,0:T(8,128)(2,1)S(1)}, u32[]{:S(2)}, u32[]{:S(2)}) %collective-permute-start.35) | collective-permute-done | bytes 639008 | tf_op jit(solution)/shard_map/ppermute | solution.py:521
  318.4 11.7 %collective-permute-done.45 = bf16[192,1536]{1,0:T(8,128)(2,1)S(1)} collective-permute-done((bf16[192,1536]{1,0:T(8,128)(2,1)S(1)}, bf16[192,1536]{1,0:T(8,128)(2,1)S(1)}, u32[]{:S(2)}, u32[]{:S(2)}) %collective-permute-start.45) | collective-permute-done | bytes 589856 | tf_op jit(solution)/shard_map/ppermute | solution.py:523
  333.4 9.8 %collective-permute-done.37 = bf16[208,1536]{1,0:T(8,128)(2,1)S(1)} collective-permute-done((bf16[208,1536]{1,0:T(8,128)(2,1)S(1)}, bf16[208,1536]{1,0:T(8,128)(2,1)S(1)}, u32[]{:S(2)}, u32[]{:S(2)}) %collective-permute-start.37) | collective-permute-done | bytes 639008 | tf_op jit(solution)/shard_map/ppermute | solution.py:523
  (372 shorter events, 112.8 us)
Async XLA Ops:
  10.7 26.3 %collective-permute-start.1 = (bf16[288,768]{1,0:T(8,128)(2,1)S(1)}, bf16[288,768]{1,0:T(8,128)(2,1)S(1)}, u32[]{:S(2)}, u32[]{:S(2)}) collective-permute-start(bf16[288,768]{1,0:T(8,128)(2,1)S(1)} %constant_dynamic-update-slice_fusion.refs_3_.refs_6_), channel_id=1, source_target_pairs={{0,8},{4,12},{8,0},{12,4},{16,24},{20,28},{24,16},{28,20},{1,9},{5... | collective-permute-start | bytes 1327112 | tf_op jit(solution)/shard_map/ppermute | solution.py:480
  10.8 28.7 %collective-permute-start.3 = (bf16[288,768]{1,0:T(8,128)(2,1)S(1)}, bf16[288,768]{1,0:T(8,128)(2,1)S(1)}, u32[]{:S(2)}, u32[]{:S(2)}) collective-permute-start(bf16[288,768]{1,0:T(8,128)(2,1)S(1)} %constant_dynamic-update-slice_fusion.refs_3_.refs_6_), channel_id=1, source_target_pairs={{0,16},{4,20},{8,24},{12,28},{16,0},{20,4},{24,8},{28,12},{1,17},{... | collective-permute-start | bytes 1327112 | tf_op jit(solution)/shard_map/ppermute | solution.py:480
  12.8 53.5 %collective-permute-start.13 = (bf16[480,768]{1,0:T(8,128)(2,1)}, bf16[480,768]{1,0:T(8,128)(2,1)}, u32[]{:S(2)}, u32[]{:S(2)}) collective-permute-start(bf16[480,768]{1,0:T(8,128)(2,1)} %pad_maximum_fusion.refs_5_.refs_4_), channel_id=1, source_target_pairs={{0,16},{4,20},{8,24},{12,28},{16,0},{20,4},{24,8},{28,12},{1,17},{... | collective-permute-start | bytes 2211848 | tf_op jit(solution)/shard_map/ppermute | solution.py:480
  28.8 37.6 %collective-permute-start.15 = (bf16[240,768]{1,0:T(8,128)(2,1)}, bf16[240,768]{1,0:T(8,128)(2,1)}, u32[]{:S(2)}, u32[]{:S(2)}) collective-permute-start(bf16[240,768]{1,0:T(8,128)(2,1)} %slice.289), channel_id=1, source_target_pairs={{0,16},{4,20},{8,24},{12,28},{16,0},{20,4},{24,8},{28,12},{1,17},{... | collective-permute-start | bytes 1105928 | tf_op jit(solution)/shard_map/ppermute | solution.py:480
  41.7 39.8 %collective-permute-start = (bf16[288,768]{1,0:T(8,128)(2,1)S(1)}, bf16[288,768]{1,0:T(8,128)(2,1)}, u32[]{:S(2)}, u32[]{:S(2)}) collective-permute-start(bf16[288,768]{1,0:T(8,128)(2,1)S(1)} %constant_dynamic-update-slice_fusion.refs_3_.refs_6_), channel_id=1, source_target_pairs={{0,4},{4,0},{8,12},{12,8},{16,20},{20,16},{24,28},{28,24},{1,5},{5... | collective-permute-start | bytes 1327112 | tf_op jit(solution)/shard_map/ppermute | solution.py:480
  51.2 30.5 %collective-permute-start.2 = (bf16[288,768]{1,0:T(8,128)(2,1)S(1)}, bf16[288,768]{1,0:T(8,128)(2,1)}, u32[]{:S(2)}, u32[]{:S(2)}) collective-permute-start(bf16[288,768]{1,0:T(8,128)(2,1)S(1)} %collective-permute-done.1.refs_5_.refs_8_), channel_id=1, source_target_pairs={{0,4},{4,0},{8,12},{12,8},{16,20},{20,16},{24,28},{28,24},{1,5},{5... | collective-permute-start | bytes 1327112 | tf_op jit(solution)/shard_map/ppermute | solution.py:480
  51.2 30.9 %collective-permute-start.4 = (bf16[288,768]{1,0:T(8,128)(2,1)S(1)}, bf16[288,768]{1,0:T(8,128)(2,1)}, u32[]{:S(2)}, u32[]{:S(2)}) collective-permute-start(bf16[288,768]{1,0:T(8,128)(2,1)S(1)} %collective-permute-done.3.refs_7_.refs_10_), channel_id=1, source_target_pairs={{0,4},{4,0},{8,12},{12,8},{16,20},{20,16},{24,28},{28,24},{1,5},{5... | collective-permute-start | bytes 1327112 | tf_op jit(solution)/shard_map/ppermute | solution.py:480
  81.5 23.1 %collective-permute-start.9 = (bf16[96,768]{1,0:T(8,128)(2,1)S(1)}, bf16[96,768]{1,0:T(8,128)(2,1)S(1)}, u32[]{:S(2)}, u32[]{:S(2)}) collective-permute-start(bf16[96,768]{1,0:T(8,128)(2,1)S(1)} %copy-done.13), channel_id=1, source_target_pairs={{0,4},{4,0},{8,12},{12,8},{16,20},{20,16},{24,28},{28,24},{1,5},{5... | collective-permute-start | bytes 442376 | tf_op jit(solution)/shard_map/ppermute | solution.py:480
  81.7 44.3 %collective-permute-start.18 = (bf16[512,768]{1,0:T(8,128)(2,1)S(1)}, bf16[512,768]{1,0:T(8,128)(2,1)S(1)}, u32[]{:S(2)}, u32[]{:S(2)}) collective-permute-start(bf16[512,768]{1,0:T(8,128)(2,1)S(1)} %get-tuple-element.61.refs_3_.refs_2_), channel_id=1, source_target_pairs={{0,4},{4,0},{8,12},{12,8},{16,20},{20,16},{24,28},{28,24},{1,5},{5... | collective-permute-start | bytes 2359304 | tf_op jit(solution)/shard_map/ppermute | solution.py:480
  108.3 24.6 %collective-permute-start.17 = (bf16[512,768]{1,0:T(8,128)(2,1)S(1)}, bf16[512,768]{1,0:T(8,128)(2,1)S(1)}, u32[]{:S(2)}, u32[]{:S(2)}) collective-permute-start(bf16[512,768]{1,0:T(8,128)(2,1)S(1)} %get-tuple-element.60.refs_1_), channel_id=1, source_target_pairs={{0,4},{4,0},{8,12},{12,8},{16,20},{20,16},{24,28},{28,24},{1,5},{5... | collective-permute-start | bytes 2359304 | tf_op jit(solution)/shard_map/ppermute | solution.py:480
  125.0 24.7 %collective-permute-start.22 = (bf16[192,768]{1,0:T(8,128)(2,1)S(1)}, bf16[192,768]{1,0:T(8,128)(2,1)S(1)}, u32[]{:S(2)}, u32[]{:S(2)}) collective-permute-start(bf16[192,768]{1,0:T(8,128)(2,1)S(1)} %slice.292), channel_id=1, source_target_pairs={{0,16},{4,20},{8,24},{12,28},{16,0},{20,4},{24,8},{28,12},{1,17},{... | collective-permute-start | bytes 884744 | tf_op jit(solution)/shard_map/ppermute | solution.py:480
  125.6 24.1 %collective-permute-start.23 = (bf16[192,768]{1,0:T(8,128)(2,1)S(1)}, bf16[192,768]{1,0:T(8,128)(2,1)S(1)}, u32[]{:S(2)}, u32[]{:S(2)}) collective-permute-start(bf16[192,768]{1,0:T(8,128)(2,1)S(1)} %slice.293), channel_id=1, source_target_pairs={{0,8},{4,12},{8,0},{12,4},{16,24},{20,28},{24,16},{28,20},{1,9},{5... | collective-permute-start | bytes 884744 | tf_op jit(solution)/shard_map/ppermute | solution.py:480
  171.0 49.8 %collective-permute-start.26 = (bf16[512,768]{1,0:T(8,128)(2,1)}, bf16[512,768]{1,0:T(8,128)(2,1)}, u32[]{:S(2)}, u32[]{:S(2)}) collective-permute-start(bf16[512,768]{1,0:T(8,128)(2,1)} %get-tuple-element.56.refs_1_), channel_id=1, source_target_pairs={{0,4},{4,0},{8,12},{12,8},{16,20},{20,16},{24,28},{28,24},{1,5},{5... | collective-permute-start | bytes 2359304 | tf_op jit(solution)/shard_map/ppermute | solution.py:480
  171.5 67.3 %collective-permute-start.28 = (bf16[512,768]{1,0:T(8,128)(2,1)}, bf16[512,768]{1,0:T(8,128)(2,1)}, u32[]{:S(2)}, u32[]{:S(2)}) collective-permute-start(bf16[512,768]{1,0:T(8,128)(2,1)} %copy-done.20), channel_id=1, source_target_pairs={{0,4},{4,0},{8,12},{12,8},{16,20},{20,16},{24,28},{28,24},{1,5},{5... | collective-permute-start | bytes 2359304 | tf_op jit(solution)/shard_map/ppermute | solution.py:480
  171.5 44.6 %collective-permute-start.40 = (bf16[192,1536]{1,0:T(8,128)(2,1)}, bf16[192,1536]{1,0:T(8,128)(2,1)S(1)}, u32[]{:S(2)}, u32[]{:S(2)}) collective-permute-start(bf16[192,1536]{1,0:T(8,128)(2,1)} %copy-done.67), channel_id=1, source_target_pairs={{0,16},{4,20},{8,24},{12,28},{16,0},{20,4},{24,8},{28,12},{1,17},{... | collective-permute-start | bytes 1769480 | tf_op jit(solution)/shard_map/ppermute | solution.py:480
  185.0 32.1 %collective-permute-start.48 = (bf16[384,768]{1,0:T(8,128)(2,1)S(1)}, bf16[384,768]{1,0:T(8,128)(2,1)S(1)}, u32[]{:S(2)}, u32[]{:S(2)}) collective-permute-start(bf16[384,768]{1,0:T(8,128)(2,1)S(1)} %copy-done.66), channel_id=1, source_target_pairs={{0,16},{4,20},{8,24},{12,28},{16,0},{20,4},{24,8},{28,12},{1,17},{... | collective-permute-start | bytes 1769480 | tf_op jit(solution)/shard_map/ppermute | solution.py:480
  187.8 30.5 %collective-permute-start.46 = (bf16[384,768]{1,0:T(8,128)(2,1)S(1)}, bf16[384,768]{1,0:T(8,128)(2,1)S(1)}, u32[]{:S(2)}, u32[]{:S(2)}) collective-permute-start(bf16[384,768]{1,0:T(8,128)(2,1)S(1)} %copy-done.64), channel_id=1, source_target_pairs={{0,8},{4,12},{8,0},{12,4},{16,24},{20,28},{24,16},{28,20},{1,9},{5... | collective-permute-start | bytes 1769480 | tf_op jit(solution)/shard_map/ppermute | solution.py:480
  216.2 25.8 %collective-permute-start.27 = (bf16[512,1152]{1,0:T(8,128)(2,1)}, bf16[512,1152]{1,0:T(8,128)(2,1)}, u32[]{:S(2)}, u32[]{:S(2)}) collective-permute-start(bf16[512,1152]{1,0:T(8,128)(2,1)} %get-tuple-element.78.refs_3_), channel_id=1, source_target_pairs={{0,4},{4,0},{8,12},{12,8},{16,20},{20,16},{24,28},{28,24},{1,5},{5... | collective-permute-start | bytes 3538952 | tf_op jit(solution)/shard_map/ppermute | solution.py:480
  220.9 27.8 %collective-permute-start.39 = (bf16[96,1536]{1,0:T(8,128)(2,1)}, bf16[96,1536]{1,0:T(8,128)(2,1)}, u32[]{:S(2)}, u32[]{:S(2)}) collective-permute-start(bf16[96,1536]{1,0:T(8,128)(2,1)} %add_convert_fusion.17), channel_id=1, source_target_pairs={{0,16},{4,20},{8,24},{12,28},{16,0},{20,4},{24,8},{28,12},{1,17},{... | collective-permute-start | bytes 884744 | tf_op jit(solution)/shard_map/ppermute | solution.py:480
  222.3 26.3 %collective-permute-start.41 = (bf16[96,1536]{1,0:T(8,128)(2,1)}, bf16[96,1536]{1,0:T(8,128)(2,1)}, u32[]{:S(2)}, u32[]{:S(2)}) collective-permute-start(bf16[96,1536]{1,0:T(8,128)(2,1)} %add_convert_fusion.14), channel_id=1, source_target_pairs={{0,8},{4,12},{8,0},{12,4},{16,24},{20,28},{24,16},{28,20},{1,9},{5... | collective-permute-start | bytes 884744 | tf_op jit(solution)/shard_map/ppermute | solution.py:480
  240.4 28.6 %collective-permute-start.47 = (bf16[192,768]{1,0:T(8,128)(2,1)S(1)}, bf16[192,768]{1,0:T(8,128)(2,1)S(1)}, u32[]{:S(2)}, u32[]{:S(2)}) collective-permute-start(bf16[192,768]{1,0:T(8,128)(2,1)S(1)} %copy-done.82), channel_id=1, source_target_pairs={{0,16},{4,20},{8,24},{12,28},{16,0},{20,4},{24,8},{28,12},{1,17},{... | collective-permute-start | bytes 884744 | tf_op jit(solution)/shard_map/ppermute | solution.py:480
  250.1 27.1 %collective-permute-start.42 = (bf16[96,1536]{1,0:T(8,128)(2,1)S(1)}, bf16[96,1536]{1,0:T(8,128)(2,1)S(1)}, u32[]{:S(2)}, u32[]{:S(2)}) collective-permute-start(bf16[96,1536]{1,0:T(8,128)(2,1)S(1)} %get-tuple-element.102), channel_id=1, source_target_pairs={{0,4},{4,0},{8,12},{12,8},{16,20},{20,16},{24,28},{28,24},{1,5},{5... | collective-permute-start | bytes 884744 | tf_op jit(solution)/shard_map/ppermute | solution.py:480
  287.4 23.3 %collective-permute-start.35 = (bf16[208,1536]{1,0:T(8,128)(2,1)S(1)}, bf16[208,1536]{1,0:T(8,128)(2,1)S(1)}, u32[]{:S(2)}, u32[]{:S(2)}) collective-permute-start(bf16[208,1536]{1,0:T(8,128)(2,1)S(1)} %pad_maximum_fusion.1), channel_id=1, source_target_pairs={{0,1},{3,2},{4,5},{7,6},{8,9},{11,10},{12,13},{15,14},{16,17},{19,... | collective-permute-start | bytes 1916936 | tf_op jit(solution)/shard_map/ppermute | solution.py:521
  317.1 26.1 %collective-permute-start.37 = (bf16[208,1536]{1,0:T(8,128)(2,1)S(1)}, bf16[208,1536]{1,0:T(8,128)(2,1)S(1)}, u32[]{:S(2)}, u32[]{:S(2)}) collective-permute-start(bf16[208,1536]{1,0:T(8,128)(2,1)S(1)} %add_convert_fusion), channel_id=1, source_target_pairs={{1,0},{2,3},{5,4},{6,7},{9,8},{10,11},{13,12},{14,15},{17,16},{18,... | collective-permute-start | bytes 1916936 | tf_op jit(solution)/shard_map/ppermute | solution.py:523
  (121 other events, 1518.8 us)

commit v2 on v1

v2 whole, which is shorter than its diff:
```python
import functools
import math

import jax
import jax.numpy as jnp
from jax import lax
from jax.experimental import pallas as pl
from jax.experimental.pallas import tpu as pltpu
from jax.sharding import PartitionSpec as P

EPS = 1e-06
F32 = jnp.float32
BF16 = jnp.bfloat16
VMEM_SPARE = 6 * 2**20
WEIGHTS = {"turn": 30.0, "expand_own": 30.0}
GELU_A = 0.7978845608028654
GELU_B = 0.044715


def dot(a, b):
    return lax.dot_general(a, b, (((1,), (0,)), ((), ())), preferred_element_type=F32)


def dot_right(a, b):
    return lax.dot_general(a, b, (((1,), (1,)), ((), ())), preferred_element_type=F32)


def dot_left(a, b):
    return lax.dot_general(a, b, (((0,), (0,)), ((), ())), preferred_element_type=F32)


def iota(shape, dim):
    return lax.broadcasted_iota(jnp.int32, shape, dim)


def call(kernel, name, meta, ins, outs, scratch=(), deps=(), limit=0):
    spaces = {"v": pltpu.VMEM, "s": pltpu.SMEM, "h": pl.ANY}
    held = [(a.shape, a.dtype) for a, m in ins if m == "v"]
    held += [(s, d) for s, d, m in outs if m == "v"]
    held += [(x.shape, x.dtype) for x in scratch if x.memory_space == pltpu.VMEM]
    need = sum(math.prod(s) * jnp.dtype(d).itemsize for s, d in held)
    ins = [(after(meta, *deps), "s")] + list(ins)
    return pl.pallas_call(
        kernel,
        name=name,
        out_shape=[jax.ShapeDtypeStruct(s, d) for s, d, _ in outs],
        in_specs=[pl.BlockSpec(memory_space=spaces[m]) for _, m in ins],
        out_specs=[pl.BlockSpec(memory_space=spaces[m]) for _, _, m in outs],
        scratch_shapes=list(scratch),
        compiler_params=pltpu.CompilerParams(vmem_limit_bytes=max(limit, need + VMEM_SPARE)),
        cost_estimate=pl.CostEstimate(
            flops=1000, bytes_accessed=int(3.7e6 * WEIGHTS.get(name, 0.0)) + 1000, transcendentals=0
        ),
    )(*[a for a, _ in ins])


def after(v, *deps):
    return lax.optimization_barrier((v,) + deps)[0] if deps else v


def place(meta, pieces, targets, copies):
    for src, row, rows, from_column, dst, base, column, width, unit, far, side in copies:
        start = base
        if unit:
            start = base + unit * jnp.bitwise_xor(meta[1], far)
            if side == 1:
                start = start + (unit // 2) * meta[2]
            if side == 2:
                start = start + (unit // 2) * (1 - meta[2])
            start = pl.multiple_of(start, 16)
        targets[dst][pl.ds(start, rows), column : column + width] = pieces[src][
            row : row + rows, from_column : from_column + width
        ]


def rows_loop(count, step, fn):
    def one(i, carry):
        fn(pl.ds(pl.multiple_of(i * step, step), step))
        return carry

    lax.fori_loop(0, count // step, one, 0)


def scatter_out(meta, scratch, outs, plan):
    for dst, row, rows, unit, far, offset in plan:
        start = offset
        if unit:
            start = pl.multiple_of(offset + unit * jnp.bitwise_xor(meta[1], far), 16)
        outs[dst][row : row + rows, :] = scratch[pl.ds(start, rows), :]


def pack_kernel(n_chips, meta, *refs):
    sources = refs[:5]
    gain_one, gain_two, rel = refs[5:8]
    kept_a, given_a, kept_b, given_b, small = refs[8:13]
    held, sems = refs[13:18], refs[18]
    handles = [pltpu.make_async_copy(a, b, sems.at[n]) for n, (a, b) in enumerate(zip(sources, held))]
    for handle in handles:
        handle.start()
    small[...] = jnp.zeros_like(small)
    small[0:1, 0 : gain_one.shape[1]] = gain_one[...].astype(F32)
    small[1:2, 0 : gain_two.shape[1]] = gain_two[...].astype(F32)
    small[2:3, :] = jnp.broadcast_to(meta[4].astype(F32), (1, 128))
    small[4 : 4 + rel.shape[0], 0 : rel.shape[1]] = rel[...].astype(F32)
    for handle in handles:
        handle.wait()
    wq, wk, wv, wo, w_in = held
    core = meta[2]
    half = wq.shape[1] // 2
    block = w_in.shape[1] // (2 * n_chips)
    for which, a_ref, b_ref in ((core, kept_a, kept_b), (1 - core, given_a, given_b)):
        for n, w in enumerate((wq, wk, wv, wo)):
            cols = pl.ds(pl.multiple_of(which * half, 128), half)
            a_ref[:, n * half : (n + 1) * half] = w[:, cols]
        for n in range(b_ref.shape[1] // block):
            cols = pl.ds(pl.multiple_of((2 * n + which) * block, 128), block)
            b_ref[:, n * block : (n + 1) * block] = w_in[:, cols]


def stack_kernel(meta, kept_a, taken_a, kept_b, taken_b, both_a, both_b):
    shard = kept_a.shape[0]
    mine = pl.ds(pl.multiple_of(shard * meta[2], 16), shard)
    theirs = pl.ds(pl.multiple_of(shard * (1 - meta[2]), 16), shard)
    for kept, taken, both in ((kept_a, taken_a, both_a), (kept_b, taken_b, both_b)):
        both[mine, :] = kept[...]
        both[theirs, :] = taken[...]


def rows_kernel(meta, *refs):
    for n, ref in enumerate(refs[:-1]):
        refs[-1][8 * n : 8 * n + 8, :] = ref[...]


def prepare_kernel(n_small, relative, levels, meta, hidden, hidden_peer, *refs):
    smalls = refs[:n_small]
    buckets, out_cot, pool_cot = refs[n_small : n_small + 3]
    normed, normed_peer, bias, low, gain_one, gain_two, length_peer, table, table_rows = refs[n_small + 3 :]
    size, width = hidden.shape
    length, prefix = meta[4], meta[5]
    count = (length - prefix).astype(F32)
    pieces = [ref[8 * n : 8 * n + 8, :] for ref in smalls for n in range(ref.shape[0] // 8)]
    shard = width // len(pieces)
    some = levels // len(pieces)
    table[...] = jnp.zeros_like(table)
    first = jnp.zeros((1, width), F32)
    second = jnp.zeros((1, width), F32)
    rest = jnp.zeros((1, width - 128), F32)
    peers = jnp.zeros((1, 128), F32)
    for p, piece in enumerate(pieces):
        where = jnp.bitwise_xor(meta[0], 2 * (p % 4) + p // 4) if relative else jnp.int32(p)
        first += pltpu.roll(jnp.concatenate([piece[0:1], rest], axis=1), shard * where, 1)
        second += pltpu.roll(jnp.concatenate([piece[1:2], rest], axis=1), shard * where, 1)
        peers += jnp.where(where == jnp.bitwise_xor(meta[0], 1), piece[2:3], 0.0)
        for b in range(some):
            table[pl.ds(some * where + b, 1), :] = piece[4 + b : 5 + b]
    length_peer[...] = peers
    gain_one[...] = first
    gain_two[...] = second

    for x_ref, n_ref in ((hidden, normed), (hidden_peer, normed_peer)):

        def rows(ds, x_ref=x_ref, n_ref=n_ref):
            x = x_ref[ds, :].astype(F32)
            inv = lax.rsqrt(jnp.mean(x * x, axis=-1, keepdims=True) + EPS)
            n_ref[ds, :] = (x * inv * gain_one[...]).astype(BF16)

        rows_loop(size, 256, rows)

    def lows(ds):
        t = iota((256, 1), 0) + ds.start
        pool = jnp.where((t >= prefix) & (t < length), 1.0, 0.0) / count
        low[ds, :] = (out_cot[ds, :].astype(F32) + pool * pool_cot[...]).astype(BF16)

    rows_loop(size, 256, lows)
    span = 2 * size
    hot = (buckets[...] == iota((levels, span), 0)).astype(BF16)
    table_rows[...] = dot_left(table[...].astype(BF16), hot)
    heads, _, wide = bias.shape
    base = heads * meta[2]

    def head(h, carry):
        row = table_rows[pl.ds(base + h, 1), :]
        first = jnp.broadcast_to(pltpu.roll(row, span - 127, 1), (8, span))
        sub = iota((8, span), 0)
        full = first
        for k in range(1, 8):
            full = jnp.where(sub == k, pltpu.roll(first, k, 1), full)
        bias[h, 0:8, :] = full[:, :wide]
        have = 8
        while have < 128:
            more = pltpu.roll(full, have, 1)
            bias[h, have : 2 * have, :] = more[:, :wide]
            full = jnp.concatenate([full, more], axis=0)
            have *= 2
        return carry

    lax.fori_loop(0, heads, head, 0)


def collect_kernel(copies, n_pieces, *refs):
    meta = refs[0]
    pieces = refs[1 : 1 + n_pieces]
    qkv, w_half = refs[1 + n_pieces :]
    place(meta, pieces, (qkv, w_half), copies)


def attend_kernel(meta, x_ref, bias, w, length, qkv, out, upper, lower, powers, inv_sums, scores):
    size = x_ref.shape[0]
    part = w.shape[1] // 3
    pairs = part // 128
    lane = iota((1, 128), 1)
    half = lane < 64
    strips = size // 128
    inv_sums[...] = jnp.zeros_like(inv_sums)

    def project(ds):
        for n in range(3):
            cols = slice(n * part, (n + 1) * part)
            qkv[ds, cols] = dot(x_ref[ds, :], w[:, cols]).astype(BF16)

    rows_loop(size, 256, project)
    masked = jnp.where(iota((size, 1), 0).astype(F32) < length[0:1, 0:1], 0.0, -1e30).astype(F32)

    def pair(p, carry):
        base = pl.multiple_of(p * 128, 128)
        qp = qkv[:, pl.ds(base, 128)].astype(F32)
        kp = qkv[:, pl.ds(base + part, 128)].astype(F32)
        vp = qkv[:, pl.ds(base + 2 * part, 128)].astype(F32)
        joined = None
        for side in range(2):
            head = 2 * p + side
            own = half if side == 0 else jnp.logical_not(half)
            spare = lane == (64 if side == 0 else 0)
            qa = jnp.where(own, qp, jnp.where(spare, 1.0, 0.0)).astype(BF16)
            ka = jnp.where(own, kp, jnp.where(spare, masked, 0.0)).astype(BF16)
            va = jnp.where(own, vp, jnp.where(spare, 1.0, 0.0)).astype(BF16)
            top = None
            for a in range(strips):
                rows = slice(128 * a, 128 * a + 128)
                off = 128 * (strips - 1 - a)
                s = dot_right(ka[rows], qa) + bias[head, :, off : off + size]
                scores[rows, :] = s
                peak = jnp.max(s, axis=0, keepdims=True)
                top = peak if top is None else jnp.maximum(top, peak)
            for a in range(strips):
                rows = slice(128 * a, 128 * a + 128)
                powers[head, rows, :] = jnp.exp(scores[rows, :] - top).astype(BF16)
            mixed = dot_left(va, powers[head]).T
            sums = jnp.sum(jnp.where(spare, mixed, 0.0), axis=1, keepdims=True)
            inv = 1.0 / sums
            inv_sums[...] = jnp.where(lane == head, inv, inv_sums[...])
            mixed = mixed * inv
            joined = mixed if side == 0 else jnp.where(half, joined, mixed)
        joined = joined.astype(BF16)
        cols = pl.ds(base, 128)
        out[:, cols] = joined
        upper[:, cols] = joined[: size // 2]
        lower[:, cols] = joined[size // 2 :]
        return carry

    lax.fori_loop(0, pairs, pair, 0)


def residual_kernel(meta, hidden, attended, upper, lower, gain, w_half, w_other, residual, normed, left, middle, right, sums, w_out):
    size, width = hidden.shape
    half = width // 2
    length = meta[4]
    core = meta[2]
    w_out[:, pl.ds(pl.multiple_of(core * half, 128), half)] = w_half[...]
    w_out[:, pl.ds(pl.multiple_of((1 - core) * half, 128), half)] = w_other[...]
    mine = pl.ds(pl.multiple_of(core * half, 128), half)
    other = pl.ds(pl.multiple_of((1 - core) * half, 128), half)
    sums[...] = jnp.zeros_like(sums)

    for first, got in ((0, upper), (size // 2, lower)):
        ds = slice(first, first + size // 2)
        x = hidden[ds, :].astype(F32)
        branch = dot(attended[ds, :], w_out[mine, :]) + dot(got[...], w_out[other, :])
        live = (iota((size // 2, 1), 0) + first) < length
        sums[0:1, :] += jnp.sum(jnp.where(live, x * x, 0.0), axis=0, keepdims=True)
        sums[1:2, :] += jnp.sum(jnp.where(live, branch * branch, 0.0), axis=0, keepdims=True)
        r = x + branch
        residual[ds, :] = r
        inv = lax.rsqrt(jnp.mean(r * r, axis=-1, keepdims=True) + EPS)
        value = (r * inv * gain[...]).astype(BF16)
        normed[ds, :] = value
        third = left.shape[1]
        for n, ref in enumerate((left, middle, right)):
            ref[ds, :] = value[:, n * third : (n + 1) * third]


def expand_kernel(copies, n_pieces, *refs):
    meta, x_ref = refs[:2]
    pieces = refs[2 : 2 + n_pieces]
    if copies:
        activated, slope, w_in = refs[2 + n_pieces :]
        place(meta, pieces, (w_in,), copies)
    else:
        w_in = pieces[0]
        activated, slope, whole = refs[2 + n_pieces :]
        third = x_ref.shape[1]
        for n, ref in enumerate((x_ref, *pieces[1:])):
            whole[:, n * third : (n + 1) * third] = ref[...]
        x_ref = whole
    chunk = 512 if w_in.shape[1] % 512 == 0 else 256

    def rows(ds):
        x = x_ref[ds, :]
        for c in range(0, w_in.shape[1], chunk):
            t = dot(x, w_in[:, c : c + chunk])
            square = t * t
            th = jnp.tanh(t * (GELU_A + (GELU_A * GELU_B) * square))
            phi = 0.5 + 0.5 * th
            activated[ds, c : c + chunk] = (t * phi).astype(BF16)
            inner = GELU_A + (3.0 * GELU_A * GELU_B) * square
            slope[ds, c : c + chunk] = (phi + 0.5 * t * (1.0 - th * th) * inner).astype(BF16)

    rows_loop(x_ref.shape[0], 256, rows)


def product_kernel(plan, n_out, *refs):
    meta, left_own, left_peer, right_own, right_peer = refs[:5]
    outs = refs[5 : 5 + n_out]
    grads = refs[5 + n_out]
    for c in range(0, grads.shape[0], 256):
        part = dot_left(left_own[:, c : c + 256], right_own[...])
        part += dot_left(left_peer[:, c : c + 256], right_peer[...])
        grads[c : c + 256, :] = part.astype(BF16)
    scatter_out(meta, grads, outs, plan)


def contract_kernel(copies, n_pieces, *refs):
    meta, slope_own, slope_peer, low_own, low_peer, w_in = refs[:6]
    pieces = refs[6 : 6 + n_pieces]
    pre_own, pre_peer, part_own, send_left, send_right, w_ffout = refs[6 + n_pieces :]
    half = send_left.shape[1]
    place(meta, pieces, (w_ffout,), copies)
    size = low_own.shape[0]
    chunk = 512 if w_in.shape[1] % 512 == 0 else 256
    for slope, low, grad_pre, part in (
        (slope_peer, low_peer, pre_peer, (send_left, send_right)),
        (slope_own, low_own, pre_own, (part_own,)),
    ):

        def rows(ds, slope=slope, low=low, grad_pre=grad_pre, part=part):
            y = low[ds, :]
            total = None
            for c in range(0, w_in.shape[1], chunk):
                g = dot_right(y, w_ffout[c : c + chunk, :])
                g = (slope[ds, c : c + chunk].astype(F32) * g).astype(BF16)
                grad_pre[ds, c : c + chunk] = g
                t = dot_right(g, w_in[:, c : c + chunk])
                total = t if total is None else total + t
            if len(part) == 2:
                part[0][ds, :] = total[:, :half].astype(BF16)
                part[1][ds, :] = total[:, half:].astype(BF16)
            else:
                part[0][ds, :] = total

        rows_loop(size, 256, rows)


def through_kernel(meta, residual, part, other, other_right, out_cot, pool_cot, gain, w_half, w_other,
                   grad_residual, low_mine, upper, lower, grad_keep, grad_send, grad_gain):
    size, width = residual.shape
    half = width // 2
    core = meta[2]
    mine = pl.ds(pl.multiple_of(core * half, 128), half)
    theirs = pl.ds(pl.multiple_of((1 - core) * half, 128), half)
    length, prefix = meta[4], meta[5]
    count = (length - prefix).astype(F32)
    grad_gain[...] = jnp.zeros_like(grad_gain)

    def rows(ds, low_given, start):
        x = residual[ds, :]
        gn = part[ds, :] + jnp.concatenate([other[ds, :], other_right[ds, :]], axis=1).astype(F32)
        inv = lax.rsqrt(jnp.mean(x * x, axis=-1, keepdims=True) + EPS)
        u = gain[...] * gn
        xr = x * inv
        t = iota((128, 1), 0) + ds.start
        pool = jnp.where((t >= prefix) & (t < length), 1.0, 0.0) / count
        go = out_cot[ds, :].astype(F32) + pool * pool_cot[...]
        g = go + inv * (u - xr * jnp.mean(xr * u, axis=-1, keepdims=True))
        grad_gain[...] += jnp.sum(xr * gn, axis=0, keepdims=True)
        grad_residual[ds, :] = g
        first, second = g[:, :half].astype(BF16), g[:, half:].astype(BF16)
        on_first = jnp.broadcast_to(core == 0, first.shape)
        a = jnp.where(on_first, g[:, :half], g[:, half:]).astype(BF16)
        b = jnp.where(on_first, g[:, half:], g[:, :half]).astype(BF16)
        low_mine[ds, :] = a
        low_given[pl.ds(ds.start - start, 128), :] = b
        grad_keep[ds, :] = (dot_right(a, w_half[mine, :]) + dot_right(b, w_other[mine, :])).astype(BF16)
        grad_send[ds, :] = (dot_right(a, w_half[theirs, :]) + dot_right(b, w_other[theirs, :])).astype(BF16)

    middle = size // 2
    for first, low_given in ((0, upper), (middle, lower)):

        def some(i, carry, first=first, low_given=low_given):
            rows(pl.ds(pl.multiple_of(first + 128 * i, 128), 128), low_given, first)
            return carry

        lax.fori_loop(0, middle // 128, some, 0)


def attend_back_kernel(meta, qkv, powers, g_ref, a_ref, inv_sums, diag_in, out, diag, grads, slant):
    size = g_ref.shape[0]
    part = qkv.shape[1] // 3
    pairs = part // 128
    strips = size // 128
    span = 2 * size
    lane = iota((1, 128), 1)
    half = lane < 64
    diag[...] = diag_in[...]

    def pair(p, carry):
        base = pl.multiple_of(p * 128, 128)
        cols = pl.ds(base, 128)
        kcols = pl.ds(base + part, 128)
        vcols = pl.ds(base + 2 * part, 128)
        qp, kp = qkv[:, cols], qkv[:, kcols]
        vp = qkv[:, vcols].astype(F32)
        do = g_ref[:, cols].astype(F32)
        prod = do * a_ref[:, cols].astype(F32)
        dq_all = None
        for side in range(2):
            head = 2 * p + side
            own = half if side == 0 else jnp.logical_not(half)
            one = 64 if side == 0 else 0
            inv = jnp.sum(jnp.where(lane == head, inv_sums[...], 0.0), axis=1, keepdims=True)
            inner = jnp.sum(jnp.where(own, prod, 0.0), axis=1, keepdims=True) * inv
            upper = inner.astype(BF16).astype(F32)
            dos = jnp.where(
                own,
                do * inv,
                jnp.where(lane == one, -upper, jnp.where(lane == one + 1, upper - inner, 0.0)),
            ).astype(BF16)
            ones = (lane == one) | (lane == one + 1)
            va = jnp.where(own, vp, jnp.where(ones, 1.0, 0.0)).astype(BF16)
            slant[...] = jnp.zeros_like(slant)
            for a in range(strips):
                rows = slice(128 * a, 128 * a + 128)
                off = 128 * (strips - 1 - a)
                e = powers[head, rows, :]
                ds = (e.astype(F32) * dot_right(va[rows], dos)).astype(BF16)
                grads[rows, :] = ds
                slant[:, off : off + size] += ds.astype(F32)
                dk = dot(ds, qp).astype(BF16)
                dv = dot(e, dos).astype(BF16)
                if side == 1:
                    dk = jnp.where(half, out[rows, kcols].astype(F32), dk.astype(F32)).astype(BF16)
                    dv = jnp.where(half, out[rows, vcols].astype(F32), dv.astype(F32)).astype(BF16)
                out[rows, kcols] = dk
                out[rows, vcols] = dv
            dq = dot_left(kp, grads[...]).T
            dq_all = dq if side == 0 else jnp.where(half, dq_all, dq)
            y = slant[...]
            rest = 64
            while rest >= 1:
                y = y[:rest] + pltpu.roll(y[rest:], span - rest, 1)
                rest //= 2
            diag[pl.ds(head, 1), :] += pltpu.roll(y, 127, 1)
        out[:, cols] = dq_all.astype(BF16)
        return carry

    lax.fori_loop(0, pairs, pair, 0)


def weights_kernel(plan, n_out, *refs):
    meta, x_own, x_peer, dqkv_own, dqkv_peer, att_own, upper, lower, att_peer, got_peer, low_own, low_upper, low_lower, small = refs[:14]
    outs = refs[14 : 14 + n_out]
    (grads,) = refs[14 + n_out :]
    middle = upper.shape[0]
    part = dqkv_own.shape[1]
    depth = x_own.shape[1]
    half = depth // 2
    for c in range(0, depth, 256):
        cols = slice(c, c + 256)
        g = dot_left(x_own[:, cols], dqkv_own[...]) + dot_left(x_peer[:, cols], dqkv_peer[...])
        grads[cols, 0:part] = g.astype(BF16)
    core = meta[2]
    mine = pl.multiple_of(core * half, 16)
    theirs = pl.multiple_of((1 - core) * half, 16)
    for c in range(0, half, 128):
        cols = slice(c, c + 128)
        g = dot_left(att_own[:, cols], low_own[...]) + dot_left(att_peer[:middle, cols], low_upper[...])
        g += dot_left(att_peer[middle:, cols], low_lower[...])
        grads[pl.ds(mine + c, 128), part:] = g.astype(BF16)
        g = dot_left(upper[:, cols], low_own[:middle]) + dot_left(lower[:, cols], low_own[middle:])
        g += dot_left(got_peer[:middle, cols], low_upper[...])
        g += dot_left(got_peer[middle:, cols], low_lower[...])
        grads[pl.ds(theirs + c, 128), part:] = g.astype(BF16)
    grads[depth:, :] = jnp.zeros((16, grads.shape[1]), BF16)
    grads[depth:, 0:128] = small[...].astype(BF16)
    scatter_out(meta, grads, outs, plan)


def inputs_kernel(meta, dqkv_own, dqkv_peer, w, hidden, hidden_peer, gain_two, diag, buckets,
                  part_own, left, right, small, gain_one):
    size, width = part_own.shape
    half = width // 2
    small[...] = jnp.zeros_like(small)
    gain_one[...] = jnp.zeros_like(gain_one)

    def share(x_ref, ds, value):
        x = x_ref[ds, :].astype(F32)
        inv = lax.rsqrt(jnp.mean(x * x, axis=-1, keepdims=True) + EPS)
        gain_one[...] += jnp.sum(x * inv * value, axis=0, keepdims=True)

    def peers(ds):
        value = dot_right(dqkv_peer[ds, :], w[...])
        share(hidden_peer, ds, value)
        value = value.astype(BF16)
        left[ds, :] = value[:, :half]
        right[ds, :] = value[:, half:]

    def own(ds):
        value = dot_right(dqkv_own[ds, :], w[...])
        share(hidden, ds, value)
        part_own[ds, :] = value

    rows_loop(size, 256, peers)
    rows_loop(size, 256, own)
    count = width // 128
    for n in range(count):
        small[n : n + 1, :] = gain_one[:, 128 * n : 128 * n + 128]
        small[count + n : count + n + 1, :] = gain_two[:, 128 * n : 128 * n + 128]
    hot = (buckets[...] == iota((128, diag.shape[1]), 0)).astype(F32)
    table = lax.dot_general(
        diag[...],
        hot,
        (((1,), (1,)), ((), ())),
        preferred_element_type=F32,
        precision=lax.Precision.HIGHEST,
    )
    lane = iota((1, 128), 1)
    few = (16 - 2 * count) * 2 - 2
    for n in range(few):
        head = few * meta[2] + n
        row = jnp.where(lane < 32, table[n : n + 1, :], 0.0)
        small[pl.ds(2 * count + head // 4, 1), :] += pltpu.roll(row, 32 * (head % 4), 1)


def hidden_kernel(meta, hidden, grad_residual, part, left, right, gain, grad_hidden):
    def rows(ds):
        total = part[ds, :] + jnp.concatenate([left[ds, :], right[ds, :]], axis=1).astype(F32)
        x = hidden[ds, :].astype(F32)
        inv = lax.rsqrt(jnp.mean(x * x, axis=-1, keepdims=True) + EPS)
        u = gain[...] * total
        xr = x * inv
        grad_hidden[ds, :] = grad_residual[ds, :] + inv * (
            u - xr * jnp.mean(xr * u, axis=-1, keepdims=True)
        )

    rows_loop(hidden.shape[0], 256, rows)


def output_kernel(meta, act_own, act_peer, w_ffout, part_own, left, right):
    size, width = part_own.shape
    half = width // 2

    def peers(ds):
        value = dot(act_peer[ds, :], w_ffout[...]).astype(BF16)
        left[ds, :] = value[:, :half]
        right[ds, :] = value[:, half:]

    def own(ds):
        part_own[ds, :] = dot(act_own[ds, :], w_ffout[...])

    rows_loop(size, 256, peers)
    rows_loop(size, 256, own)


def finish_kernel(meta, residual, part, left, right, sums, hidden_out, pooled, stats):
    size, width = residual.shape
    length, prefix = meta[4], meta[5]
    count = (length - prefix).astype(F32)
    pooled[...] = jnp.zeros_like(pooled)
    stats[...] = jnp.zeros_like(stats)

    def rows(ds):
        branch = part[ds, :] + jnp.concatenate([left[ds, :], right[ds, :]], axis=1).astype(F32)
        out = residual[ds, :] + branch
        hidden_out[ds, :] = out.astype(BF16)
        t = iota((128, 1), 0) + ds.start
        live = t < length
        stats[0:1, :] += jnp.sum(jnp.where(live, branch * branch, 0.0), axis=0, keepdims=True)
        pooled[...] += jnp.sum(jnp.where((t >= prefix) & live, out, 0.0), axis=0, keepdims=True)

    rows_loop(size, 128, rows)
    pooled[...] = pooled[...] / count
    total = jnp.sum(stats[0:1, :])
    first = jnp.sum(sums[0:1, :])
    second = jnp.sum(sums[1:2, :])
    denominator = length.astype(F32) * width
    column = iota(stats.shape, 1)
    values = jnp.where(column == 0, first, jnp.where(column == 1, second, total))
    stats[...] = jnp.sqrt(values / denominator)


def total(*parts):
    value = parts[0].astype(F32)
    for part in parts[1:]:
        value = value + part.astype(F32)
    return value.astype(BF16)


def turn_kernel(meta, keep_a, got_x, keep_b, got_y, on_y, on_x):
    h = on_x.shape[0]
    on_y[...] = total(keep_a[h:], got_x[h:])
    on_x[...] = total(keep_b[h:], got_y[h:])


def add_kernel(meta, a, b, out):
    out[...] = total(a[...], b[...])


def land_half_kernel(meta, keep_a, got_x, last_y, keep_b, got_y, last_x, keep, send):
    h, width = last_x.shape
    upper = total(keep_a[:h], got_x[:h], last_y[:h])
    lower = total(keep_b[:h], got_y[:h], last_x[...])
    first = jnp.broadcast_to(meta[3] % 2 == 0, upper.shape)
    keep[:, :width] = jnp.where(first, upper.astype(F32), lower.astype(F32)).astype(BF16)
    send[:, :width] = jnp.where(first, lower.astype(F32), upper.astype(F32)).astype(BF16)
    if keep.shape[1] > width:
        rows = slice(2 * h, 2 * h + 16)
        small = total(keep_a[rows, 0:128], got_x[rows, 0:128], last_y[h:, 0:128])
        for out in (keep, send):
            out[:, width:] = jnp.zeros((h, 128), BF16)
            out[:16, width:] = small


def halve_kernel(width, meta, a, b, keep, send):
    h = keep.shape[0]
    place_at = pl.multiple_of(h * (meta[3] // 2), 16)
    other_at = pl.multiple_of(h * (1 - meta[3] // 2), 16)
    keep[:, :width] = total(a[pl.ds(place_at, h), :width], b[pl.ds(place_at, h), :width])
    send[:, :width] = total(a[pl.ds(other_at, h), :width], b[pl.ds(other_at, h), :width])
    if width < keep.shape[1]:
        extra = total(a[:h, width:], b[:h, width:])
        keep[:, width:] = extra
        send[:, width:] = extra


def last_kernel(meta, a, b, out, small):
    width = out.shape[1]
    out[...] = total(a[:, :width], b[:, :width])
    small[...] = a[:16, width:].astype(F32) + b[:16, width:].astype(F32)


def join_rows_kernel(meta, own, by_low, by_high, by_both, out):
    h = own.shape[0]
    low, high = meta[3] % 2, meta[3] // 2
    for value, at_low, at_high in (
        (own, low, high),
        (by_low, 1 - low, high),
        (by_high, low, 1 - high),
        (by_both, 1 - low, 1 - high),
    ):
        out[pl.ds(pl.multiple_of(h * (2 * at_low + at_high), 16), h), :] = value[...].astype(F32)


def join_kernel(meta, own, by_low, by_high, by_both, mine, other):
    h = own.shape[0]
    low, high = meta[3] % 2, meta[3] // 2
    for value, at_low, at_high in (
        (own, low, high),
        (by_low, 1 - low, high),
        (by_high, low, 1 - high),
        (by_both, 1 - low, 1 - high),
    ):
        rows = pl.ds(pl.multiple_of(h * at_high, 16), h)

        @pl.when(at_low == meta[2])
        def _(value=value, rows=rows):
            mine[rows, :] = value[...]

        @pl.when(at_low != meta[2])
        def _(value=value, rows=rows):
            other[rows, :] = value[...]


def weave_in_kernel(block, meta, mine, other, out):
    for which, ref in ((meta[2], mine), (1 - meta[2], other)):
        for n in range(ref.shape[1] // block):
            cols = pl.ds(pl.multiple_of((2 * n + which) * block, 128), block)
            out[:, cols] = ref[:, n * block : (n + 1) * block].astype(F32)


def weave_at_kernel(meta, mine, other, *outs):
    half = outs[0].shape[1] // 2
    for which, ref in ((meta[2], mine), (1 - meta[2], other)):
        cols = pl.ds(pl.multiple_of(which * half, 128), half)
        for n, out in enumerate(outs):
            out[:, cols] = ref[:, n * half : (n + 1) * half].astype(F32)


def swap(v, axis, count, far):
    return lax.ppermute(v, axis, [(i, i ^ far) for i in range(count)])


def message_plan(unit):
    h = unit // 2
    plan = []
    for dst, (near, far) in enumerate(((1, 3), (2, 3), (0, 2), (0, 1))):
        offset = 0 if dst in (0, 2) else h
        plan.append((dst, 0, h, unit, near, offset))
        plan.append((dst, h, h, unit, far, offset))
    return plan


class Link:
    def __init__(self, far):
        self.far = far
        self.sent = []

    def send(self, v):
        if len(self.sent) >= 2:
            v = after(v, self.sent[-2])
        got = swap(v, "fsdp", 8, self.far)
        self.sent.append(got)
        return got


def body(
    nf,
    nz,
    hidden_in,
    norm_gain_attn,
    w_query,
    w_key,
    w_value,
    w_out,
    rel_bias,
    norm_gain_ffn,
    w_in,
    w_ffout,
    bucket_index,
    row_lengths,
    prefix_lengths,
    out_cotangent,
    pool_cotangent,
):
    fast = nf == 8 and nz == 4
    size, width = hidden_in.shape
    shard = w_query.shape[0]
    heads = rel_bias.shape[1]
    levels = rel_bias.shape[0] * nf
    full_ff = w_in.shape[1]
    part_ff = full_ff // 2
    block = w_ffout.shape[0]
    half = width // 2
    few = heads // 2
    me = lax.axis_index("fsdp").astype(jnp.int32)
    where = lax.axis_index("dp").astype(jnp.int32)
    core = me & 1
    zero = jnp.zeros((), jnp.int32)

    def by_core(first, second):
        return jnp.where(core == 0, first, second)

    def peer(v):
        return swap(v, "fsdp", nf, 1)

    def dma(n):
        return pltpu.SemaphoreType.DMA((n,))

    def vm(*arrays):
        return [(a, "v") for a in arrays]

    meta = jnp.stack([me, me >> 1, core, where, row_lengths[0], prefix_lengths[0], zero, zero])
    hidden_peer = peer(hidden_in)
    wide = 3 * half
    buckets = jnp.concatenate([bucket_index[::-1], jnp.full((1,), -1, jnp.int32)])[None, :]

    if fast:
        kept_a, given_a, kept_b, given_b, small = call(
            functools.partial(pack_kernel, nf // 2),
            "pack",
            meta,
            [(a, "h") for a in (w_query, w_key, w_value, w_out, w_in)]
            + vm(norm_gain_attn[None], norm_gain_ffn[None], rel_bias),
            [((shard, 4 * half), BF16, "v")] * 2
            + [((shard, part_ff), BF16, "v")] * 2
            + [((8, 128), F32, "v")],
            [pltpu.VMEM(w.shape, BF16) for w in (w_query, w_key, w_value, w_out, w_in)] + [dma(5)],
            limit=56 * 2**20,
        )
        on_x, on_y = Link(2), Link(4)
        taken_a, taken_b = peer(given_a), peer(given_b)
        both_a, both_b = call(
            stack_kernel,
            "stack",
            meta,
            vm(kept_a, taken_a, kept_b, taken_b),
            [((2 * shard, 4 * half), BF16, "v"), ((2 * shard, part_ff), BF16, "v")],
            deps=(hidden_peer,),
            limit=56 * 2**20,
        )

        def near(v):
            return [v, on_x.send(v), on_y.send(v)]

        def distant(three, *deps):
            v, by_x, by_y = three
            h = v.shape[0] // 2
            far_y = on_y.send(after(by_x, *deps)[:h])
            far_x = on_x.send(after(by_y, *deps)[h:])
            return three + [far_y, far_x]

        def rows_of(five):
            h = five[3].shape[0]
            return zip(five, (0, 0, 0, 0, h), (0, 1, 2, 3, 3))

        a_pieces = near(both_a)
        smalls = [small] + [swap(after(small, both_a), "fsdp", nf, far) for far in (2, 4, 6)]
        a_pieces = distant(a_pieces, *smalls)
        (small,) = call(rows_kernel, "rows", meta, vm(*smalls), [((32, 128), F32, "v")])
        smalls = [small, peer(small)]
        a_copies = []
        for number, (piece, row, far) in enumerate(rows_of(a_pieces)):
            rows = piece.shape[0]
            a_copies.append((number, 0, rows, 0, 0, row, 0, wide, 2 * shard, far, 0))
            a_copies.append((number, 0, rows, wide, 1, row, 0, half, 2 * shard, far, 0))
        b_pieces = near(both_b)
    else:

        def whole(v):
            return lax.all_gather(v, "fsdp", axis=0, tiled=True)

        a_full = [whole(w) for w in (w_query, w_key, w_value, w_out)]
        a_full = [by_core(w[:, :half], w[:, half:]) for w in a_full]
        qkv_w, out_half = jnp.concatenate(a_full[:3], axis=1), a_full[3]
        b_full = whole(w_in).reshape(width, nf // 2, 2, block)
        b_pieces = [by_core(b_full[:, :, 0], b_full[:, :, 1]).reshape(width, part_ff)]
        b_copies = [(0, 0, width, 0, 0, 0, 0, part_ff, 0, 0, 0)]
        c_full = whole(w_ffout).reshape(nf // 2, 2, block, width)
        c_pieces = [by_core(c_full[:, 0], c_full[:, 1]).reshape(part_ff, width)]
        c_copies = [(0, 0, part_ff, 0, 0, 0, 0, width, 0, 0, 0)]
        pad = jnp.zeros((1, 128 - shard), BF16)
        rows = [norm_gain_attn[None], norm_gain_ffn[None]]
        rows = [jnp.concatenate([r, pad], axis=1) for r in rows]
        rel = jnp.pad(rel_bias, ((0, 4 - rel_bias.shape[0]), (0, 128 - heads)))
        small = jnp.concatenate(rows + [jnp.zeros((2, 128), BF16), rel], axis=0).astype(F32)
        small = small.at[2].set(row_lengths[0].astype(F32))
        smalls = [whole(small)]

    normed, normed_peer, bias, low, gain_one, gain_two, length_peer = call(
        functools.partial(prepare_kernel, len(smalls), fast, levels),
        "prepare",
        meta,
        vm(hidden_in, hidden_peer, *smalls, buckets, out_cotangent, pool_cotangent),
        [
            ((size, width), BF16, "v"),
            ((size, width), BF16, "v"),
            ((few, 128, 2 * size - 128), F32, "v"),
            ((size, width), BF16, "v"),
            ((1, width), F32, "v"),
            ((1, width), F32, "v"),
            ((1, 128), F32, "v"),
        ],
        [pltpu.VMEM((levels, 128), F32), pltpu.VMEM((128, 2 * size), F32)],
    )
    if fast:
        qkv_w, out_half = call(
            functools.partial(collect_kernel, a_copies, len(a_pieces)),
            "collect",
            meta,
            vm(*a_pieces),
            [((width, wide), BF16, "v"), ((width, half), BF16, "v")],
            deps=(gain_one,),
        )
    out_other = peer(out_half)

    def attend(x, length, name, *deps):
        return call(
            attend_kernel,
            name,
            meta,
            vm(x, bias, qkv_w, length),
            [
                ((size, wide), BF16, "v"),
                ((size, half), BF16, "v"),
                ((size // 2, half), BF16, "v"),
                ((size // 2, half), BF16, "v"),
                ((few, size, size), BF16, "v"),
                ((size, 128), F32, "v"),
            ],
            [pltpu.VMEM((size, size), F32)],
            deps=deps,
        )

    qkv_peer, given_att, *given_halves, powers_peer, sums_peer = attend(
        normed_peer, length_peer, "attend_peer"
    )
    low_peer = peer(after(low, given_att))
    if fast:
        b_pieces = distant(b_pieces, given_att)
        b_copies = [
            (number, 0, piece.shape[0], 0, 0, row, 0, part_ff, 2 * shard, far, 0)
            for number, (piece, row, far) in enumerate(rows_of(b_pieces))
        ]
        c_pieces = near(w_ffout)
    served = tuple(b_pieces[n] for n in (1, 2)) if fast else ()
    length_own = jnp.broadcast_to(row_lengths.astype(F32)[None], (1, 128))
    qkv_own, attended, _, _, powers_own, sums_own = attend(
        normed, length_own, "attend_own", given_att, out_other, *served
    )
    served = tuple(b_pieces[n] for n in (3, 4)) if fast else ()
    got_att = [peer(after(v, attended, *served)) for v in given_halves]
    residual, normed_two, *thirds, sums = call(
        residual_kernel,
        "residual",
        meta,
        vm(hidden_in, attended, *got_att, gain_two, out_half, out_other),
        [((size, width), F32, "v"), ((size, width), BF16, "v")]
        + [((size, width // 3), BF16, "v")] * 3
        + [((8, width), F32, "v")],
        [pltpu.VMEM((width, width), BF16)],
        deps=(low_peer,),
    )
    thirds = [peer(v) for v in thirds]
    shape_in = pltpu.VMEM((width, part_ff), BF16)
    shape_ff = pltpu.VMEM((part_ff, width), BF16)
    if fast:
        ff_plan, in_plan = message_plan(block), message_plan(2 * shard)
        ff_outs = [((block, width), BF16, "v")] * 4
        in_outs = [((2 * shard, part_ff), BF16, "v")] * 4
    else:
        ff_plan = [(0, 0, part_ff, 0, 0, 0)]
        in_plan = [(0, 0, width, 0, 0, 0)]
        ff_outs = [((part_ff, width), BF16, "v")]
        in_outs = [((width, part_ff), BF16, "v")]
    act_own, slope_own, in_w = call(
        functools.partial(expand_kernel, b_copies, len(b_pieces)),
        "expand_own",
        meta,
        vm(normed_two, *b_pieces),
        [((size, part_ff), BF16, "v")] * 2 + [((width, part_ff), BF16, "v")],
        deps=tuple(thirds),
    )
    act_peer, slope_peer, normed_two_peer = call(
        functools.partial(expand_kernel, (), 3),
        "expand_peer",
        meta,
        vm(thirds[0], in_w, *thirds[1:]),
        [((size, part_ff), BF16, "v")] * 2 + [((size, width), BF16, "v")],
    )
    served = tuple(c_pieces[n] for n in (1, 2)) if fast else ()
    if fast:
        c_pieces = distant(c_pieces, act_peer)
        c_copies = [
            (number, 0, piece.shape[0], 0, 0, row, 0, width, block, far, 0)
            for number, (piece, row, far) in enumerate(rows_of(c_pieces))
        ]
    got_att_peer = peer(after(attended, act_peer, *served))
    ff_parts = call(
        functools.partial(product_kernel, ff_plan, len(ff_outs)),
        "product",
        meta,
        vm(act_own, act_peer, low, low_peer),
        ff_outs,
        [shape_ff],
        deps=(got_att_peer,),
    )
    ff_parts = list(ff_parts)
    if fast:
        ff_x = on_x.send(after(ff_parts[0], c_pieces[3], c_pieces[4]))
        ff_y = on_y.send(after(ff_parts[1], c_pieces[3], c_pieces[4]))
    pre_own, pre_peer, part_gn, *send_gn, ff_w = call(
        functools.partial(contract_kernel, c_copies, len(c_pieces)),
        "contract",
        meta,
        vm(slope_own, slope_peer, low, low_peer, in_w, *c_pieces),
        [((size, part_ff), BF16, "v")] * 2
        + [((size, width), F32, "v")]
        + [((size, half), BF16, "v")] * 2
        + [((part_ff, width), BF16, "v")],
        deps=(ff_parts[0],),
    )
    in_parts = call(
        functools.partial(product_kernel, in_plan, len(in_outs)),
        "outer",
        meta,
        vm(normed_two, normed_two_peer, pre_own, pre_peer),
        in_outs,
        [shape_in],
    )
    in_parts = list(in_parts)
    last = in_parts[0]

    def turn(parts, by_x, by_y, *deps):
        h = parts[3].shape[0] // 2
        columns = parts[3].shape[1]
        to_y, to_x = call(
            turn_kernel,
            "turn",
            meta,
            vm(parts[2], by_x, parts[3], by_y),
            [((parts[2].shape[0] - h, columns), BF16, "v"), ((h, columns), BF16, "v")],
            deps=deps,
        )
        return on_y.send(to_y), on_x.send(to_x), to_y

    def add(a, b, *deps):
        (out,) = call(add_kernel, "add", meta, vm(a, b), [(a.shape, BF16, "v")], deps=deps)
        return out

    if fast:
        other_gn = [peer(v) for v in send_gn]
        in_x = on_x.send(after(in_parts[0], ff_x))
        in_y = on_y.send(after(in_parts[1], ff_y))
        last_y, last_x, last = turn(ff_parts, ff_x, ff_y, last)
        ff_last = (last_y, last_x)
    else:
        other_gn = [peer(v) for v in send_gn]
    grad_residual, low_mine, *low_given, grad_keep, grad_send, grad_gain_two = call(
        through_kernel,
        "through",
        meta,
        vm(residual, part_gn, *other_gn, out_cotangent, pool_cotangent, gain_two, out_half, out_other),
        [
            ((size, width), F32, "v"),
            ((size, half), BF16, "v"),
            ((size // 2, half), BF16, "v"),
            ((size // 2, half), BF16, "v"),
            ((size, half), BF16, "v"),
            ((size, half), BF16, "v"),
            ((1, width), F32, "v"),
        ],
        deps=(last,),
    )
    grad_got = peer(grad_send)
    last = grad_gain_two
    head_rows = 8

    def halve_first(parts, by_x, by_y, last_y, last_x, *deps, extra=0):
        rows, columns = parts[3].shape
        keep, send = call(
            land_half_kernel,
            "land",
            meta,
            vm(parts[2], by_x, last_y, parts[3], by_y, last_x),
            [((rows // 2, columns + extra), BF16, "v")] * 2,
            deps=deps,
        )
        return keep, swap(send, "dp", nz, 1)

    def halve_next(keep, got, *deps, extra=0):
        rows, columns = keep.shape
        keep, send = call(
            functools.partial(halve_kernel, columns - extra),
            "halve",
            meta,
            vm(keep, got),
            [((rows // 2, columns), BF16, "v")] * 2,
            deps=deps,
        )
        return keep, swap(send, "dp", nz, 2)

    def quarter(keep, got, *deps):
        own = add(keep, got, *deps)
        return own, swap(own, "dp", nz, 1), swap(own, "dp", nz, 2)

    def quarters(own, by_low, by_high, *deps):
        return own, by_low, by_high, swap(after(by_high, *deps), "dp", nz, 1)

    def shards(four, *deps):
        columns = four[0].shape[1]
        return call(join_kernel, "join", meta, vm(*four), [((shard, columns), BF16, "v")] * 2, deps=deps)

    def attend_back(qkv, powers, g, att, sums, diag, name, *deps):
        return call(
            attend_back_kernel,
            name,
            meta,
            vm(qkv, powers, g, att, sums, diag),
            [((size, wide), BF16, "v"), ((head_rows, 2 * size), F32, "v")],
            [pltpu.VMEM((size, size), BF16), pltpu.VMEM((128, 2 * size), F32)],
            deps=deps,
        )

    diag = jnp.zeros((head_rows, 2 * size), F32)
    dqkv_own, diag = attend_back(
        qkv_own, powers_own, grad_keep, attended, sums_own, diag, "attend_back_own", last
    )
    last = dqkv_own
    if fast:
        last_y, last_x, last = turn(in_parts, in_x, in_y, last)
        in_last = (last_y, last_x)
    dqkv_peer, diag = attend_back(
        qkv_peer, powers_peer, grad_got, given_att, sums_peer, diag, "attend_back_peer", last
    )
    last = diag
    if fast:
        ff_keep, ff_one = halve_first(ff_parts, ff_x, ff_y, *ff_last, last)
        in_keep, in_one = halve_first(in_parts, in_x, in_y, *in_last, ff_keep)
        last = in_keep
        at_plan = message_plan(2 * shard)
        at_plan = at_plan + [(n, 2 * shard, 16, 0, 0, width) for n in (0, 2)]
        at_outs = [((2 * shard + (16 if n in (0, 2) else 0), 4 * half), BF16, "v") for n in range(4)]
    else:
        at_plan = [(0, 0, width + 16, 0, 0, 0)]
        at_outs = [((width + 16, 4 * half), BF16, "v")]
    part_gh, *send_gh, small_grads = call(
        inputs_kernel,
        "inputs",
        meta,
        vm(dqkv_own, dqkv_peer, qkv_w, hidden_in, hidden_peer, grad_gain_two, diag, buckets),
        [((size, width), F32, "v")] + [((size, half), BF16, "v")] * 2 + [((16, 128), F32, "v")],
        [pltpu.VMEM((1, width), F32)],
        deps=(last,),
    )
    low_other = [peer(after(v, part_gh)) for v in low_given]
    other_gh = [peer(v) for v in send_gh]
    at_parts = call(
        functools.partial(weights_kernel, at_plan, len(at_outs)),
        "weights",
        meta,
        vm(
            normed,
            normed_peer,
            dqkv_own,
            dqkv_peer,
            attended,
            *got_att,
            given_att,
            got_att_peer,
            low_mine,
            *low_other,
            small_grads,
        ),
        at_outs,
        [pltpu.VMEM((width + 16, 4 * half), BF16)],
        deps=(part_gh,),
    )
    at_parts = list(at_parts)
    last = at_parts[0]
    if fast:
        at_x = on_x.send(at_parts[0])
        at_y = on_y.send(at_parts[1])
    (grad_hidden,) = call(
        hidden_kernel,
        "hidden",
        meta,
        vm(hidden_in, grad_residual, part_gh, *other_gh, gain_one),
        [((size, width), F32, "v")],
        deps=(last,),
    )
    last = grad_hidden
    if fast:
        ff_keep, ff_two = halve_next(ff_keep, ff_one, last)
        in_keep, in_two = halve_next(in_keep, in_one, ff_keep)
        last = in_keep
    part_branch, *send_branch = call(
        output_kernel,
        "output",
        meta,
        vm(act_own, act_peer, ff_w),
        [((size, width), F32, "v")] + [((size, half), BF16, "v")] * 2,
        deps=(last,),
    )
    last = part_branch

    if fast:
        last_y, last_x, last = turn(at_parts, at_x, at_y, last)
        at_last = (last_y, last_x)
        ff_four = quarter(ff_keep, ff_two, last)
        in_four = quarter(in_keep, in_two, ff_four[0])
        at_keep, at_one = halve_first(at_parts, at_x, at_y, *at_last, in_four[0], extra=128)
        ff_four = quarters(*ff_four, at_keep)
        last = at_keep
        other_branch = [peer(after(v, last)) for v in send_branch]
    else:
        other_branch = [peer(v) for v in send_branch]
    hidden_out, pooled, stats = call(
        finish_kernel,
        "finish",
        meta,
        vm(residual, part_branch, *other_branch, sums),
        [((size, width), BF16, "v"), ((1, width), F32, "v"), ((1, width), F32, "v")],
        deps=(last,),
    )
    last = stats
    if fast:
        at_keep, at_two = halve_next(at_keep, at_one, last, extra=128)
        in_four = quarters(*in_four, at_keep)
        (grad_ffout,) = call(
            join_rows_kernel,
            "join_rows",
            meta,
            vm(*ff_four),
            [((block, width), F32, "v")],
            deps=(at_keep,),
        )
        own_at, small_grads = call(
            last_kernel,
            "last",
            meta,
            vm(at_keep, at_two),
            [((shard // 2, 4 * half), BF16, "v"), ((16, 128), F32, "v")],
            deps=(grad_ffout,),
        )
        at_four = own_at, swap(own_at, "dp", nz, 1), swap(own_at, "dp", nz, 2)
        small_grads = small_grads + peer(small_grads)
        mine_in, other_in = shards(in_four, own_at)
        got_in = peer(other_in)
        at_four = quarters(*at_four, mine_in)
        (grad_in,) = call(
            functools.partial(weave_in_kernel, block),
            "weave_in",
            meta,
            vm(mine_in, got_in),
            [((shard, full_ff), F32, "v")],
        )
        mine_at, other_at = shards(at_four, grad_in)
        got_at = peer(other_at)
        grad_at = call(
            weave_at_kernel, "weave_at", meta, vm(mine_at, got_at), [((shard, width), F32, "v")] * 4
        )
    else:

        def reduced(v):
            v = lax.psum_scatter(v, "fsdp", scatter_dimension=0, tiled=True)
            return lax.psum(v, "dp").astype(F32)

        def spread(v, axis):
            none = jnp.zeros_like(v)
            return by_core(jnp.stack([v, none], axis), jnp.stack([none, v], axis))

        grad_ffout = reduced(
            spread(ff_parts[0].reshape(nf // 2, block, width), 1).reshape(full_ff, width)
        )
        grad_in = reduced(
            spread(in_parts[0].reshape(width, nf // 2, block), 2).reshape(width, full_ff)
        )
        grads = spread(at_parts[0][:width].reshape(width, 4, half), 2).reshape(width, 4 * width)
        grads = reduced(grads)
        grad_at = [grads[:, n * width : (n + 1) * width] for n in range(4)]
        small_grads = lax.psum(small_grads, ("fsdp", "dp"))

    count = width // 128
    rows = levels // nf
    table = small_grads[2 * count :].reshape(-1)[: heads * levels].reshape(heads, levels)
    grad_table = lax.dynamic_slice_in_dim(table, me * rows, rows, 1).T
    gains = small_grads[: 2 * count].reshape(2, width)
    gains = lax.dynamic_slice_in_dim(gains, me * shard, shard, 1)
    return (
        hidden_out,
        pooled,
        grad_hidden,
        gains[0],
        grad_at[0],
        grad_at[1],
        grad_at[2],
        grad_at[3],
        grad_table,
        gains[1],
        grad_in,
        grad_ffout,
        stats[:, :3],
    )


def solution(mesh):
    token = P(("fsdp", "dp"), None)
    weight = P("fsdp", None)
    return jax.shard_map(
        functools.partial(body, mesh.shape["fsdp"], mesh.shape["dp"]),
        mesh=mesh,
        in_specs=(
            token,
            P("fsdp"),
            weight,
            weight,
            weight,
            weight,
            weight,
            P("fsdp"),
            weight,
            weight,
            P(),
            P(("fsdp", "dp")),
            P(("fsdp", "dp")),
            token,
            token,
        ),
        out_specs=(
            token,
            token,
            token,
            P("fsdp"),
            weight,
            weight,
            weight,
            weight,
            weight,
            P("fsdp"),
            weight,
            weight,
            token,
        ),
        check_vma=False,
    )
```

time: 352 us -> 247 us (0.70); the launches traced: 348 us -> 246 us
  waiting for transfers between devices: 114 us -> 80.2 us
  local copies, waits for them, and re-layouts: 43.6 us -> 12.5 us
  blocking collectives: 14.2 us -> 0 us
  other arithmetic: 12.9 us -> 0.08 us
  Pallas kernels: 109 us -> 103 us
    ppermute x9 -> x0, waiting for transfers between devices: 43.7 us -> none  [the longest x3 24.3 us: chain_sum(): back = lax.ppermute(v, 'dp', [(1, 0), (2, 3)])]
    unnamed x193 -> x37, local copies, waits for them, and re-layouts: 27.4 us -> 7.16 us
    ppermute x9 -> x0, starting transfers between devices: 20.2 us -> none  [the longest x3 14.2 us: chain_sum(): v = add(v, lax.ppermute(v, 'dp', [(0, 1), (3, 2)]))]
    ppermute x44 -> x66, starting transfers between devices: 29.3 us -> 48.4 us  [swap(): return lax.ppermute(v, axis, [(i, i ^ far) for i in range(count)])]
    unnamed x1 -> x0, blocking collectives: 14.2 us -> none
    ppermute x44 -> x66, waiting for transfers between devices: 70.6 us -> 80.2 us  [swap(): return lax.ppermute(v, axis, [(i, i ^ far) for i in range(count)])]
    convert_element_type x20 -> x0, other arithmetic: 8.42 us -> none  [the longest x16 5.45 us: add(): return (a.astype(F32) + b.astype(F32)).astype(BF16)]
    pallas_call x12 -> x38, Pallas kernels: 109 us -> 103 us  [call(): pl.pallas_call(kernel, name=name, out_shape=[jax.ShapeDtypeStruct(s, d) f...]
  transfers between devices with their start and end apart: 53 -> 66, of which waited for: 17 -> 32; matrix products, arithmetic and copies ran while one was open for 6% -> 3% of each run, Pallas kernels for 27% -> 37%
where the time goes in v2:
time: 247 us; the launch traced here: 246 us
  Pallas kernels  103 us (42%)
  waiting for transfers between devices  80.2 us (32%)
  starting transfers between devices  48.4 us (20%)
  local copies, waits for them, and re-layouts  12.5 us (5%)
    pallas_call x38, Pallas kernels, call(): pl.pallas_call(kernel, name=name, out_shape=[jax.ShapeDtypeStruct(s, d) f...  103 us
    ppermute x66, waiting for transfers between devices, swap(): return lax.ppermute(v, axis, [(i, i ^ far) for i in range(count)])  80.2 us
    ppermute x66, starting transfers between devices, swap(): return lax.ppermute(v, axis, [(i, i ^ far) for i in range(count)])  48.4 us
    unnamed x37, local copies, waits for them, and re-layouts  7.16 us
  transfers between devices with their start and end apart: 66, of which 32 were waited for; matrix products, arithmetic and copies ran while one was open for 3% of the time, Pallas kernels for 37%

profile of v2, /device:TPU:0, one launch (start us, length us, event | category | flops | bytes accessed | tf_op | source)
XLA Modules:
  0.0 246.3 jit_solution(3504570109395259508)
XLA Ops:
  3.1 3.4 %pack.1 = (bf16[96,1536]{1,0:T(8,128)(2,1)}, bf16[96,1536]{1,0:T(8,128)(2,1)}, bf16[96,1536]{1,0:T(8,128)(2,1)}, bf16[96,1536]{1,0:T(8,128)(2,1)}, f32[8,128]{1,0:T(8,128)}) custom-call(s32[8]{0:T(128)} %stack.20.meta.refs_0_, bf16[96,768]{1,0:T(8,128)(2,1)} %refs_0_.1, bf16[96,768]{1,0:T(8,128)(2,1)} %refs_1_.1, bf16[96,768]{1,0:T(8,128)(2,1)} %refs_2_.1, ...), custom_call_target="tpu_custom_call" | custom-call | flops 1000 | bytes 1000 | tf_op jit(solution)/shard_map/pack/pallas_call | solution.py:43
  16.5 3.0 %collective-permute-start.5 = (f32[8,128]{1,0:T(8,128)}, f32[8,128]{1,0:T(8,128)S(1)}, u32[]{:S(2)}, u32[]{:S(2)}) collective-permute-start(f32[8,128]{1,0:T(8,128)} %get-tuple-element.197.refs_0_), channel_id=1, source_target_pairs={{0,24},{4,28},{8,16},{12,20},{16,8},{20,12},{24,0},{28,4},{1,25},{... | collective-permute-start | bytes 12296 | tf_op jit(solution)/shard_map/ppermute | solution.py:698
  19.4 9.2 %collective-permute-done.3.refs_1_ = f32[8,128]{1,0:T(8,128)S(1)} collective-permute-done((f32[8,128]{1,0:T(8,128)}, f32[8,128]{1,0:T(8,128)S(1)}, u32[]{:S(2)}, u32[]{:S(2)}) %collective-permute-start.3) | collective-permute-done | bytes 4128 | tf_op jit(solution)/shard_map/ppermute | solution.py:698
  42.2 5.0 %prepare.1 = (bf16[512,768]{1,0:T(8,128)(2,1)S(1)}, bf16[512,768]{1,0:T(8,128)(2,1)S(1)}, f32[6,128,896]{2,1,0:T(8,128)S(1)}, bf16[512,768]{1,0:T(8,128)(2,1)S(1...) custom-call(s32[8]{0:T(128)S(1)} %copy-done.4, bf16[512,768]{1,0:T(8,128)(2,1)S(1)} %copy-done, ...), custom_call_target="tpu_custom_call" | custom-call | flops 1000 | bytes 1000 | tf_op jit(solution)/shard_map/prepare/pallas_call | solution.py:43
  48.7 6.7 %attend_peer.1 = (bf16[512,1152]{1,0:T(8,128)(2,1)S(1)}, bf16[512,384]{1,0:T(8,128)(2,1)S(1)}, bf16[256,384]{1,0:T(8,128)(2,1)S(1)}, bf16[256,384]{1,0:T(8,128)(...) custom-call(s32[8]{0:T(128)S(1)} %copy-done.4, ...), custom_call_target="tpu_custom_call" | custom-call | flops 1000 | bytes 1000 | tf_op jit(solution)/shard_map/attend_peer/pallas_call | solution.py:43
  62.1 7.5 %attend_own.1 = (bf16[512,1152]{1,0:T(8,128)(2,1)S(1)}, bf16[512,384]{1,0:T(8,128)(2,1)S(1)}, bf16[256,384]{1,0:T(8,128)(2,1)}, bf16[256,384]{1,0:T(8,128)(2,1)}...) custom-call(s32[8]{0:T(128)S(1)} %copy-done.4, bf16[512,768]{1,0:T(8,128)(2,1)S(1)} %get-tuple-element.215.x_ref.refs_1_, ...), custom_call_target="tpu_custom_call" | custom-call | flops 1000 | bytes 1000 | tf_op jit(solution)/shard_map/attend_own/pallas_call | solution.py:43
  76.7 4.1 %expand_own.1 = (bf16[512,1536]{1,0:T(8,128)(2,1)S(1)}, bf16[512,1536]{1,0:T(8,128)(2,1)S(1)}, bf16[768,1536]{1,0:T(8,128)(2,1)S(1)}) custom-call(s32[8]{0:T(128)S(1)} %copy-done.4, bf16[512,768]{1,0:T(8,128)(2,1)S(1)} %get-tuple-element.226.refs_1_, bf16[192,1536]{1,0:T(8,128)(2,1)S(1)} %copy-done.7, bf16[192,1536]{1,0:T(8,128)(2,1)} %collective-permute-done.13.refs_3_, ...), custom_call_target="tpu_custom_call" | custom-call | flops 1000 | bytes 111001000 | tf_op jit(solution)/shard_map/expand_own/pallas_call | solution.py:43
  80.8 3.5 %expand_peer.1 = (bf16[512,1536]{1,0:T(8,128)(2,1)S(1)}, bf16[512,1536]{1,0:T(8,128)(2,1)S(1)}, bf16[512,768]{1,0:T(8,128)(2,1)S(1)}) custom-call(s32[8]{0:T(128)S(1)} %copy-done.4, bf16[512,256]{1,0:T(8,128)(2,1)S(1)} %collective-permute-done.19.refs_1_, bf16[768,1536]{1,0:T(8,128)(2,1)S(1)} %get-tuple-element.231.refs_2_.refs_5_, ...), custom_call_target="tpu_custom_call" | custom-call | flops 1000 | bytes 1000 | tf_op jit(solution)/shard_map/expand_peer/pallas_call | solution.py:43
  86.8 4.3 %product.1 = (bf16[384,768]{1,0:T(8,128)(2,1)}, bf16[384,768]{1,0:T(8,128)(2,1)}, bf16[384,768]{1,0:T(8,128)(2,1)S(1)}, bf16[384,768]{1,0:T(8,128)(2,1)S(1)}) custom-call(s32[8]{0:T(128)S(1)} %copy-done.4, bf16[512,1536]{1,0:T(8,128)(2,1)S(1)} %get-tuple-element.238.refs_1_.act_own, bf16[512,1536]{1,0:T(8,128)(2,1)S(1)} %get-tuple-element.233.refs_2_.act_peer, ...), custom_call_target="tpu_custom_call" | custom-call | flops 1000 | bytes 1000 | tf_op jit(solution)/shard_map/product/pallas_call | solution.py:43
  96.3 7.2 %contract.1 = (bf16[512,1536]{1,0:T(8,128)(2,1)S(1)}, bf16[512,1536]{1,0:T(8,128)(2,1)S(1)}, f32[512,768]{1,0:T(8,128)S(1)}, bf16[512,384]{1,0:T(8,128)(2,1)S(1)...) custom-call(s32[8]{0:T(128)S(1)} %copy-done.4, bf16[512,1536]{1,0:T(8,128)(2,1)S(1)} %get-tuple-element.241.refs_1_, ...), custom_call_target="tpu_custom_call" | custom-call | flops 1000 | bytes 1000 | tf_op jit(solution)/shard_map/contract/pallas_call | solution.py:43
  103.5 3.3 %outer.1 = (bf16[192,1536]{1,0:T(8,128)(2,1)S(1)}, bf16[192,1536]{1,0:T(8,128)(2,1)S(1)}, bf16[192,1536]{1,0:T(8,128)(2,1)S(1)}, bf16[192,1536]{1,0:T(8,128)(2,1)S(1)}) custom-call(s32[8]{0:T(128)S(1)} %copy-done.4, bf16[512,768]{1,0:T(8,128)(2,1)S(1)} %get-tuple-element.226.refs_1_, bf16[512,768]{1,0:T(8,128)(2,1)S(1)} %get-tuple-element.232.refs_2_, ...), custom_call_target="tpu_custom_call" | custom-call | flops 1000 | bytes 1000 | tf_op jit(solution)/shard_map/outer/pallas_call | solution.py:43
  113.4 3.6 %through.1 = (f32[512,768]{1,0:T(8,128)S(1)}, bf16[512,384]{1,0:T(8,128)(2,1)S(1)}, bf16[256,384]{1,0:T(8,128)(2,1)S(1)}, bf16[256,384]{1,0:T(8,128)(2,1)S(1)}, ...) custom-call(s32[8]{0:T(128)S(1)} %copy-done.4, ...), custom_call_target="tpu_custom_call" | custom-call | flops 1000 | bytes 1000 | tf_op jit(solution)/shard_map/through/pallas_call | solution.py:43
  117.2 8.7 %attend_back_own.1 = (bf16[512,1152]{1,0:T(8,128)(2,1)S(1)}, f32[8,1024]{1,0:T(8,128)S(1)}) custom-call(s32[8]{0:T(128)S(1)} %copy-done.4, bf16[512,1152]{1,0:T(8,128)(2,1)S(1)} %copy-done.3, bf16[6,512,512]{2,1,0:T(8,128)(2,1)S(1)} %get-tuple-element.267.powers, bf16[512,384]{1,0:T(8,128)(2,1)S(1)} %get-tuple-element.268.g_ref, ...), custom_call_target="tpu_custom_call" | custom-call | flops 1000 | bytes 1000 | tf_op jit(solution)/shard_map/attend_back_own/pallas_call | solution.py:43
  130.9 9.0 %attend_back_peer.1 = (bf16[512,1152]{1,0:T(8,128)(2,1)S(1)}, f32[8,1024]{1,0:T(8,128)S(1)}) custom-call(s32[8]{0:T(128)S(1)} %copy-done.4, bf16[512,1152]{1,0:T(8,128)(2,1)S(1)} %get-tuple-element.281.qkv, bf16[6,512,512]{2,1,0:T(8,128)(2,1)S(1)} %get-tuple-element.282.powers, bf16[512,384]{1,0:T(8,128)(2,1)S(1)} %collective-permute-done.33.g_ref, ...), custom_call_target="tpu_custom_call" | custom-call | flops 1000 | bytes 1000 | tf_op jit(solution)/shard_map/attend_back_peer/pallas_call | solution.py:43
  143.6 4.1 %inputs.1 = (f32[512,768]{1,0:T(8,128)S(1)}, bf16[512,384]{1,0:T(8,128)(2,1)S(1)}, bf16[512,384]{1,0:T(8,128)(2,1)S(1)}, f32[16,128]{1,0:T(8,128)S(1)}) custom-call(s32[8]{0:T(128)S(1)} %copy-done.4, bf16[512,1152]{1,0:T(8,128)(2,1)S(1)} %get-tuple-element.270.dqkv_own.refs_3_, bf16[512,1152]{1,0:T(8,128)(2,1)S(1)} %get-tuple-element.298.dqkv_peer.refs_4_, ...), custom_call_target="tpu_custom_call" | custom-call | flops 1000 | bytes 1000 | tf_op jit(solution)/shard_map/inputs/pallas_call | solution.py:43
  149.5 3.8 %weights.1 = (bf16[208,1536]{1,0:T(8,128)(2,1)S(1)}, bf16[192,1536]{1,0:T(8,128)(2,1)S(1)}, bf16[208,1536]{1,0:T(8,128)(2,1)S(1)}, bf16[192,1536]{1,0:T(8,128)(2,1)S(1)}) custom-call(s32[8]{0:T(128)S(1)} %copy-done.4, bf16[512,768]{1,0:T(8,128)(2,1)S(1)} %get-tuple-element.215.x_ref.refs_1_, bf16[512,768]{1,0:T(8,128)(2,1)S(1)} %get-tuple-element.199.x_ref.refs_2_, ...), custom_call_target="tpu_custom_call" | custom-call | flops 1000 | bytes 1000 | tf_op jit(solution)/shard_map/weights/pallas_call | solution.py:43
  159.9 5.3 %collective-permute-done.42.b = bf16[192,768]{1,0:T(8,128)(2,1)S(1)} collective-permute-done((bf16[192,768]{1,0:T(8,128)(2,1)S(1)}, bf16[192,768]{1,0:T(8,128)(2,1)S(1)}, u32[]{:S(2)}, u32[]{:S(2)}) %collective-permute-start.42) | collective-permute-done | bytes 294944 | tf_op jit(solution)/shard_map/ppermute | solution.py:698
  165.8 5.3 %collective-permute-done.43.b = bf16[96,1536]{1,0:T(8,128)(2,1)S(1)} collective-permute-done((bf16[96,1536]{1,0:T(8,128)(2,1)S(1)}, bf16[96,1536]{1,0:T(8,128)(2,1)S(1)}, u32[]{:S(2)}, u32[]{:S(2)}) %collective-permute-start.43) | collective-permute-done | bytes 294944 | tf_op jit(solution)/shard_map/ppermute | solution.py:698
  171.7 3.6 %output.1 = (f32[512,768]{1,0:T(8,128)S(1)}, bf16[512,384]{1,0:T(8,128)(2,1)S(1)}, bf16[512,384]{1,0:T(8,128)(2,1)S(1)}) custom-call(s32[8]{0:T(128)S(1)} %copy-done.4, bf16[512,1536]{1,0:T(8,128)(2,1)S(1)} %get-tuple-element.238.refs_1_.act_own, bf16[512,1536]{1,0:T(8,128)(2,1)S(1)} %get-tuple-element.233.refs_2_.act_peer, ...), custom_call_target="tpu_custom_call" | custom-call | flops 1000 | bytes 1000 | tf_op jit(solution)/shard_map/output/pallas_call | solution.py:43
  181.1 10.4 %collective-permute-done.46.b = bf16[96,768]{1,0:T(8,128)(2,1)S(1)} collective-permute-done((bf16[96,768]{1,0:T(8,128)(2,1)S(1)}, bf16[96,768]{1,0:T(8,128)(2,1)S(1)}, u32[]{:S(2)}, u32[]{:S(2)}) %collective-permute-start.46) | collective-permute-done | bytes 147488 | tf_op jit(solution)/shard_map/ppermute | solution.py:698
  196.2 3.4 %collective-permute-start.54 = (bf16[96,768]{1,0:T(8,128)(2,1)S(1)}, bf16[96,768]{1,0:T(8,128)(2,1)S(1)}, u32[]{:S(2)}, u32[]{:S(2)}) collective-permute-start(bf16[96,768]{1,0:T(8,128)(2,1)S(1)} %add.16.own), channel_id=1, source_target_pairs={{0,2},{1,3},{2,0},{3,1},{4,6},{5,7},{6,4},{7,5},{8,10},{9,11},{10,... | collective-permute-start | bytes 442376 | tf_op jit(solution)/shard_map/ppermute | solution.py:698
  201.6 9.8 %collective-permute-done.52.b = bf16[96,1664]{1,0:T(8,128)(2,1)S(1)} collective-permute-done((bf16[96,1664]{1,0:T(8,128)(2,1)S(1)}, bf16[96,1664]{1,0:T(8,128)(2,1)S(1)}, u32[]{:S(2)}, u32[]{:S(2)}) %collective-permute-start.52) | collective-permute-done | bytes 319520 | tf_op jit(solution)/shard_map/ppermute | solution.py:698
  216.8 6.0 %collective-permute-done.53.by_low = bf16[96,768]{1,0:T(8,128)(2,1)S(1)} collective-permute-done((bf16[96,768]{1,0:T(8,128)(2,1)S(1)}, bf16[96,768]{1,0:T(8,128)(2,1)S(1)}, u32[]{:S(2)}, u32[]{:S(2)}) %collective-permute-start.53) | collective-permute-done | bytes 147488 | tf_op jit(solution)/shard_map/ppermute | solution.py:698
  222.8 3.2 %collective-permute-done.55.by_both = bf16[96,768]{1,0:T(8,128)(2,1)S(1)} collective-permute-done((bf16[96,768]{1,0:T(8,128)(2,1)S(1)}, bf16[96,768]{1,0:T(8,128)(2,1)S(1)}, u32[]{:S(2)}, u32[]{:S(2)}) %collective-permute-start.55) | collective-permute-done | bytes 147488 | tf_op jit(solution)/shard_map/ppermute | solution.py:698
  (202 shorter events, 110.5 us)
Async XLA Ops:
  11.8 19.5 %collective-permute-start.7 = (bf16[192,1536]{1,0:T(8,128)(2,1)}, bf16[192,1536]{1,0:T(8,128)(2,1)S(1)}, u32[]{:S(2)}, u32[]{:S(2)}) collective-permute-start(bf16[192,1536]{1,0:T(8,128)(2,1)} %get-tuple-element.196.refs_1_), channel_id=1, source_target_pairs={{0,8},{4,12},{8,0},{12,4},{16,24},{20,28},{24,16},{28,20},{1,9},{5... | collective-permute-start | bytes 1769480 | tf_op jit(solution)/shard_map/ppermute | solution.py:698
  14.4 19.1 %collective-permute-start.8 = (bf16[192,1536]{1,0:T(8,128)(2,1)}, bf16[192,1536]{1,0:T(8,128)(2,1)S(1)}, u32[]{:S(2)}, u32[]{:S(2)}) collective-permute-start(bf16[192,1536]{1,0:T(8,128)(2,1)} %get-tuple-element.196.refs_1_), channel_id=1, source_target_pairs={{0,16},{4,20},{8,24},{12,28},{16,0},{20,4},{24,8},{28,12},{1,17},{... | collective-permute-start | bytes 1769480 | tf_op jit(solution)/shard_map/ppermute | solution.py:698
  16.5 14.2 %collective-permute-start.5 = (f32[8,128]{1,0:T(8,128)}, f32[8,128]{1,0:T(8,128)S(1)}, u32[]{:S(2)}, u32[]{:S(2)}) collective-permute-start(f32[8,128]{1,0:T(8,128)} %get-tuple-element.197.refs_0_), channel_id=1, source_target_pairs={{0,24},{4,28},{8,16},{12,20},{16,8},{20,12},{24,0},{28,4},{1,25},{... | collective-permute-start | bytes 12296 | tf_op jit(solution)/shard_map/ppermute | solution.py:698
  32.0 15.2 %collective-permute-start.9 = (bf16[96,1536]{1,0:T(8,128)(2,1)}, bf16[96,1536]{1,0:T(8,128)(2,1)}, u32[]{:S(2)}, u32[]{:S(2)}) collective-permute-start(bf16[96,1536]{1,0:T(8,128)(2,1)} %slice.36), channel_id=1, source_target_pairs={{0,16},{4,20},{8,24},{12,28},{16,0},{20,4},{24,8},{28,12},{1,17},{... | collective-permute-start | bytes 884744 | tf_op jit(solution)/shard_map/ppermute | solution.py:698
  34.8 21.1 %collective-permute-start.13 = (bf16[192,1536]{1,0:T(8,128)(2,1)}, bf16[192,1536]{1,0:T(8,128)(2,1)}, u32[]{:S(2)}, u32[]{:S(2)}) collective-permute-start(bf16[192,1536]{1,0:T(8,128)(2,1)} %get-tuple-element.213.refs_2_), channel_id=1, source_target_pairs={{0,8},{4,12},{8,0},{12,4},{16,24},{20,28},{24,16},{28,20},{1,9},{5... | collective-permute-start | bytes 1769480 | tf_op jit(solution)/shard_map/ppermute | solution.py:698
  36.3 22.1 %collective-permute-start.14 = (bf16[192,1536]{1,0:T(8,128)(2,1)}, bf16[192,1536]{1,0:T(8,128)(2,1)}, u32[]{:S(2)}, u32[]{:S(2)}) collective-permute-start(bf16[192,1536]{1,0:T(8,128)(2,1)} %get-tuple-element.213.refs_2_), channel_id=1, source_target_pairs={{0,16},{4,20},{8,24},{12,28},{16,0},{20,4},{24,8},{28,12},{1,17},{... | collective-permute-start | bytes 1769480 | tf_op jit(solution)/shard_map/ppermute | solution.py:698
  55.5 15.7 %collective-permute-start.11 = (bf16[512,768]{1,0:T(8,128)(2,1)S(1)}, bf16[512,768]{1,0:T(8,128)(2,1)S(1)}, u32[]{:S(2)}, u32[]{:S(2)}) collective-permute-start(bf16[512,768]{1,0:T(8,128)(2,1)S(1)} %get-tuple-element.208.refs_3_), channel_id=1, source_target_pairs={{0,4},{4,0},{8,12},{12,8},{16,20},{20,16},{24,28},{28,24},{1,5},{5... | collective-permute-start | bytes 2359304 | tf_op jit(solution)/shard_map/ppermute | solution.py:698
  60.1 24.2 %collective-permute-start.22 = (bf16[384,768]{1,0:T(8,128)(2,1)S(1)}, bf16[384,768]{1,0:T(8,128)(2,1)S(1)}, u32[]{:S(2)}, u32[]{:S(2)}) collective-permute-start(bf16[384,768]{1,0:T(8,128)(2,1)S(1)} %copy-done.5), channel_id=1, source_target_pairs={{0,8},{4,12},{8,0},{12,4},{16,24},{20,28},{24,16},{28,20},{1,9},{5... | collective-permute-start | bytes 1769480 | tf_op jit(solution)/shard_map/ppermute | solution.py:698
  61.5 22.7 %collective-permute-start.23 = (bf16[384,768]{1,0:T(8,128)(2,1)S(1)}, bf16[384,768]{1,0:T(8,128)(2,1)S(1)}, u32[]{:S(2)}, u32[]{:S(2)}) collective-permute-start(bf16[384,768]{1,0:T(8,128)(2,1)S(1)} %copy-done.5), channel_id=1, source_target_pairs={{0,16},{4,20},{8,24},{12,28},{16,0},{20,4},{24,8},{28,12},{1,17},{... | collective-permute-start | bytes 1769480 | tf_op jit(solution)/shard_map/ppermute | solution.py:698
  95.2 14.6 %collective-permute-start.27 = (bf16[384,768]{1,0:T(8,128)(2,1)}, bf16[384,768]{1,0:T(8,128)(2,1)S(1)}, u32[]{:S(2)}, u32[]{:S(2)}) collective-permute-start(bf16[384,768]{1,0:T(8,128)(2,1)} %get-tuple-element.253), channel_id=1, source_target_pairs={{0,8},{4,12},{8,0},{12,4},{16,24},{20,28},{24,16},{28,20},{1,9},{5... | collective-permute-start | bytes 1769480 | tf_op jit(solution)/shard_map/ppermute | solution.py:698
  95.7 14.6 %collective-permute-start.28 = (bf16[384,768]{1,0:T(8,128)(2,1)}, bf16[384,768]{1,0:T(8,128)(2,1)S(1)}, u32[]{:S(2)}, u32[]{:S(2)}) collective-permute-start(bf16[384,768]{1,0:T(8,128)(2,1)} %get-tuple-element.257), channel_id=1, source_target_pairs={{0,16},{4,20},{8,24},{12,28},{16,0},{20,4},{24,8},{28,12},{1,17},{... | collective-permute-start | bytes 1769480 | tf_op jit(solution)/shard_map/ppermute | solution.py:698
  109.8 19.2 %collective-permute-start.31 = (bf16[192,1536]{1,0:T(8,128)(2,1)S(1)}, bf16[192,1536]{1,0:T(8,128)(2,1)S(1)}, u32[]{:S(2)}, u32[]{:S(2)}) collective-permute-start(bf16[192,1536]{1,0:T(8,128)(2,1)S(1)} %get-tuple-element.274), channel_id=1, source_target_pairs={{0,8},{4,12},{8,0},{12,4},{16,24},{20,28},{24,16},{28,20},{1,9},{5... | collective-permute-start | bytes 1769480 | tf_op jit(solution)/shard_map/ppermute | solution.py:698
  110.3 18.6 %collective-permute-start.32 = (bf16[192,1536]{1,0:T(8,128)(2,1)S(1)}, bf16[192,1536]{1,0:T(8,128)(2,1)S(1)}, u32[]{:S(2)}, u32[]{:S(2)}) collective-permute-start(bf16[192,1536]{1,0:T(8,128)(2,1)S(1)} %get-tuple-element.278), channel_id=1, source_target_pairs={{0,16},{4,20},{8,24},{12,28},{16,0},{20,4},{24,8},{28,12},{1,17},{... | collective-permute-start | bytes 1769480 | tf_op jit(solution)/shard_map/ppermute | solution.py:698
  153.3 22.1 %collective-permute-start.44 = (bf16[208,1536]{1,0:T(8,128)(2,1)S(1)}, bf16[208,1536]{1,0:T(8,128)(2,1)S(1)}, u32[]{:S(2)}, u32[]{:S(2)}) collective-permute-start(bf16[208,1536]{1,0:T(8,128)(2,1)S(1)} %get-tuple-element.323), channel_id=1, source_target_pairs={{0,8},{4,12},{8,0},{12,4},{16,24},{20,28},{24,16},{28,20},{1,9},{5... | collective-permute-start | bytes 1916936 | tf_op jit(solution)/shard_map/ppermute | solution.py:698
  154.8 20.5 %collective-permute-start.45 = (bf16[192,1536]{1,0:T(8,128)(2,1)S(1)}, bf16[192,1536]{1,0:T(8,128)(2,1)S(1)}, u32[]{:S(2)}, u32[]{:S(2)}) collective-permute-start(bf16[192,1536]{1,0:T(8,128)(2,1)S(1)} %get-tuple-element.326), channel_id=1, source_target_pairs={{0,16},{4,20},{8,24},{12,28},{16,0},{20,4},{24,8},{28,12},{1,17},{... | collective-permute-start | bytes 1769480 | tf_op jit(solution)/shard_map/ppermute | solution.py:698
  157.0 14.2 %collective-permute-start.43 = (bf16[96,1536]{1,0:T(8,128)(2,1)S(1)}, bf16[96,1536]{1,0:T(8,128)(2,1)S(1)}, u32[]{:S(2)}, u32[]{:S(2)}) collective-permute-start(bf16[96,1536]{1,0:T(8,128)(2,1)S(1)} %get-tuple-element.316), channel_id=1, source_target_pairs={{0,1},{1,0},{2,3},{3,2},{4,5},{5,4},{6,7},{7,6},{8,9},{9,8},{10,11... | collective-permute-start | bytes 884744 | tf_op jit(solution)/shard_map/ppermute | solution.py:698
  176.1 18.0 %collective-permute-start.48 = (bf16[112,1536]{1,0:T(8,128)(2,1)S(1)}, bf16[112,1536]{1,0:T(8,128)(2,1)S(1)}, u32[]{:S(2)}, u32[]{:S(2)}) collective-permute-start(bf16[112,1536]{1,0:T(8,128)(2,1)S(1)} %get-tuple-element.333), channel_id=1, source_target_pairs={{0,16},{4,20},{8,24},{12,28},{16,0},{20,4},{24,8},{28,12},{1,17},{... | collective-permute-start | bytes 1032200 | tf_op jit(solution)/shard_map/ppermute | solution.py:698
  177.7 16.4 %collective-permute-start.49 = (bf16[96,1536]{1,0:T(8,128)(2,1)S(1)}, bf16[96,1536]{1,0:T(8,128)(2,1)S(1)}, u32[]{:S(2)}, u32[]{:S(2)}) collective-permute-start(bf16[96,1536]{1,0:T(8,128)(2,1)S(1)} %get-tuple-element.335), channel_id=1, source_target_pairs={{0,8},{4,12},{8,0},{12,4},{16,24},{20,28},{24,16},{28,20},{1,9},{5... | collective-permute-start | bytes 884744 | tf_op jit(solution)/shard_map/ppermute | solution.py:698
  195.5 15.8 %collective-permute-start.52 = (bf16[96,1664]{1,0:T(8,128)(2,1)S(1)}, bf16[96,1664]{1,0:T(8,128)(2,1)S(1)}, u32[]{:S(2)}, u32[]{:S(2)}) collective-permute-start(bf16[96,1664]{1,0:T(8,128)(2,1)S(1)} %get-tuple-element.347), channel_id=1, source_target_pairs={{0,1},{1,0},{2,3},{3,2},{4,5},{5,4},{6,7},{7,6},{8,9},{9,8},{10,11... | collective-permute-start | bytes 958472 | tf_op jit(solution)/shard_map/ppermute | solution.py:698
  196.2 18.6 %collective-permute-start.54 = (bf16[96,768]{1,0:T(8,128)(2,1)S(1)}, bf16[96,768]{1,0:T(8,128)(2,1)S(1)}, u32[]{:S(2)}, u32[]{:S(2)}) collective-permute-start(bf16[96,768]{1,0:T(8,128)(2,1)S(1)} %add.16.own), channel_id=1, source_target_pairs={{0,2},{1,3},{2,0},{3,1},{4,6},{5,7},{6,4},{7,5},{8,10},{9,11},{10,... | collective-permute-start | bytes 442376 | tf_op jit(solution)/shard_map/ppermute | solution.py:698
  199.6 17.2 %collective-permute-start.59 = (bf16[48,1536]{1,0:T(8,128)(2,1)S(1)}, bf16[48,1536]{1,0:T(8,128)(2,1)S(1)}, u32[]{:S(2)}, u32[]{:S(2)}) collective-permute-start(bf16[48,1536]{1,0:T(8,128)(2,1)S(1)} %add.17.own), channel_id=1, source_target_pairs={{0,2},{1,3},{2,0},{3,1},{4,6},{5,7},{6,4},{7,5},{8,10},{9,11},{10,... | collective-permute-start | bytes 442376 | tf_op jit(solution)/shard_map/ppermute | solution.py:698
  212.0 15.7 %collective-permute-start.56 = (bf16[48,1664]{1,0:T(8,128)(2,1)S(1)}, bf16[48,1664]{1,0:T(8,128)(2,1)S(1)}, u32[]{:S(2)}, u32[]{:S(2)}) collective-permute-start(bf16[48,1664]{1,0:T(8,128)(2,1)S(1)} %get-tuple-element.352), channel_id=1, source_target_pairs={{0,2},{1,3},{2,0},{3,1},{4,6},{5,7},{6,4},{7,5},{8,10},{9,11},{10,... | collective-permute-start | bytes 479240 | tf_op jit(solution)/shard_map/ppermute | solution.py:698
  214.8 15.1 %collective-permute-start.58 = (bf16[48,1536]{1,0:T(8,128)(2,1)S(1)}, bf16[48,1536]{1,0:T(8,128)(2,1)S(1)}, u32[]{:S(2)}, u32[]{:S(2)}) collective-permute-start(bf16[48,1536]{1,0:T(8,128)(2,1)S(1)} %add.17.own), channel_id=1, source_target_pairs={{0,1},{1,0},{2,3},{3,2},{4,5},{5,4},{6,7},{7,6},{8,9},{9,8},{10,11... | collective-permute-start | bytes 442376 | tf_op jit(solution)/shard_map/ppermute | solution.py:698
  216.8 15.4 %collective-permute-start.60 = (bf16[48,1536]{1,0:T(8,128)(2,1)S(1)}, bf16[48,1536]{1,0:T(8,128)(2,1)S(1)}, u32[]{:S(2)}, u32[]{:S(2)}) collective-permute-start(bf16[48,1536]{1,0:T(8,128)(2,1)S(1)} %collective-permute-done.59.by_high), channel_id=1, source_target_pairs={{0,1},{1,0},{2,3},{3,2},{4,5},{5,4},{6,7},{7,6},{8,9},{9,8},{10,11... | collective-permute-start | bytes 442376 | tf_op jit(solution)/shard_map/ppermute | solution.py:698
  (59 other events, 520.6 us)

commit v3 on v2

--- a/solution.py
+++ b/solution.py
@@ -89,19 +89,31 @@
         outs[dst][row : row + rows, :] = scratch[pl.ds(start, rows), :]
 
 
+def small_block(meta, gain_one, gain_two, rel):
+    row, lane = iota((16, 128), 0), iota((16, 128), 1)
+    block = jnp.where((row == 2) & (lane == 0), (meta[4] // 256).astype(F32), 0.0)
+    block = jnp.where((row == 2) & (lane == 1), (meta[4] % 256).astype(F32), block)
+    parts = [(0, gain_one), (1, gain_two)] + [(4 + n, rel[n : n + 1, :]) for n in range(rel.shape[0])]
+    for at, value in parts:
+        value = value[...].astype(F32)
+        wide = jnp.concatenate([value, jnp.zeros((1, 128 - value.shape[1]), F32)], axis=1)
+        block = jnp.where(row == at, wide, block)
+    return block.astype(BF16)
+
+
 def pack_kernel(n_chips, meta, *refs):
     sources = refs[:5]
     gain_one, gain_two, rel = refs[5:8]
-    kept_a, given_a, kept_b, given_b, small = refs[8:13]
-    held, sems = refs[13:18], refs[18]
+    kept_a, given_a, kept_b, given_b = refs[8:12]
+    held, sems = refs[12:17], refs[17]
     handles = [pltpu.make_async_copy(a, b, sems.at[n]) for n, (a, b) in enumerate(zip(sources, held))]
     for handle in handles:
         handle.start()
-    small[...] = jnp.zeros_like(small)
-    small[0:1, 0 : gain_one.shape[1]] = gain_one[...].astype(F32)
-    small[1:2, 0 : gain_two.shape[1]] = gain_two[...].astype(F32)
-    small[2:3, :] = jnp.broadcast_to(meta[4].astype(F32), (1, 128))
-    small[4 : 4 + rel.shape[0], 0 : rel.shape[1]] = rel[...].astype(F32)
+    width = 4 * (held[0].shape[1] // 2)
+    block = small_block(meta, gain_one, gain_two, rel)
+    for out in (kept_a, given_a):
+        out[:, width:] = jnp.zeros((out.shape[0], 128), BF16)
+        out[0:16, width:] = block
     for handle in handles:
         handle.wait()
     wq, wk, wv, wo, w_in = held
@@ -117,43 +129,63 @@
             b_ref[:, n * block : (n + 1) * block] = w_in[:, cols]
 
 
-def stack_kernel(meta, kept_a, taken_a, kept_b, taken_b, both_a, both_b):
-    shard = kept_a.shape[0]
-    mine = pl.ds(pl.multiple_of(shard * meta[2], 16), shard)
-    theirs = pl.ds(pl.multiple_of(shard * (1 - meta[2]), 16), shard)
-    for kept, taken, both in ((kept_a, taken_a, both_a), (kept_b, taken_b, both_b)):
-        both[mine, :] = kept[...]
-        both[theirs, :] = taken[...]
-
-
-def rows_kernel(meta, *refs):
-    for n, ref in enumerate(refs[:-1]):
-        refs[-1][8 * n : 8 * n + 8, :] = ref[...]
-
-
-def prepare_kernel(n_small, relative, levels, meta, hidden, hidden_peer, *refs):
-    smalls = refs[:n_small]
-    buckets, out_cot, pool_cot = refs[n_small : n_small + 3]
-    normed, normed_peer, bias, low, gain_one, gain_two, length_peer, table, table_rows = refs[n_small + 3 :]
-    size, width = hidden.shape
+def stack_kernel(meta, kept, taken, both):
+    shard = kept.shape[0]
+    both[pl.ds(pl.multiple_of(shard * meta[2], 16), shard), :] = kept[...]
+    both[pl.ds(pl.multiple_of(shard * (1 - meta[2]), 16), shard), :] = taken[...]
+
+
+def cut_kernel(meta, by_x, by_y, upper, lower):
+    h = upper.shape[0]
+    upper[...] = by_x[:h, :]
+    lower[...] = by_y[h:, :]
+
+
+def low_kernel(meta, out_cot, pool_cot, low):
+    size = low.shape[0]
     length, prefix = meta[4], meta[5]
     count = (length - prefix).astype(F32)
-    pieces = [ref[8 * n : 8 * n + 8, :] for ref in smalls for n in range(ref.shape[0] // 8)]
-    shard = width // len(pieces)
-    some = levels // len(pieces)
+
+    def lows(ds):
+        t = iota((256, 1), 0) + ds.start
+        pool = jnp.where((t >= prefix) & (t < length), 1.0, 0.0) / count
+        low[ds, :] = (out_cot[ds, :].astype(F32) + pool * pool_cot[...]).astype(BF16)
+
+    rows_loop(size, 256, lows)
+
+
+def prepare_kernel(copies, n_pieces, levels, meta, hidden, hidden_peer, buckets, *refs):
+    pieces = refs[:n_pieces]
+    normed, normed_peer, bias, gain_one, gain_two, length_peer = refs[n_pieces : n_pieces + 6]
+    rest = refs[n_pieces + 6 :]
+    if copies:
+        qkv, w_half, table, table_rows = rest
+        place(meta, pieces, (qkv, w_half), copies)
+        count = n_pieces
+        column = pieces[0].shape[1] - 128
+        blocks = [ref[0:16, column:].astype(F32) for ref in pieces]
+        places = [jnp.bitwise_xor(meta[0], 2 * (p % 4) + p // 4) for p in range(count)]
+    else:
+        table, table_rows = rest
+        count = pieces[0].shape[0] // 16
+        blocks = [pieces[0][16 * p : 16 * p + 16, :].astype(F32) for p in range(count)]
+        places = [jnp.int32(p) for p in range(count)]
+    size, width = hidden.shape
+    shard = width // count
+    some = levels // count
     table[...] = jnp.zeros_like(table)
     first = jnp.zeros((1, width), F32)
     second = jnp.zeros((1, width), F32)
     rest = jnp.zeros((1, width - 128), F32)
-    peers = jnp.zeros((1, 128), F32)
-    for p, piece in enumerate(pieces):
-        where = jnp.bitwise_xor(meta[0], 2 * (p % 4) + p // 4) if relative else jnp.int32(p)
+    peers = jnp.zeros((1, 1), F32)
+    for where, piece in zip(places, blocks):
         first += pltpu.roll(jnp.concatenate([piece[0:1], rest], axis=1), shard * where, 1)
         second += pltpu.roll(jnp.concatenate([piece[1:2], rest], axis=1), shard * where, 1)
-        peers += jnp.where(where == jnp.bitwise_xor(meta[0], 1), piece[2:3], 0.0)
+        length = 256.0 * piece[2:3, 0:1] + piece[2:3, 1:2]
+        peers += jnp.where(where == jnp.bitwise_xor(meta[0], 1), length, 0.0)
         for b in range(some):
             table[pl.ds(some * where + b, 1), :] = piece[4 + b : 5 + b]
-    length_peer[...] = peers
+    length_peer[...] = jnp.broadcast_to(peers, (1, 128))
     gain_one[...] = first
     gain_two[...] = second
 
@@ -166,12 +198,6 @@
 
         rows_loop(size, 256, rows)
 
-    def lows(ds):
-        t = iota((256, 1), 0) + ds.start
-        pool = jnp.where((t >= prefix) & (t < length), 1.0, 0.0) / count
-        low[ds, :] = (out_cot[ds, :].astype(F32) + pool * pool_cot[...]).astype(BF16)
-
-    rows_loop(size, 256, lows)
     span = 2 * size
     hot = (buckets[...] == iota((levels, span), 0)).astype(BF16)
     table_rows[...] = dot_left(table[...].astype(BF16), hot)
@@ -195,13 +221,6 @@
         return carry
 
     lax.fori_loop(0, heads, head, 0)
-
-
-def collect_kernel(copies, n_pieces, *refs):
-    meta = refs[0]
-    pieces = refs[1 : 1 + n_pieces]
-    qkv, w_half = refs[1 + n_pieces :]
-    place(meta, pieces, (qkv, w_half), copies)
 
 
 def attend_kernel(meta, x_ref, bias, w, length, qkv, out, upper, lower, powers, inv_sums, scores):
@@ -332,13 +351,13 @@
 def contract_kernel(copies, n_pieces, *refs):
     meta, slope_own, slope_peer, low_own, low_peer, w_in = refs[:6]
     pieces = refs[6 : 6 + n_pieces]
-    pre_own, pre_peer, part_own, send_left, send_right, w_ffout = refs[6 + n_pieces :]
-    half = send_left.shape[1]
+    pre_own, pre_peer, part_own, *sends, w_ffout = refs[6 + n_pieces :]
+    third = sends[0].shape[1]
     place(meta, pieces, (w_ffout,), copies)
     size = low_own.shape[0]
     chunk = 512 if w_in.shape[1] % 512 == 0 else 256
     for slope, low, grad_pre, part in (
-        (slope_peer, low_peer, pre_peer, (send_left, send_right)),
+        (slope_peer, low_peer, pre_peer, sends),
         (slope_own, low_own, pre_own, (part_own,)),
     ):
 
@@ -351,16 +370,16 @@
                 grad_pre[ds, c : c + chunk] = g
                 t = dot_right(g, w_in[:, c : c + chunk])
                 total = t if total is None else total + t
-            if len(part) == 2:
-                part[0][ds, :] = total[:, :half].astype(BF16)
-                part[1][ds, :] = total[:, half:].astype(BF16)
+            if len(part) > 1:
+                for n, ref in enumerate(part):
+                    ref[ds, :] = total[:, n * third : (n + 1) * third].astype(BF16)
             else:
                 part[0][ds, :] = total
 
         rows_loop(size, 256, rows)
 
 
-def through_kernel(meta, residual, part, other, other_right, out_cot, pool_cot, gain, w_half, w_other,
+def through_kernel(meta, residual, part, left, center, right, out_cot, pool_cot, gain, w_half, w_other,
                    grad_residual, low_mine, upper, lower, grad_keep, grad_send, grad_gain):
     size, width = residual.shape
     half = width // 2
@@ -373,7 +392,7 @@
 
     def rows(ds, low_given, start):
         x = residual[ds, :]
-        gn = part[ds, :] + jnp.concatenate([other[ds, :], other_right[ds, :]], axis=1).astype(F32)
+        gn = part[ds, :] + jnp.concatenate([left[ds, :], center[ds, :], right[ds, :]], axis=1).astype(F32)
         inv = lax.rsqrt(jnp.mean(x * x, axis=-1, keepdims=True) + EPS)
         u = gain[...] * gn
         xr = x * inv
@@ -466,9 +485,9 @@
 
 
 def weights_kernel(plan, n_out, *refs):
-    meta, x_own, x_peer, dqkv_own, dqkv_peer, att_own, upper, lower, att_peer, got_peer, low_own, low_upper, low_lower, small = refs[:14]
-    outs = refs[14 : 14 + n_out]
-    (grads,) = refs[14 + n_out :]
+    meta, x_own, x_peer, dqkv_own, dqkv_peer, att_own, upper, lower, att_peer, got_upper, got_lower, low_own, low_upper, low_lower, small = refs[:15]
+    outs = refs[15 : 15 + n_out]
+    (grads,) = refs[15 + n_out :]
     middle = upper.shape[0]
     part = dqkv_own.shape[1]
     depth = x_own.shape[1]
@@ -486,8 +505,8 @@
         g += dot_left(att_peer[middle:, cols], low_lower[...])
         grads[pl.ds(mine + c, 128), part:] = g.astype(BF16)
         g = dot_left(upper[:, cols], low_own[:middle]) + dot_left(lower[:, cols], low_own[middle:])
-        g += dot_left(got_peer[:middle, cols], low_upper[...])
-        g += dot_left(got_peer[middle:, cols], low_lower[...])
+        g += dot_left(got_upper[:, cols], low_upper[...])
+        g += dot_left(got_lower[:, cols], low_lower[...])
         grads[pl.ds(theirs + c, 128), part:] = g.astype(BF16)
     grads[depth:, :] = jnp.zeros((16, grads.shape[1]), BF16)
     grads[depth:, 0:128] = small[...].astype(BF16)
@@ -773,28 +792,34 @@
     buckets = jnp.concatenate([bucket_index[::-1], jnp.full((1,), -1, jnp.int32)])[None, :]
 
     if fast:
-        kept_a, given_a, kept_b, given_b, small = call(
+        kept_a, given_a, kept_b, given_b = call(
             functools.partial(pack_kernel, nf // 2),
             "pack",
             meta,
             [(a, "h") for a in (w_query, w_key, w_value, w_out, w_in)]
             + vm(norm_gain_attn[None], norm_gain_ffn[None], rel_bias),
-            [((shard, 4 * half), BF16, "v")] * 2
-            + [((shard, part_ff), BF16, "v")] * 2
-            + [((8, 128), F32, "v")],
+            [((shard, 4 * half + 128), BF16, "v")] * 2 + [((shard, part_ff), BF16, "v")] * 2,
             [pltpu.VMEM(w.shape, BF16) for w in (w_query, w_key, w_value, w_out, w_in)] + [dma(5)],
             limit=56 * 2**20,
         )
         on_x, on_y = Link(2), Link(4)
-        taken_a, taken_b = peer(given_a), peer(given_b)
-        both_a, both_b = call(
+        taken_a = peer(given_a)
+        x_kept, y_taken = on_x.send(kept_a), on_y.send(taken_a)
+        x_taken, y_kept = on_x.send(taken_a), on_y.send(kept_a)
+        far_kept, far_taken = on_y.send(x_kept), on_x.send(y_taken)
+        a_pieces = [kept_a, x_kept, y_kept, far_kept, taken_a, x_taken, y_taken, far_taken]
+        a_copies = []
+        for number in range(8):
+            far, side = number % 4, 1 + number // 4
+            a_copies.append((number, 0, shard, 0, 0, 0, 0, wide, 2 * shard, far, side))
+            a_copies.append((number, 0, shard, wide, 1, 0, 0, half, 2 * shard, far, side))
+        taken_b = peer(after(given_b, hidden_peer, taken_a))
+        (both_b,) = call(
             stack_kernel,
             "stack",
             meta,
-            vm(kept_a, taken_a, kept_b, taken_b),
-            [((2 * shard, 4 * half), BF16, "v"), ((2 * shard, part_ff), BF16, "v")],
-            deps=(hidden_peer,),
-            limit=56 * 2**20,
+            vm(kept_b, taken_b),
+            [((2 * shard, part_ff), BF16, "v")],
         )
 
         def near(v):
@@ -803,25 +828,16 @@
         def distant(three, *deps):
             v, by_x, by_y = three
             h = v.shape[0] // 2
-            far_y = on_y.send(after(by_x, *deps)[:h])
-            far_x = on_x.send(after(by_y, *deps)[h:])
+            upper, lower = call(
+                cut_kernel, "cut", meta, vm(by_x, by_y), [((h, v.shape[1]), BF16, "v")] * 2, deps=deps
+            )
+            far_y, far_x = on_y.send(upper), on_x.send(lower)
             return three + [far_y, far_x]
 
         def rows_of(five):
             h = five[3].shape[0]
             return zip(five, (0, 0, 0, 0, h), (0, 1, 2, 3, 3))
 
-        a_pieces = near(both_a)
-        smalls = [small] + [swap(after(small, both_a), "fsdp", nf, far) for far in (2, 4, 6)]
-        a_pieces = distant(a_pieces, *smalls)
-        (small,) = call(rows_kernel, "rows", meta, vm(*smalls), [((32, 128), F32, "v")])
-        smalls = [small, peer(small)]
-        a_copies = []
-        for number, (piece, row, far) in enumerate(rows_of(a_pieces)):
-            rows = piece.shape[0]
-            a_copies.append((number, 0, rows, 0, 0, row, 0, wide, 2 * shard, far, 0))
-            a_copies.append((number, 0, rows, wide, 1, row, 0, half, 2 * shard, far, 0))
-        b_pieces = near(both_b)
     else:
 
         def whole(v):
@@ -836,39 +852,36 @@
         c_full = whole(w_ffout).reshape(nf // 2, 2, block, width)
         c_pieces = [by_core(c_full[:, 0], c_full[:, 1]).reshape(part_ff, width)]
         c_copies = [(0, 0, part_ff, 0, 0, 0, 0, width, 0, 0, 0)]
-        pad = jnp.zeros((1, 128 - shard), BF16)
-        rows = [norm_gain_attn[None], norm_gain_ffn[None]]
-        rows = [jnp.concatenate([r, pad], axis=1) for r in rows]
-        rel = jnp.pad(rel_bias, ((0, 4 - rel_bias.shape[0]), (0, 128 - heads)))
-        small = jnp.concatenate(rows + [jnp.zeros((2, 128), BF16), rel], axis=0).astype(F32)
-        small = small.at[2].set(row_lengths[0].astype(F32))
-        smalls = [whole(small)]
-
-    normed, normed_peer, bias, low, gain_one, gain_two, length_peer = call(
-        functools.partial(prepare_kernel, len(smalls), fast, levels),
+        length = row_lengths[0]
+        split = jnp.stack([length // 256, length % 256]).astype(BF16)[None]
+        rows = [norm_gain_attn[None], norm_gain_ffn[None], split, split, rel_bias]
+        rows = [jnp.pad(r, ((0, 0), (0, 128 - r.shape[1]))) for r in rows]
+        small = jnp.concatenate(rows, axis=0)
+        a_pieces, a_copies = [whole(jnp.pad(small, ((0, 16 - small.shape[0]), (0, 0))))], ()
+
+    (low,) = call(
+        low_kernel, "low", meta, vm(out_cotangent, pool_cotangent), [((size, width), BF16, "v")]
+    )
+    normed, normed_peer, bias, gain_one, gain_two, length_peer, *weights = call(
+        functools.partial(prepare_kernel, a_copies, len(a_pieces), levels),
         "prepare",
         meta,
-        vm(hidden_in, hidden_peer, *smalls, buckets, out_cotangent, pool_cotangent),
+        vm(hidden_in, hidden_peer, buckets, *a_pieces),
         [
             ((size, width), BF16, "v"),
             ((size, width), BF16, "v"),
             ((few, 128, 2 * size - 128), F32, "v"),
-            ((size, width), BF16, "v"),
             ((1, width), F32, "v"),
             ((1, width), F32, "v"),
             ((1, 128), F32, "v"),
-        ],
+        ]
+        + ([((width, wide), BF16, "v"), ((width, half), BF16, "v")] if fast else []),
         [pltpu.VMEM((levels, 128), F32), pltpu.VMEM((128, 2 * size), F32)],
+        deps=(low,),
     )
     if fast:
-        qkv_w, out_half = call(
-            functools.partial(collect_kernel, a_copies, len(a_pieces)),
-            "collect",
-            meta,
-            vm(*a_pieces),
-            [((width, wide), BF16, "v"), ((width, half), BF16, "v")],
-            deps=(gain_one,),
-        )
+        b_pieces = near(both_b)
+        qkv_w, out_half = weights
     out_other = peer(out_half)
 
     def attend(x, length, name, *deps):
@@ -902,7 +915,7 @@
         c_pieces = near(w_ffout)
     served = tuple(b_pieces[n] for n in (1, 2)) if fast else ()
     length_own = jnp.broadcast_to(row_lengths.astype(F32)[None], (1, 128))
-    qkv_own, attended, _, _, powers_own, sums_own = attend(
+    qkv_own, attended, *own_halves, powers_own, sums_own = attend(
         normed, length_own, "attend_own", given_att, out_other, *served
     )
     served = tuple(b_pieces[n] for n in (3, 4)) if fast else ()
@@ -938,21 +951,20 @@
         [((size, part_ff), BF16, "v")] * 2 + [((width, part_ff), BF16, "v")],
         deps=tuple(thirds),
     )
+    if fast:
+        c_pieces = distant(c_pieces, act_own)
+        c_copies = [
+            (number, 0, piece.shape[0], 0, 0, row, 0, width, block, far, 0)
+            for number, (piece, row, far) in enumerate(rows_of(c_pieces))
+        ]
     act_peer, slope_peer, normed_two_peer = call(
         functools.partial(expand_kernel, (), 3),
         "expand_peer",
         meta,
         vm(thirds[0], in_w, *thirds[1:]),
         [((size, part_ff), BF16, "v")] * 2 + [((size, width), BF16, "v")],
-    )
-    served = tuple(c_pieces[n] for n in (1, 2)) if fast else ()
-    if fast:
-        c_pieces = distant(c_pieces, act_peer)
-        c_copies = [
-            (number, 0, piece.shape[0], 0, 0, row, 0, width, block, far, 0)
-            for number, (piece, row, far) in enumerate(rows_of(c_pieces))
-        ]
-    got_att_peer = peer(after(attended, act_peer, *served))
+        deps=tuple(c_pieces[n] for n in (1, 2)) if fast else (),
+    )
     ff_parts = call(
         functools.partial(product_kernel, ff_plan, len(ff_outs)),
         "product",
@@ -960,7 +972,6 @@
         vm(act_own, act_peer, low, low_peer),
         ff_outs,
         [shape_ff],
-        deps=(got_att_peer,),
     )
     ff_parts = list(ff_parts)
     if fast:
@@ -973,7 +984,7 @@
         vm(slope_own, slope_peer, low, low_peer, in_w, *c_pieces),
         [((size, part_ff), BF16, "v")] * 2
         + [((size, width), F32, "v")]
-        + [((size, half), BF16, "v")] * 2
+        + [((size, width // 3), BF16, "v")] * 3
         + [((part_ff, width), BF16, "v")],
         deps=(ff_parts[0],),
     )
@@ -1005,14 +1016,7 @@
         (out,) = call(add_kernel, "add", meta, vm(a, b), [(a.shape, BF16, "v")], deps=deps)
         return out
 
-    if fast:
-        other_gn = [peer(v) for v in send_gn]
-        in_x = on_x.send(after(in_parts[0], ff_x))
-        in_y = on_y.send(after(in_parts[1], ff_y))
-        last_y, last_x, last = turn(ff_parts, ff_x, ff_y, last)
-        ff_last = (last_y, last_x)
-    else:
-        other_gn = [peer(v) for v in send_gn]
+    other_gn = [peer(v) for v in send_gn]
     grad_residual, low_mine, *low_given, grad_keep, grad_send, grad_gain_two = call(
         through_kernel,
         "through",
@@ -1031,6 +1035,9 @@
     )
     grad_got = peer(grad_send)
     last = grad_gain_two
+    if fast:
+        last_y, last_x, last = turn(ff_parts, ff_x, ff_y, last)
+        ff_last = (last_y, last_x)
     head_rows = 8
 
     def halve_first(parts, by_x, by_y, last_y, last_x, *deps, extra=0):
@@ -1081,20 +1088,23 @@
 
     diag = jnp.zeros((head_rows, 2 * size), F32)
     dqkv_own, diag = attend_back(
-        qkv_own, powers_own, grad_keep, attended, sums_own, diag, "attend_back_own", last
+        qkv_own, powers_own, grad_keep, attended, sums_own, diag, "attend_back_own", last, grad_got
     )
     last = dqkv_own
     if fast:
-        last_y, last_x, last = turn(in_parts, in_x, in_y, last)
-        in_last = (last_y, last_x)
+        ff_keep, ff_one = halve_first(ff_parts, ff_x, ff_y, *ff_last, last)
+        in_x = on_x.send(after(in_parts[0], dqkv_own))
+        in_y = on_y.send(after(in_parts[1], dqkv_own))
+        last = ff_keep
     dqkv_peer, diag = attend_back(
         qkv_peer, powers_peer, grad_got, given_att, sums_peer, diag, "attend_back_peer", last
     )
     last = diag
     if fast:
-        ff_keep, ff_one = halve_first(ff_parts, ff_x, ff_y, *ff_last, last)
-        in_keep, in_one = halve_first(in_parts, in_x, in_y, *in_last, ff_keep)
-        last = in_keep
+        ff_keep, ff_two = halve_next(ff_keep, ff_one, last)
+        last = ff_keep
+    got_att_peer = [peer(after(v, last)) for v in own_halves]
+    if fast:
         at_plan = message_plan(2 * shard)
         at_plan = at_plan + [(n, 2 * shard, 16, 0, 0, width) for n in (0, 2)]
         at_outs = [((2 * shard + (16 if n in (0, 2) else 0), 4 * half), BF16, "v") for n in range(4)]
@@ -1110,8 +1120,11 @@
         [pltpu.VMEM((1, width), F32)],
         deps=(last,),
     )
-    low_other = [peer(after(v, part_gh)) for v in low_given]
-    other_gh = [peer(v) for v in send_gh]
+    low_other = [peer(after(v, part_gh, *got_att_peer)) for v in low_given]
+    last = part_gh
+    if fast:
+        last_y, last_x, last = turn(in_parts, in_x, in_y, last)
+        in_last = (last_y, last_x)
     at_parts = call(
         functools.partial(weights_kernel, at_plan, len(at_outs)),
         "weights",
@@ -1124,20 +1137,33 @@
             attended,
             *got_att,
             given_att,
-            got_att_peer,
+            *got_att_peer,
             low_mine,
             *low_other,
             small_grads,
         ),
         at_outs,
         [pltpu.VMEM((width + 16, 4 * half), BF16)],
-        deps=(part_gh,),
+        deps=(last,),
     )
     at_parts = list(at_parts)
     last = at_parts[0]
     if fast:
         at_x = on_x.send(at_parts[0])
         at_y = on_y.send(at_parts[1])
+        in_keep, in_one = halve_first(in_parts, in_x, in_y, *in_last, last)
+        ff_four = quarter(ff_keep, ff_two, in_keep)
+        last = ff_four[0]
+    other_gh = [peer(after(v, last)) for v in send_gh]
+    part_branch, *send_branch = call(
+        output_kernel,
+        "output",
+        meta,
+        vm(act_own, act_peer, ff_w),
+        [((size, width), F32, "v")] + [((size, half), BF16, "v")] * 2,
+        deps=(last,),
+    )
+    last = part_branch
     (grad_hidden,) = call(
         hidden_kernel,
         "hidden",
@@ -1147,28 +1173,23 @@
         deps=(last,),
     )
     last = grad_hidden
+
     if fast:
-        ff_keep, ff_two = halve_next(ff_keep, ff_one, last)
-        in_keep, in_two = halve_next(in_keep, in_one, ff_keep)
-        last = in_keep
-    part_branch, *send_branch = call(
-        output_kernel,
-        "output",
-        meta,
-        vm(act_own, act_peer, ff_w),
-        [((size, width), F32, "v")] + [((size, half), BF16, "v")] * 2,
-        deps=(last,),
-    )
-    last = part_branch
-
-    if fast:
-        last_y, last_x, last = turn(at_parts, at_x, at_y, last)
+        in_keep, in_two = halve_next(in_keep, in_one, last)
+        last_y, last_x, last = turn(at_parts, at_x, at_y, in_keep)
         at_last = (last_y, last_x)
-        ff_four = quarter(ff_keep, ff_two, last)
-        in_four = quarter(in_keep, in_two, ff_four[0])
-        at_keep, at_one = halve_first(at_parts, at_x, at_y, *at_last, in_four[0], extra=128)
-        ff_four = quarters(*ff_four, at_keep)
-        last = at_keep
+        ff_four = quarters(*ff_four, last)
+        (grad_ffout,) = call(
+            join_rows_kernel,
+            "join_rows",
+            meta,
+            vm(*ff_four),
+            [((block, width), F32, "v")],
+            deps=(last,),
+        )
+        at_keep, at_one = halve_first(at_parts, at_x, at_y, *at_last, grad_ffout, extra=128)
+        in_four = quarter(in_keep, in_two, at_keep)
+        last = in_four[0]
         other_branch = [peer(after(v, last)) for v in send_branch]
     else:
         other_branch = [peer(v) for v in send_branch]
@@ -1184,35 +1205,28 @@
     if fast:
         at_keep, at_two = halve_next(at_keep, at_one, last, extra=128)
         in_four = quarters(*in_four, at_keep)
-        (grad_ffout,) = call(
-            join_rows_kernel,
-            "join_rows",
-            meta,
-            vm(*ff_four),
-            [((block, width), F32, "v")],
-            deps=(at_keep,),
-        )
+        mine_in, other_in = shards(in_four, at_keep)
+        got_in = peer(other_in)
         own_at, small_grads = call(
             last_kernel,
             "last",
             meta,
             vm(at_keep, at_two),
             [((shard // 2, 4 * half), BF16, "v"), ((16, 128), F32, "v")],
-            deps=(grad_ffout,),
+            deps=(mine_in,),
         )
         at_four = own_at, swap(own_at, "dp", nz, 1), swap(own_at, "dp", nz, 2)
         small_grads = small_grads + peer(small_grads)
-        mine_in, other_in = shards(in_four, own_at)
-        got_in = peer(other_in)
-        at_four = quarters(*at_four, mine_in)
         (grad_in,) = call(
             functools.partial(weave_in_kernel, block),
             "weave_in",
             meta,
             vm(mine_in, got_in),
             [((shard, full_ff), F32, "v")],
+            deps=(own_at,),
         )
-        mine_at, other_at = shards(at_four, grad_in)
+        at_four = quarters(*at_four, grad_in)
+        mine_at, other_at = shards(at_four, small_grads)
         got_at = peer(other_at)
         grad_at = call(
             weave_at_kernel, "weave_at", meta, vm(mine_at, got_at), [((shard, width), F32, "v")] * 4

time: 247 us -> 226 us (0.915)
  waiting for transfers between devices: 80.2 us -> 58.3 us
  starting transfers between devices: 48.4 us -> 53.8 us
  local copies, waits for them, and re-layouts: 12.5 us -> 8.75 us
    ppermute x66, waiting for transfers between devices: 80.2 us -> 58.3 us  [swap(): return lax.ppermute(v, axis, [(i, i ^ far) for i in range(count)])]
    ppermute x66, starting transfers between devices: 48.4 us -> 53.8 us  [swap(): return lax.ppermute(v, axis, [(i, i ^ far) for i in range(count)])]
    slice x6 -> x0, local copies, waits for them, and re-layouts: 3.47 us -> none  [the longest x3 1.74 us: distant(): far_y = on_y.send(after(by_x, *deps)[:h])]
    pallas_call x38 -> x39, Pallas kernels: 103 us -> 102 us  [call(): pl.pallas_call(kernel, name=name, out_shape=[jax.ShapeDtypeStruct(s, d) f...]
    unnamed x37 -> x45, local copies, waits for them, and re-layouts: 7.16 us -> 6.85 us
  transfers between devices with their start and end apart: 66 -> 66, of which waited for: 32 -> 22; matrix products, arithmetic and copies ran while one was open for 3% -> 1% of each run, Pallas kernels for 37% -> 43%
where the time goes in v3:
time: 226 us; the launch traced here: 225 us
  Pallas kernels  102 us (45%)
  waiting for transfers between devices  58.3 us (26%)
  starting transfers between devices  53.8 us (24%)
  local copies, waits for them, and re-layouts  8.75 us (4%)
  between operations  2.58 us (1%)
    pallas_call x39, Pallas kernels, call(): pl.pallas_call(kernel, name=name, out_shape=[jax.ShapeDtypeStruct(s, d) f...  102 us
    ppermute x66, waiting for transfers between devices, swap(): return lax.ppermute(v, axis, [(i, i ^ far) for i in range(count)])  58.3 us
    ppermute x66, starting transfers between devices, swap(): return lax.ppermute(v, axis, [(i, i ^ far) for i in range(count)])  53.8 us
    unnamed x45, local copies, waits for them, and re-layouts  6.85 us
  transfers between devices with their start and end apart: 66, of which 22 were waited for; matrix products, arithmetic and copies ran while one was open for 1% of the time, Pallas kernels for 43%

profile of v3, /device:TPU:0, one launch (start us, length us, event | category | flops | bytes accessed | tf_op | source)
XLA Modules:
  0.0 225.2 jit_solution(5833891559860335468)
XLA Ops:
  3.1 3.3 %pack.1 = (bf16[96,1664]{1,0:T(8,128)(2,1)}, bf16[96,1664]{1,0:T(8,128)(2,1)}, bf16[96,1536]{1,0:T(8,128)(2,1)}, bf16[96,1536]{1,0:T(8,128)(2,1)}) custom-call(s32[8]{0:T(128)} %stack.20.meta.refs_0_, bf16[96,768]{1,0:T(8,128)(2,1)} %refs_0_.1, bf16[96,768]{1,0:T(8,128)(2,1)} %refs_1_.1, bf16[96,768]{1,0:T(8,128)(2,1)} %refs_2_.1, bf16[96,768]{1,0:T(8,128)(2,1)} %refs_3_.1, ...), custom_call_target="tpu_custom_call" | custom-call | flops 1000 | bytes 1000 | tf_op jit(solution)/shard_map/pack/pallas_call | solution.py:43
  13.0 5.1 %collective-permute-done.1.refs_1_ = bf16[96,1664]{1,0:T(8,128)(2,1)} collective-permute-done((bf16[96,1664]{1,0:T(8,128)(2,1)}, bf16[96,1664]{1,0:T(8,128)(2,1)}, u32[]{:S(2)}, u32[]{:S(2)}) %collective-permute-start.1) | collective-permute-done | bytes 319520 | tf_op jit(solution)/shard_map/ppermute | solution.py:717
  36.6 5.6 %prepare.1 = (bf16[512,768]{1,0:T(8,128)(2,1)S(1)}, bf16[512,768]{1,0:T(8,128)(2,1)S(1)}, f32[6,128,896]{2,1,0:T(8,128)S(1)}, f32[1,768]{1,0:T(1,128)S(1)}, f32[...) custom-call(s32[8]{0:T(128)S(1)} %copy-done.7, ...), custom_call_target="tpu_custom_call" | custom-call | flops 1000 | bytes 1000 | tf_op jit(solution)/shard_map/prepare/pallas_call | solution.py:43
  42.3 6.8 %attend_peer.1 = (bf16[512,1152]{1,0:T(8,128)(2,1)S(1)}, bf16[512,384]{1,0:T(8,128)(2,1)S(1)}, bf16[256,384]{1,0:T(8,128)(2,1)S(1)}, bf16[256,384]{1,0:T(8,128)(...) custom-call(s32[8]{0:T(128)S(1)} %copy-done.7, ...), custom_call_target="tpu_custom_call" | custom-call | flops 1000 | bytes 1000 | tf_op jit(solution)/shard_map/attend_peer/pallas_call | solution.py:43
  55.1 6.8 %attend_own.1 = (bf16[512,1152]{1,0:T(8,128)(2,1)S(1)}, bf16[512,384]{1,0:T(8,128)(2,1)S(1)}, bf16[256,384]{1,0:T(8,128)(2,1)S(1)}, bf16[256,384]{1,0:T(8,128)(2...) custom-call(s32[8]{0:T(128)S(1)} %copy-done.7, bf16[512,768]{1,0:T(8,128)(2,1)S(1)} %get-tuple-element.213.x_ref.refs_1_, ...), custom_call_target="tpu_custom_call" | custom-call | flops 1000 | bytes 1000 | tf_op jit(solution)/shard_map/attend_own/pallas_call | solution.py:43
  68.3 4.3 %expand_own.1 = (bf16[512,1536]{1,0:T(8,128)(2,1)S(1)}, bf16[512,1536]{1,0:T(8,128)(2,1)S(1)}, bf16[768,1536]{1,0:T(8,128)(2,1)S(1)}) custom-call(s32[8]{0:T(128)S(1)} %copy-done.7, bf16[512,768]{1,0:T(8,128)(2,1)S(1)} %get-tuple-element.225.refs_1_, bf16[192,1536]{1,0:T(8,128)(2,1)} %stack.21.refs_2_, ...), custom_call_target="tpu_custom_call" | custom-call | flops 1000 | bytes 111001000 | tf_op jit(solution)/shard_map/expand_own/pallas_call | solution.py:43
  76.8 3.5 %expand_peer.1 = (bf16[512,1536]{1,0:T(8,128)(2,1)S(1)}, bf16[512,1536]{1,0:T(8,128)(2,1)S(1)}, bf16[512,768]{1,0:T(8,128)(2,1)S(1)}) custom-call(s32[8]{0:T(128)S(1)} %copy-done.7, bf16[512,256]{1,0:T(8,128)(2,1)S(1)} %collective-permute-done.19.refs_1_, bf16[768,1536]{1,0:T(8,128)(2,1)S(1)} %get-tuple-element.233.refs_2_.refs_5_, ...), custom_call_target="tpu_custom_call" | custom-call | flops 1000 | bytes 1000 | tf_op jit(solution)/shard_map/expand_peer/pallas_call | solution.py:43
  80.2 3.4 %product.1 = (bf16[384,768]{1,0:T(8,128)(2,1)S(1)}, bf16[384,768]{1,0:T(8,128)(2,1)S(1)}, bf16[384,768]{1,0:T(8,128)(2,1)S(1)}, bf16[384,768]{1,0:T(8,128)(2,1)S(1)}) custom-call(s32[8]{0:T(128)S(1)} %copy-done.7, bf16[512,1536]{1,0:T(8,128)(2,1)S(1)} %get-tuple-element.235.refs_1_.act_own, bf16[512,1536]{1,0:T(8,128)(2,1)S(1)} %get-tuple-element.236.refs_2_.act_peer, ...), custom_call_target="tpu_custom_call" | custom-call | flops 1000 | bytes 1000 | tf_op jit(solution)/shard_map/product/pallas_call | solution.py:43
  86.1 7.2 %contract.1 = (bf16[512,1536]{1,0:T(8,128)(2,1)S(1)}, bf16[512,1536]{1,0:T(8,128)(2,1)S(1)}, f32[512,768]{1,0:T(8,128)S(1)}, bf16[512,256]{1,0:T(8,128)(2,1)}, b...) custom-call(s32[8]{0:T(128)S(1)} %copy-done.7, ...), custom_call_target="tpu_custom_call" | custom-call | flops 1000 | bytes 1000 | tf_op jit(solution)/shard_map/contract/pallas_call | solution.py:43
  94.0 3.3 %outer.1 = (bf16[192,1536]{1,0:T(8,128)(2,1)S(1)}, bf16[192,1536]{1,0:T(8,128)(2,1)S(1)}, bf16[192,1536]{1,0:T(8,128)(2,1)S(1)}, bf16[192,1536]{1,0:T(8,128)(2,1)S(1)}) custom-call(s32[8]{0:T(128)S(1)} %copy-done.7, bf16[512,768]{1,0:T(8,128)(2,1)S(1)} %get-tuple-element.225.refs_1_, bf16[512,768]{1,0:T(8,128)(2,1)S(1)} %get-tuple-element.234.refs_2_, ...), custom_call_target="tpu_custom_call" | custom-call | flops 1000 | bytes 1000 | tf_op jit(solution)/shard_map/outer/pallas_call | solution.py:43
  97.3 3.6 %through.1 = (f32[512,768]{1,0:T(8,128)S(1)}, bf16[512,384]{1,0:T(8,128)(2,1)S(1)}, bf16[256,384]{1,0:T(8,128)(2,1)S(1)}, bf16[256,384]{1,0:T(8,128)(2,1)S(1)}, ...) custom-call(s32[8]{0:T(128)S(1)} %copy-done.7, ...), custom_call_target="tpu_custom_call" | custom-call | flops 1000 | bytes 1000 | tf_op jit(solution)/shard_map/through/pallas_call | solution.py:43
  103.9 8.7 %attend_back_own.1 = (bf16[512,1152]{1,0:T(8,128)(2,1)S(1)}, f32[8,1024]{1,0:T(8,128)S(1)}) custom-call(s32[8]{0:T(128)S(1)} %copy-done.7, bf16[512,1152]{1,0:T(8,128)(2,1)S(1)} %copy-done.5, bf16[6,512,512]{2,1,0:T(8,128)(2,1)S(1)} %get-tuple-element.268.powers, bf16[512,384]{1,0:T(8,128)(2,1)S(1)} %get-tuple-element.269.g_ref, ...), custom_call_target="tpu_custom_call" | custom-call | flops 1000 | bytes 1000 | tf_op jit(solution)/shard_map/attend_back_own/pallas_call | solution.py:43
  117.6 9.0 %attend_back_peer.1 = (bf16[512,1152]{1,0:T(8,128)(2,1)S(1)}, f32[8,1024]{1,0:T(8,128)S(1)}) custom-call(s32[8]{0:T(128)S(1)} %copy-done.7, bf16[512,1152]{1,0:T(8,128)(2,1)S(1)} %copy-done.3, bf16[6,512,512]{2,1,0:T(8,128)(2,1)S(1)} %get-tuple-element.279.powers, bf16[512,384]{1,0:T(8,128)(2,1)S(1)} %collective-permute-done.29.g_ref, ...), custom_call_target="tpu_custom_call" | custom-call | flops 1000 | bytes 1000 | tf_op jit(solution)/shard_map/attend_back_peer/pallas_call | solution.py:43
  127.8 4.1 %inputs.1 = (f32[512,768]{1,0:T(8,128)S(1)}, bf16[512,384]{1,0:T(8,128)(2,1)S(1)}, bf16[512,384]{1,0:T(8,128)(2,1)S(1)}, f32[16,128]{1,0:T(8,128)S(1)}) custom-call(s32[8]{0:T(128)S(1)} %copy-done.7, bf16[512,1152]{1,0:T(8,128)(2,1)S(1)} %get-tuple-element.271.dqkv_own.refs_3_, bf16[512,1152]{1,0:T(8,128)(2,1)S(1)} %get-tuple-element.287.dqkv_peer.refs_4_, ...), custom_call_target="tpu_custom_call" | custom-call | flops 1000 | bytes 1000 | tf_op jit(solution)/shard_map/inputs/pallas_call | solution.py:43
  134.9 3.8 %weights.1 = (bf16[208,1536]{1,0:T(8,128)(2,1)S(1)}, bf16[192,1536]{1,0:T(8,128)(2,1)S(1)}, bf16[208,1536]{1,0:T(8,128)(2,1)S(1)}, bf16[192,1536]{1,0:T(8,128)(2,1)S(1)}) custom-call(s32[8]{0:T(128)S(1)} %copy-done.7, bf16[512,768]{1,0:T(8,128)(2,1)S(1)} %get-tuple-element.213.x_ref.refs_1_, bf16[512,768]{1,0:T(8,128)(2,1)S(1)} %get-tuple-element.199.x_ref.refs_2_, ...), custom_call_target="tpu_custom_call" | custom-call | flops 1000 | bytes 1000 | tf_op jit(solution)/shard_map/weights/pallas_call | solution.py:43
  144.6 5.3 %collective-permute-done.41.b = bf16[96,768]{1,0:T(8,128)(2,1)S(1)} collective-permute-done((bf16[96,768]{1,0:T(8,128)(2,1)S(1)}, bf16[96,768]{1,0:T(8,128)(2,1)S(1)}, u32[]{:S(2)}, u32[]{:S(2)}) %collective-permute-start.41) | collective-permute-done | bytes 147488 | tf_op jit(solution)/shard_map/ppermute | solution.py:717
  151.0 3.6 %output.1 = (f32[512,768]{1,0:T(8,128)S(1)}, bf16[512,384]{1,0:T(8,128)(2,1)S(1)}, bf16[512,384]{1,0:T(8,128)(2,1)S(1)}) custom-call(s32[8]{0:T(128)S(1)} %copy-done.7, bf16[512,1536]{1,0:T(8,128)(2,1)S(1)} %get-tuple-element.235.refs_1_.act_own, bf16[512,1536]{1,0:T(8,128)(2,1)S(1)} %get-tuple-element.236.refs_2_.act_peer, ...), custom_call_target="tpu_custom_call" | custom-call | flops 1000 | bytes 1000 | tf_op jit(solution)/shard_map/output/pallas_call | solution.py:43
  166.1 4.7 %collective-permute-done.48.by_high = bf16[96,768]{1,0:T(8,128)(2,1)S(1)} collective-permute-done((bf16[96,768]{1,0:T(8,128)(2,1)S(1)}, bf16[96,768]{1,0:T(8,128)(2,1)S(1)}, u32[]{:S(2)}, u32[]{:S(2)}) %collective-permute-start.48) | collective-permute-done | bytes 147488 | tf_op jit(solution)/shard_map/ppermute | solution.py:717
  170.8 3.2 %collective-permute-start.52 = (bf16[48,1536]{1,0:T(8,128)(2,1)S(1)}, bf16[48,1536]{1,0:T(8,128)(2,1)S(1)}, u32[]{:S(2)}, u32[]{:S(2)}) collective-permute-start(bf16[48,1536]{1,0:T(8,128)(2,1)S(1)} %get-tuple-element.345), channel_id=1, source_target_pairs={{0,2},{1,3},{2,0},{3,1},{4,6},{5,7},{6,4},{7,5},{8,10},{9,11},{10,... | collective-permute-start | bytes 442376 | tf_op jit(solution)/shard_map/ppermute | solution.py:717
  174.0 5.3 %collective-permute-done.49.by_both = bf16[96,768]{1,0:T(8,128)(2,1)S(1)} collective-permute-done((bf16[96,768]{1,0:T(8,128)(2,1)S(1)}, bf16[96,768]{1,0:T(8,128)(2,1)S(1)}, u32[]{:S(2)}, u32[]{:S(2)}) %collective-permute-start.49) | collective-permute-done | bytes 147488 | tf_op jit(solution)/shard_map/ppermute | solution.py:717
  187.0 9.5 %collective-permute-done.55.b = bf16[96,1664]{1,0:T(8,128)(2,1)S(1)} collective-permute-done((bf16[96,1664]{1,0:T(8,128)(2,1)S(1)}, bf16[96,1664]{1,0:T(8,128)(2,1)S(1)}, u32[]{:S(2)}, u32[]{:S(2)}) %collective-permute-start.55) | collective-permute-done | bytes 319520 | tf_op jit(solution)/shard_map/ppermute | solution.py:717
  200.6 4.0 %collective-permute-done.58.by_both = bf16[48,1536]{1,0:T(8,128)(2,1)S(1)} collective-permute-done((bf16[48,1536]{1,0:T(8,128)(2,1)S(1)}, bf16[48,1536]{1,0:T(8,128)(2,1)S(1)}, u32[]{:S(2)}, u32[]{:S(2)}) %collective-permute-start.58) | collective-permute-done | bytes 147488 | tf_op jit(solution)/shard_map/ppermute | solution.py:717
  210.8 4.7 %collective-permute-done.62.by_high = bf16[48,1536]{1,0:T(8,128)(2,1)S(1)} collective-permute-done((bf16[48,1536]{1,0:T(8,128)(2,1)S(1)}, bf16[48,1536]{1,0:T(8,128)(2,1)S(1)}, u32[]{:S(2)}, u32[]{:S(2)}) %collective-permute-start.62) | collective-permute-done | bytes 147488 | tf_op jit(solution)/shard_map/ppermute | solution.py:717
  217.6 3.7 %collective-permute-done.64.by_both = bf16[48,1536]{1,0:T(8,128)(2,1)S(1)} collective-permute-done((bf16[48,1536]{1,0:T(8,128)(2,1)S(1)}, bf16[48,1536]{1,0:T(8,128)(2,1)S(1)}, u32[]{:S(2)}, u32[]{:S(2)}) %collective-permute-start.64) | collective-permute-done | bytes 147488 | tf_op jit(solution)/shard_map/ppermute | solution.py:717
  (205 shorter events, 100.0 us)
Async XLA Ops:
  0.7 12.3 %collective-permute-start = (bf16[512,768]{1,0:T(8,128)(2,1)}, bf16[512,768]{1,0:T(8,128)(2,1)S(1)}, u32[]{:S(2)}, u32[]{:S(2)}) collective-permute-start(bf16[512,768]{1,0:T(8,128)(2,1)} %hidden.9), channel_id=1, source_target_pairs={{0,4},{4,0},{8,12},{12,8},{16,20},{20,16},{24,28},{28,24},{1,5},{5... | collective-permute-start | bytes 2359304 | tf_op jit(solution)/shard_map/ppermute | solution.py:717
  6.6 11.5 %collective-permute-start.1 = (bf16[96,1664]{1,0:T(8,128)(2,1)}, bf16[96,1664]{1,0:T(8,128)(2,1)}, u32[]{:S(2)}, u32[]{:S(2)}) collective-permute-start(bf16[96,1664]{1,0:T(8,128)(2,1)} %get-tuple-element.195.refs_0_), channel_id=1, source_target_pairs={{0,8},{4,12},{8,0},{12,4},{16,24},{20,28},{24,16},{28,20},{1,9},{5... | collective-permute-start | bytes 958472 | tf_op jit(solution)/shard_map/ppermute | solution.py:717
  11.0 14.9 %collective-permute-start.6 = (bf16[96,1664]{1,0:T(8,128)(2,1)S(1)}, bf16[96,1664]{1,0:T(8,128)(2,1)S(1)}, u32[]{:S(2)}, u32[]{:S(2)}) collective-permute-start(bf16[96,1664]{1,0:T(8,128)(2,1)S(1)} %collective-permute-done.3.refs_4_), channel_id=1, source_target_pairs={{0,8},{4,12},{8,0},{12,4},{16,24},{20,28},{24,16},{28,20},{1,9},{5... | collective-permute-start | bytes 958472 | tf_op jit(solution)/shard_map/ppermute | solution.py:717
  12.5 15.2 %collective-permute-start.2 = (bf16[96,1664]{1,0:T(8,128)(2,1)}, bf16[96,1664]{1,0:T(8,128)(2,1)S(1)}, u32[]{:S(2)}, u32[]{:S(2)}) collective-permute-start(bf16[96,1664]{1,0:T(8,128)(2,1)} %get-tuple-element.195.refs_0_), channel_id=1, source_target_pairs={{0,16},{4,20},{8,24},{12,28},{16,0},{20,4},{24,8},{28,12},{1,17},{... | collective-permute-start | bytes 958472 | tf_op jit(solution)/shard_map/ppermute | solution.py:717
  20.0 13.7 %collective-permute-start.5 = (bf16[96,1664]{1,0:T(8,128)(2,1)}, bf16[96,1664]{1,0:T(8,128)(2,1)}, u32[]{:S(2)}, u32[]{:S(2)}) collective-permute-start(bf16[96,1664]{1,0:T(8,128)(2,1)} %collective-permute-done.1.refs_1_), channel_id=1, source_target_pairs={{0,16},{4,20},{8,24},{12,28},{16,0},{20,4},{24,8},{28,12},{1,17},{... | collective-permute-start | bytes 958472 | tf_op jit(solution)/shard_map/ppermute | solution.py:717
  21.5 12.2 %collective-permute-start.7 = (bf16[96,1664]{1,0:T(8,128)(2,1)}, bf16[96,1664]{1,0:T(8,128)(2,1)}, u32[]{:S(2)}, u32[]{:S(2)}) collective-permute-start(bf16[96,1664]{1,0:T(8,128)(2,1)} %collective-permute-done.4.refs_6_), channel_id=1, source_target_pairs={{0,8},{4,12},{8,0},{12,4},{16,24},{20,28},{24,16},{28,20},{1,9},{5... | collective-permute-start | bytes 958472 | tf_op jit(solution)/shard_map/ppermute | solution.py:717
  26.7 23.0 %collective-permute-start.11 = (bf16[192,1536]{1,0:T(8,128)(2,1)}, bf16[192,1536]{1,0:T(8,128)(2,1)}, u32[]{:S(2)}, u32[]{:S(2)}) collective-permute-start(bf16[192,1536]{1,0:T(8,128)(2,1)} %stack.21.refs_2_), channel_id=1, source_target_pairs={{0,8},{4,12},{8,0},{12,4},{16,24},{20,28},{24,16},{28,20},{1,9},{5... | collective-permute-start | bytes 1769480 | tf_op jit(solution)/shard_map/ppermute | solution.py:717
  28.4 21.3 %collective-permute-start.12 = (bf16[192,1536]{1,0:T(8,128)(2,1)}, bf16[192,1536]{1,0:T(8,128)(2,1)}, u32[]{:S(2)}, u32[]{:S(2)}) collective-permute-start(bf16[192,1536]{1,0:T(8,128)(2,1)} %stack.21.refs_2_), channel_id=1, source_target_pairs={{0,16},{4,20},{8,24},{12,28},{16,0},{20,4},{24,8},{28,12},{1,17},{... | collective-permute-start | bytes 1769480 | tf_op jit(solution)/shard_map/ppermute | solution.py:717
  42.2 12.3 %collective-permute-start.9 = (bf16[768,384]{1,0:T(8,128)(2,1)S(1)}, bf16[768,384]{1,0:T(8,128)(2,1)S(1)}, u32[]{:S(2)}, u32[]{:S(2)}) collective-permute-start(bf16[768,384]{1,0:T(8,128)(2,1)S(1)} %get-tuple-element.206.w_half), channel_id=1, source_target_pairs={{0,4},{4,0},{8,12},{12,8},{16,20},{20,16},{24,28},{28,24},{1,5},{5... | collective-permute-start | bytes 1769480 | tf_op jit(solution)/shard_map/ppermute | solution.py:717
  49.1 13.8 %collective-permute-start.8 = (bf16[512,768]{1,0:T(8,128)(2,1)S(1)}, bf16[512,768]{1,0:T(8,128)(2,1)S(1)}, u32[]{:S(2)}, u32[]{:S(2)}) collective-permute-start(bf16[512,768]{1,0:T(8,128)(2,1)S(1)} %low.1.refs_3_), channel_id=1, source_target_pairs={{0,4},{4,0},{8,12},{12,8},{16,20},{20,16},{24,28},{28,24},{1,5},{5... | collective-permute-start | bytes 2359304 | tf_op jit(solution)/shard_map/ppermute | solution.py:717
  54.0 20.1 %collective-permute-start.17 = (bf16[384,768]{1,0:T(8,128)(2,1)S(1)}, bf16[384,768]{1,0:T(8,128)(2,1)S(1)}, u32[]{:S(2)}, u32[]{:S(2)}) collective-permute-start(bf16[384,768]{1,0:T(8,128)(2,1)S(1)} %copy-done.8), channel_id=1, source_target_pairs={{0,8},{4,12},{8,0},{12,4},{16,24},{20,28},{24,16},{28,20},{1,9},{5... | collective-permute-start | bytes 1769480 | tf_op jit(solution)/shard_map/ppermute | solution.py:717
  54.5 19.6 %collective-permute-start.18 = (bf16[384,768]{1,0:T(8,128)(2,1)S(1)}, bf16[384,768]{1,0:T(8,128)(2,1)S(1)}, u32[]{:S(2)}, u32[]{:S(2)}) collective-permute-start(bf16[384,768]{1,0:T(8,128)(2,1)S(1)} %copy-done.8), channel_id=1, source_target_pairs={{0,16},{4,20},{8,24},{12,28},{16,0},{20,4},{24,8},{28,12},{1,17},{... | collective-permute-start | bytes 1769480 | tf_op jit(solution)/shard_map/ppermute | solution.py:717
  83.7 17.8 %collective-permute-start.27 = (bf16[384,768]{1,0:T(8,128)(2,1)S(1)}, bf16[384,768]{1,0:T(8,128)(2,1)S(1)}, u32[]{:S(2)}, u32[]{:S(2)}) collective-permute-start(bf16[384,768]{1,0:T(8,128)(2,1)S(1)} %get-tuple-element.259), channel_id=1, source_target_pairs={{0,8},{4,12},{8,0},{12,4},{16,24},{20,28},{24,16},{28,20},{1,9},{5... | collective-permute-start | bytes 1769480 | tf_op jit(solution)/shard_map/ppermute | solution.py:717
  84.8 16.7 %collective-permute-start.28 = (bf16[384,768]{1,0:T(8,128)(2,1)S(1)}, bf16[384,768]{1,0:T(8,128)(2,1)S(1)}, u32[]{:S(2)}, u32[]{:S(2)}) collective-permute-start(bf16[384,768]{1,0:T(8,128)(2,1)S(1)} %get-tuple-element.263), channel_id=1, source_target_pairs={{0,16},{4,20},{8,24},{12,28},{16,0},{20,4},{24,8},{28,12},{1,17},{... | collective-permute-start | bytes 1769480 | tf_op jit(solution)/shard_map/ppermute | solution.py:717
  113.5 13.1 %collective-permute-start.32 = (bf16[192,768]{1,0:T(8,128)(2,1)S(1)}, bf16[192,768]{1,0:T(8,128)(2,1)S(1)}, u32[]{:S(2)}, u32[]{:S(2)}) collective-permute-start(bf16[192,768]{1,0:T(8,128)(2,1)S(1)} %get-tuple-element.284), channel_id=1, source_target_pairs={{0,1},{1,0},{2,3},{3,2},{4,5},{5,4},{6,7},{7,6},{8,9},{9,8},{10,11... | collective-permute-start | bytes 884744 | tf_op jit(solution)/shard_map/ppermute | solution.py:717
  115.1 17.4 %collective-permute-start.33 = (bf16[192,1536]{1,0:T(8,128)(2,1)S(1)}, bf16[192,1536]{1,0:T(8,128)(2,1)S(1)}, u32[]{:S(2)}, u32[]{:S(2)}) collective-permute-start(bf16[192,1536]{1,0:T(8,128)(2,1)S(1)} %get-tuple-element.292), channel_id=1, source_target_pairs={{0,8},{4,12},{8,0},{12,4},{16,24},{20,28},{24,16},{28,20},{1,9},{5... | collective-permute-start | bytes 1769480 | tf_op jit(solution)/shard_map/ppermute | solution.py:717
  116.2 16.4 %collective-permute-start.34 = (bf16[192,1536]{1,0:T(8,128)(2,1)S(1)}, bf16[192,1536]{1,0:T(8,128)(2,1)S(1)}, u32[]{:S(2)}, u32[]{:S(2)}) collective-permute-start(bf16[192,1536]{1,0:T(8,128)(2,1)S(1)} %get-tuple-element.296), channel_id=1, source_target_pairs={{0,16},{4,20},{8,24},{12,28},{16,0},{20,4},{24,8},{28,12},{1,17},{... | collective-permute-start | bytes 1769480 | tf_op jit(solution)/shard_map/ppermute | solution.py:717
  138.6 22.0 %collective-permute-start.45 = (bf16[208,1536]{1,0:T(8,128)(2,1)S(1)}, bf16[208,1536]{1,0:T(8,128)(2,1)S(1)}, u32[]{:S(2)}, u32[]{:S(2)}) collective-permute-start(bf16[208,1536]{1,0:T(8,128)(2,1)S(1)} %get-tuple-element.332), channel_id=1, source_target_pairs={{0,8},{4,12},{8,0},{12,4},{16,24},{20,28},{24,16},{28,20},{1,9},{5... | collective-permute-start | bytes 1916936 | tf_op jit(solution)/shard_map/ppermute | solution.py:717
  139.8 20.9 %collective-permute-start.46 = (bf16[192,1536]{1,0:T(8,128)(2,1)S(1)}, bf16[192,1536]{1,0:T(8,128)(2,1)S(1)}, u32[]{:S(2)}, u32[]{:S(2)}) collective-permute-start(bf16[192,1536]{1,0:T(8,128)(2,1)S(1)} %get-tuple-element.335), channel_id=1, source_target_pairs={{0,16},{4,20},{8,24},{12,28},{16,0},{20,4},{24,8},{28,12},{1,17},{... | collective-permute-start | bytes 1769480 | tf_op jit(solution)/shard_map/ppermute | solution.py:717
  161.4 19.7 %collective-permute-start.50 = (bf16[112,1536]{1,0:T(8,128)(2,1)S(1)}, bf16[112,1536]{1,0:T(8,128)(2,1)S(1)}, u32[]{:S(2)}, u32[]{:S(2)}) collective-permute-start(bf16[112,1536]{1,0:T(8,128)(2,1)S(1)} %get-tuple-element.340), channel_id=1, source_target_pairs={{0,16},{4,20},{8,24},{12,28},{16,0},{20,4},{24,8},{28,12},{1,17},{... | collective-permute-start | bytes 1032200 | tf_op jit(solution)/shard_map/ppermute | solution.py:717
  163.4 17.6 %collective-permute-start.51 = (bf16[96,1536]{1,0:T(8,128)(2,1)S(1)}, bf16[96,1536]{1,0:T(8,128)(2,1)S(1)}, u32[]{:S(2)}, u32[]{:S(2)}) collective-permute-start(bf16[96,1536]{1,0:T(8,128)(2,1)S(1)} %get-tuple-element.342), channel_id=1, source_target_pairs={{0,8},{4,12},{8,0},{12,4},{16,24},{20,28},{24,16},{28,20},{1,9},{5... | collective-permute-start | bytes 884744 | tf_op jit(solution)/shard_map/ppermute | solution.py:717
  183.0 13.6 %collective-permute-start.55 = (bf16[96,1664]{1,0:T(8,128)(2,1)S(1)}, bf16[96,1664]{1,0:T(8,128)(2,1)S(1)}, u32[]{:S(2)}, u32[]{:S(2)}) collective-permute-start(bf16[96,1664]{1,0:T(8,128)(2,1)S(1)} %get-tuple-element.356), channel_id=1, source_target_pairs={{0,1},{1,0},{2,3},{3,2},{4,5},{5,4},{6,7},{7,6},{8,9},{9,8},{10,11... | collective-permute-start | bytes 958472 | tf_op jit(solution)/shard_map/ppermute | solution.py:717
  183.0 14.2 %collective-permute-start.57 = (bf16[48,1536]{1,0:T(8,128)(2,1)S(1)}, bf16[48,1536]{1,0:T(8,128)(2,1)S(1)}, u32[]{:S(2)}, u32[]{:S(2)}) collective-permute-start(bf16[48,1536]{1,0:T(8,128)(2,1)S(1)} %add.17.own), channel_id=1, source_target_pairs={{0,2},{1,3},{2,0},{3,1},{4,6},{5,7},{6,4},{7,5},{8,10},{9,11},{10,... | collective-permute-start | bytes 442376 | tf_op jit(solution)/shard_map/ppermute | solution.py:717
  185.0 15.5 %collective-permute-start.56 = (bf16[48,1536]{1,0:T(8,128)(2,1)S(1)}, bf16[48,1536]{1,0:T(8,128)(2,1)S(1)}, u32[]{:S(2)}, u32[]{:S(2)}) collective-permute-start(bf16[48,1536]{1,0:T(8,128)(2,1)S(1)} %add.17.own), channel_id=1, source_target_pairs={{0,1},{1,0},{2,3},{3,2},{4,5},{5,4},{6,7},{7,6},{8,9},{9,8},{10,11... | collective-permute-start | bytes 442376 | tf_op jit(solution)/shard_map/ppermute | solution.py:717
  (63 other events, 489.5 us)

commit v4 on v3

--- a/solution.py
+++ b/solution.py
@@ -237,7 +237,7 @@
             cols = slice(n * part, (n + 1) * part)
             qkv[ds, cols] = dot(x_ref[ds, :], w[:, cols]).astype(BF16)
 
-    rows_loop(size, 256, project)
+    rows_loop(size, size, project)
     masked = jnp.where(iota((size, 1), 0).astype(F32) < length[0:1, 0:1], 0.0, -1e30).astype(F32)
 
     def pair(p, carry):
@@ -277,7 +277,7 @@
         lower[:, cols] = joined[size // 2 :]
         return carry
 
-    lax.fori_loop(0, pairs, pair, 0)
+    lax.fori_loop(0, pairs, pair, 0, unroll=True)
 
 
 def residual_kernel(meta, hidden, attended, upper, lower, gain, w_half, w_other, residual, normed, left, middle, right, sums, w_out):
@@ -334,17 +334,18 @@
             inner = GELU_A + (3.0 * GELU_A * GELU_B) * square
             slope[ds, c : c + chunk] = (phi + 0.5 * t * (1.0 - th * th) * inner).astype(BF16)
 
-    rows_loop(x_ref.shape[0], 256, rows)
+    rows_loop(x_ref.shape[0], x_ref.shape[0], rows)
 
 
 def product_kernel(plan, n_out, *refs):
     meta, left_own, left_peer, right_own, right_peer = refs[:5]
     outs = refs[5 : 5 + n_out]
     grads = refs[5 + n_out]
-    for c in range(0, grads.shape[0], 256):
-        part = dot_left(left_own[:, c : c + 256], right_own[...])
-        part += dot_left(left_peer[:, c : c + 256], right_peer[...])
-        grads[c : c + 256, :] = part.astype(BF16)
+    step = 512 if grads.shape[0] % 512 == 0 else 384
+    for c in range(0, grads.shape[0], step):
+        part = dot_left(left_own[:, c : c + step], right_own[...])
+        part += dot_left(left_peer[:, c : c + step], right_peer[...])
+        grads[c : c + step, :] = part.astype(BF16)
     scatter_out(meta, grads, outs, plan)
 
 
@@ -376,7 +377,7 @@
             else:
                 part[0][ds, :] = total
 
-        rows_loop(size, 256, rows)
+        rows_loop(size, size, rows)
 
 
 def through_kernel(meta, residual, part, left, center, right, out_cot, pool_cot, gain, w_half, w_other,
@@ -396,7 +397,7 @@
         inv = lax.rsqrt(jnp.mean(x * x, axis=-1, keepdims=True) + EPS)
         u = gain[...] * gn
         xr = x * inv
-        t = iota((128, 1), 0) + ds.start
+        t = iota((256, 1), 0) + ds.start
         pool = jnp.where((t >= prefix) & (t < length), 1.0, 0.0) / count
         go = out_cot[ds, :].astype(F32) + pool * pool_cot[...]
         g = go + inv * (u - xr * jnp.mean(xr * u, axis=-1, keepdims=True))
@@ -407,7 +408,7 @@
         a = jnp.where(on_first, g[:, :half], g[:, half:]).astype(BF16)
         b = jnp.where(on_first, g[:, half:], g[:, :half]).astype(BF16)
         low_mine[ds, :] = a
-        low_given[pl.ds(ds.start - start, 128), :] = b
+        low_given[pl.ds(ds.start - start, 256), :] = b
         grad_keep[ds, :] = (dot_right(a, w_half[mine, :]) + dot_right(b, w_other[mine, :])).astype(BF16)
         grad_send[ds, :] = (dot_right(a, w_half[theirs, :]) + dot_right(b, w_other[theirs, :])).astype(BF16)
 
@@ -415,10 +416,10 @@
     for first, low_given in ((0, upper), (middle, lower)):
 
         def some(i, carry, first=first, low_given=low_given):
-            rows(pl.ds(pl.multiple_of(first + 128 * i, 128), 128), low_given, first)
+            rows(pl.ds(pl.multiple_of(first + 256 * i, 256), 256), low_given, first)
             return carry
 
-        lax.fori_loop(0, middle // 128, some, 0)
+        lax.fori_loop(0, middle // 256, some, 0)
 
 
 def attend_back_kernel(meta, qkv, powers, g_ref, a_ref, inv_sums, diag_in, out, diag, grads, slant):
@@ -440,7 +441,7 @@
         vp = qkv[:, vcols].astype(F32)
         do = g_ref[:, cols].astype(F32)
         prod = do * a_ref[:, cols].astype(F32)
-        dq_all = None
+        dq_all = dk_all = dv_all = None
         for side in range(2):
             head = 2 * p + side
             own = half if side == 0 else jnp.logical_not(half)
@@ -459,17 +460,13 @@
             for a in range(strips):
                 rows = slice(128 * a, 128 * a + 128)
                 off = 128 * (strips - 1 - a)
-                e = powers[head, rows, :]
-                ds = (e.astype(F32) * dot_right(va[rows], dos)).astype(BF16)
+                ds = (powers[head, rows, :].astype(F32) * dot_right(va[rows], dos)).astype(BF16)
                 grads[rows, :] = ds
                 slant[:, off : off + size] += ds.astype(F32)
-                dk = dot(ds, qp).astype(BF16)
-                dv = dot(e, dos).astype(BF16)
-                if side == 1:
-                    dk = jnp.where(half, out[rows, kcols].astype(F32), dk.astype(F32)).astype(BF16)
-                    dv = jnp.where(half, out[rows, vcols].astype(F32), dv.astype(F32)).astype(BF16)
-                out[rows, kcols] = dk
-                out[rows, vcols] = dv
+            dk = dot(grads[...], qp)
+            dv = dot(powers[head], dos)
+            dk_all = dk if side == 0 else jnp.where(half, dk_all, dk)
+            dv_all = dv if side == 0 else jnp.where(half, dv_all, dv)
             dq = dot_left(kp, grads[...]).T
             dq_all = dq if side == 0 else jnp.where(half, dq_all, dq)
             y = slant[...]
@@ -479,9 +476,11 @@
                 rest //= 2
             diag[pl.ds(head, 1), :] += pltpu.roll(y, 127, 1)
         out[:, cols] = dq_all.astype(BF16)
+        out[:, kcols] = dk_all.astype(BF16)
+        out[:, vcols] = dv_all.astype(BF16)
         return carry
 
-    lax.fori_loop(0, pairs, pair, 0)
+    lax.fori_loop(0, pairs, pair, 0, unroll=True)
 
 
 def weights_kernel(plan, n_out, *refs):
@@ -492,22 +491,22 @@
     part = dqkv_own.shape[1]
     depth = x_own.shape[1]
     half = depth // 2
-    for c in range(0, depth, 256):
-        cols = slice(c, c + 256)
+    for c in range(0, depth, 384):
+        cols = slice(c, c + 384)
         g = dot_left(x_own[:, cols], dqkv_own[...]) + dot_left(x_peer[:, cols], dqkv_peer[...])
         grads[cols, 0:part] = g.astype(BF16)
     core = meta[2]
     mine = pl.multiple_of(core * half, 16)
     theirs = pl.multiple_of((1 - core) * half, 16)
-    for c in range(0, half, 128):
-        cols = slice(c, c + 128)
+    for c in range(0, half, 384):
+        cols = slice(c, c + 384)
         g = dot_left(att_own[:, cols], low_own[...]) + dot_left(att_peer[:middle, cols], low_upper[...])
         g += dot_left(att_peer[middle:, cols], low_lower[...])
-        grads[pl.ds(mine + c, 128), part:] = g.astype(BF16)
+        grads[pl.ds(mine + c, 384), part:] = g.astype(BF16)
         g = dot_left(upper[:, cols], low_own[:middle]) + dot_left(lower[:, cols], low_own[middle:])
         g += dot_left(got_upper[:, cols], low_upper[...])
         g += dot_left(got_lower[:, cols], low_lower[...])
-        grads[pl.ds(theirs + c, 128), part:] = g.astype(BF16)
+        grads[pl.ds(theirs + c, 384), part:] = g.astype(BF16)
     grads[depth:, :] = jnp.zeros((16, grads.shape[1]), BF16)
     grads[depth:, 0:128] = small[...].astype(BF16)
     scatter_out(meta, grads, outs, plan)
@@ -537,8 +536,8 @@
         share(hidden, ds, value)
         part_own[ds, :] = value
 
-    rows_loop(size, 256, peers)
-    rows_loop(size, 256, own)
+    rows_loop(size, size, peers)
+    rows_loop(size, size, own)
     count = width // 128
     for n in range(count):
         small[n : n + 1, :] = gain_one[:, 128 * n : 128 * n + 128]
@@ -585,8 +584,8 @@
     def own(ds):
         part_own[ds, :] = dot(act_own[ds, :], w_ffout[...])
 
-    rows_loop(size, 256, peers)
-    rows_loop(size, 256, own)
+    rows_loop(size, size, peers)
+    rows_loop(size, size, own)
 
 
 def finish_kernel(meta, residual, part, left, right, sums, hidden_out, pooled, stats):
@@ -1152,8 +1151,7 @@
         at_x = on_x.send(at_parts[0])
         at_y = on_y.send(at_parts[1])
         in_keep, in_one = halve_first(in_parts, in_x, in_y, *in_last, last)
-        ff_four = quarter(ff_keep, ff_two, in_keep)
-        last = ff_four[0]
+        last = in_keep
     other_gh = [peer(after(v, last)) for v in send_gh]
     part_branch, *send_branch = call(
         output_kernel,
@@ -1175,21 +1173,22 @@
     last = grad_hidden
 
     if fast:
+        ff_four = quarter(ff_keep, ff_two, last)
+        last_y, last_x, last = turn(at_parts, at_x, at_y, ff_four[0])
+        at_last = (last_y, last_x)
         in_keep, in_two = halve_next(in_keep, in_one, last)
-        last_y, last_x, last = turn(at_parts, at_x, at_y, in_keep)
-        at_last = (last_y, last_x)
-        ff_four = quarters(*ff_four, last)
+        ff_four = quarters(*ff_four, in_keep)
+        at_keep, at_one = halve_first(at_parts, at_x, at_y, *at_last, in_keep, extra=128)
+        in_four = quarter(in_keep, in_two, at_keep)
         (grad_ffout,) = call(
             join_rows_kernel,
             "join_rows",
             meta,
             vm(*ff_four),
             [((block, width), F32, "v")],
-            deps=(last,),
+            deps=(in_four[0],),
         )
-        at_keep, at_one = halve_first(at_parts, at_x, at_y, *at_last, grad_ffout, extra=128)
-        in_four = quarter(in_keep, in_two, at_keep)
-        last = in_four[0]
+        last = grad_ffout
         other_branch = [peer(after(v, last)) for v in send_branch]
     else:
         other_branch = [peer(v) for v in send_branch]

time: 226 us -> 214 us (0.947)
  Pallas kernels: 102 us -> 88.9 us
  waiting for transfers between devices: 58.3 us -> 50.5 us
  starting transfers between devices: 53.8 us -> 60 us
    pallas_call x39, Pallas kernels: 102 us -> 88.9 us  [call(): pl.pallas_call(kernel, name=name, out_shape=[jax.ShapeDtypeStruct(s, d) f...]
    ppermute x66, waiting for transfers between devices: 58.3 us -> 50.5 us  [swap(): return lax.ppermute(v, axis, [(i, i ^ far) for i in range(count)])]
    ppermute x66, starting transfers between devices: 53.8 us -> 60 us  [swap(): return lax.ppermute(v, axis, [(i, i ^ far) for i in range(count)])]
  transfers between devices with their start and end apart: 66 -> 66, of which waited for: 22 -> 27; matrix products, arithmetic and copies ran while one was open for 1% -> 1% of each run, Pallas kernels for 43% -> 40%
where the time goes in v4:
time: 214 us; the launch traced here: 211 us
  Pallas kernels  88.9 us (42%)
  starting transfers between devices  60 us (28%)
  waiting for transfers between devices  50.5 us (24%)
  local copies, waits for them, and re-layouts  8.75 us (4%)
  between operations  2.95 us (1%)
    pallas_call x39, Pallas kernels, call(): pl.pallas_call(kernel, name=name, out_shape=[jax.ShapeDtypeStruct(s, d) f...  88.9 us
    ppermute x66, starting transfers between devices, swap(): return lax.ppermute(v, axis, [(i, i ^ far) for i in range(count)])  60 us
    ppermute x66, waiting for transfers between devices, swap(): return lax.ppermute(v, axis, [(i, i ^ far) for i in range(count)])  50.5 us
    unnamed x45, local copies, waits for them, and re-layouts  6.85 us
  transfers between devices with their start and end apart: 66, of which 27 were waited for; matrix products, arithmetic and copies ran while one was open for 1% of the time, Pallas kernels for 40%

profile of v4, /device:TPU:0, one launch (start us, length us, event | category | flops | bytes accessed | tf_op | source)
XLA Modules:
  0.0 211.2 jit_solution(5877014188882403234)
XLA Ops:
  3.1 3.3 %pack.1 = (bf16[96,1664]{1,0:T(8,128)(2,1)}, bf16[96,1664]{1,0:T(8,128)(2,1)}, bf16[96,1536]{1,0:T(8,128)(2,1)}, bf16[96,1536]{1,0:T(8,128)(2,1)}) custom-call(s32[8]{0:T(128)} %stack.20.meta.refs_0_, bf16[96,768]{1,0:T(8,128)(2,1)} %refs_0_.1, bf16[96,768]{1,0:T(8,128)(2,1)} %refs_1_.1, bf16[96,768]{1,0:T(8,128)(2,1)} %refs_2_.1, bf16[96,768]{1,0:T(8,128)(2,1)} %refs_3_.1, ...), custom_call_target="tpu_custom_call" | custom-call | flops 1000 | bytes 1000 | tf_op jit(solution)/shard_map/pack/pallas_call | solution.py:43
  6.6 2.9 %collective-permute-start.1 = (bf16[96,1664]{1,0:T(8,128)(2,1)}, bf16[96,1664]{1,0:T(8,128)(2,1)}, u32[]{:S(2)}, u32[]{:S(2)}) collective-permute-start(bf16[96,1664]{1,0:T(8,128)(2,1)} %get-tuple-element.195.refs_0_), channel_id=1, source_target_pairs={{0,8},{4,12},{8,0},{12,4},{16,24},{20,28},{24,16},{28,20},{1,9},{5... | collective-permute-start | bytes 958472 | tf_op jit(solution)/shard_map/ppermute | solution.py:716
  13.0 5.1 %collective-permute-done.1.refs_1_ = bf16[96,1664]{1,0:T(8,128)(2,1)} collective-permute-done((bf16[96,1664]{1,0:T(8,128)(2,1)}, bf16[96,1664]{1,0:T(8,128)(2,1)}, u32[]{:S(2)}, u32[]{:S(2)}) %collective-permute-start.1) | collective-permute-done | bytes 319520 | tf_op jit(solution)/shard_map/ppermute | solution.py:716
  31.0 2.7 %collective-permute-done.5.refs_3_ = bf16[96,1664]{1,0:T(8,128)(2,1)} collective-permute-done((bf16[96,1664]{1,0:T(8,128)(2,1)}, bf16[96,1664]{1,0:T(8,128)(2,1)}, u32[]{:S(2)}, u32[]{:S(2)}) %collective-permute-start.5) | collective-permute-done | bytes 319520 | tf_op jit(solution)/shard_map/ppermute | solution.py:716
  36.6 6.1 %prepare.1 = (bf16[512,768]{1,0:T(8,128)(2,1)S(1)}, bf16[512,768]{1,0:T(8,128)(2,1)S(1)}, f32[6,128,896]{2,1,0:T(8,128)S(1)}, f32[1,768]{1,0:T(1,128)S(1)}, f32[...) custom-call(s32[8]{0:T(128)S(1)} %copy-done.7, ...), custom_call_target="tpu_custom_call" | custom-call | flops 1000 | bytes 1000 | tf_op jit(solution)/shard_map/prepare/pallas_call | solution.py:43
  42.8 5.6 %attend_peer.1 = (bf16[512,1152]{1,0:T(8,128)(2,1)S(1)}, bf16[512,384]{1,0:T(8,128)(2,1)S(1)}, bf16[256,384]{1,0:T(8,128)(2,1)S(1)}, bf16[256,384]{1,0:T(8,128)(...) custom-call(s32[8]{0:T(128)S(1)} %copy-done.7, ...), custom_call_target="tpu_custom_call" | custom-call | flops 1000 | bytes 1000 | tf_op jit(solution)/shard_map/attend_peer/pallas_call | solution.py:43
  54.4 5.6 %attend_own.1 = (bf16[512,1152]{1,0:T(8,128)(2,1)S(1)}, bf16[512,384]{1,0:T(8,128)(2,1)S(1)}, bf16[256,384]{1,0:T(8,128)(2,1)S(1)}, bf16[256,384]{1,0:T(8,128)(2...) custom-call(s32[8]{0:T(128)S(1)} %copy-done.7, bf16[512,768]{1,0:T(8,128)(2,1)S(1)} %get-tuple-element.213.x_ref.refs_1_, ...), custom_call_target="tpu_custom_call" | custom-call | flops 1000 | bytes 1000 | tf_op jit(solution)/shard_map/attend_own/pallas_call | solution.py:43
  67.6 4.4 %expand_own.1 = (bf16[512,1536]{1,0:T(8,128)(2,1)S(1)}, bf16[512,1536]{1,0:T(8,128)(2,1)S(1)}, bf16[768,1536]{1,0:T(8,128)(2,1)S(1)}) custom-call(s32[8]{0:T(128)S(1)} %copy-done.7, bf16[512,768]{1,0:T(8,128)(2,1)S(1)} %get-tuple-element.225.refs_1_, bf16[192,1536]{1,0:T(8,128)(2,1)} %stack.21.refs_2_, ...), custom_call_target="tpu_custom_call" | custom-call | flops 1000 | bytes 111001000 | tf_op jit(solution)/shard_map/expand_own/pallas_call | solution.py:43
  76.0 3.2 %expand_peer.1 = (bf16[512,1536]{1,0:T(8,128)(2,1)S(1)}, bf16[512,1536]{1,0:T(8,128)(2,1)S(1)}, bf16[512,768]{1,0:T(8,128)(2,1)S(1)}) custom-call(s32[8]{0:T(128)S(1)} %copy-done.7, bf16[512,256]{1,0:T(8,128)(2,1)S(1)} %collective-permute-done.19.refs_1_, bf16[768,1536]{1,0:T(8,128)(2,1)S(1)} %get-tuple-element.233.refs_2_.refs_5_, ...), custom_call_target="tpu_custom_call" | custom-call | flops 1000 | bytes 1000 | tf_op jit(solution)/shard_map/expand_peer/pallas_call | solution.py:43
  79.3 3.4 %product.1 = (bf16[384,768]{1,0:T(8,128)(2,1)S(1)}, bf16[384,768]{1,0:T(8,128)(2,1)S(1)}, bf16[384,768]{1,0:T(8,128)(2,1)S(1)}, bf16[384,768]{1,0:T(8,128)(2,1)S(1)}) custom-call(s32[8]{0:T(128)S(1)} %copy-done.7, bf16[512,1536]{1,0:T(8,128)(2,1)S(1)} %get-tuple-element.235.refs_1_.act_own, bf16[512,1536]{1,0:T(8,128)(2,1)S(1)} %get-tuple-element.236.refs_2_.act_peer, ...), custom_call_target="tpu_custom_call" | custom-call | flops 1000 | bytes 1000 | tf_op jit(solution)/shard_map/product/pallas_call | solution.py:43
  85.4 6.0 %contract.1 = (bf16[512,1536]{1,0:T(8,128)(2,1)S(1)}, bf16[512,1536]{1,0:T(8,128)(2,1)S(1)}, f32[512,768]{1,0:T(8,128)S(1)}, bf16[512,256]{1,0:T(8,128)(2,1)}, b...) custom-call(s32[8]{0:T(128)S(1)} %copy-done.7, ...), custom_call_target="tpu_custom_call" | custom-call | flops 1000 | bytes 1000 | tf_op jit(solution)/shard_map/contract/pallas_call | solution.py:43
  92.1 3.5 %outer.1 = (bf16[192,1536]{1,0:T(8,128)(2,1)S(1)}, bf16[192,1536]{1,0:T(8,128)(2,1)S(1)}, bf16[192,1536]{1,0:T(8,128)(2,1)S(1)}, bf16[192,1536]{1,0:T(8,128)(2,1)S(1)}) custom-call(s32[8]{0:T(128)S(1)} %copy-done.7, bf16[512,768]{1,0:T(8,128)(2,1)S(1)} %get-tuple-element.225.refs_1_, bf16[512,768]{1,0:T(8,128)(2,1)S(1)} %get-tuple-element.234.refs_2_, ...), custom_call_target="tpu_custom_call" | custom-call | flops 1000 | bytes 1000 | tf_op jit(solution)/shard_map/outer/pallas_call | solution.py:43
  100.9 5.0 %attend_back_own.1 = (bf16[512,1152]{1,0:T(8,128)(2,1)S(1)}, f32[8,1024]{1,0:T(8,128)S(1)}) custom-call(s32[8]{0:T(128)S(1)} %copy-done.7, bf16[512,1152]{1,0:T(8,128)(2,1)S(1)} %copy-done.5, bf16[6,512,512]{2,1,0:T(8,128)(2,1)S(1)} %get-tuple-element.268.powers, bf16[512,384]{1,0:T(8,128)(2,1)S(1)} %get-tuple-element.269.g_ref, ...), custom_call_target="tpu_custom_call" | custom-call | flops 1000 | bytes 1000 | tf_op jit(solution)/shard_map/attend_back_own/pallas_call | solution.py:43
  111.9 5.0 %attend_back_peer.1 = (bf16[512,1152]{1,0:T(8,128)(2,1)S(1)}, f32[8,1024]{1,0:T(8,128)S(1)}) custom-call(s32[8]{0:T(128)S(1)} %copy-done.7, bf16[512,1152]{1,0:T(8,128)(2,1)S(1)} %copy-done.3, bf16[6,512,512]{2,1,0:T(8,128)(2,1)S(1)} %get-tuple-element.279.powers, bf16[512,384]{1,0:T(8,128)(2,1)S(1)} %collective-permute-done.29.g_ref, ...), custom_call_target="tpu_custom_call" | custom-call | flops 1000 | bytes 1000 | tf_op jit(solution)/shard_map/attend_back_peer/pallas_call | solution.py:43
  118.8 3.6 %inputs.1 = (f32[512,768]{1,0:T(8,128)S(1)}, bf16[512,384]{1,0:T(8,128)(2,1)S(1)}, bf16[512,384]{1,0:T(8,128)(2,1)S(1)}, f32[16,128]{1,0:T(8,128)S(1)}) custom-call(s32[8]{0:T(128)S(1)} %copy-done.7, bf16[512,1152]{1,0:T(8,128)(2,1)S(1)} %get-tuple-element.271.dqkv_own.refs_3_, bf16[512,1152]{1,0:T(8,128)(2,1)S(1)} %get-tuple-element.287.dqkv_peer.refs_4_, ...), custom_call_target="tpu_custom_call" | custom-call | flops 1000 | bytes 1000 | tf_op jit(solution)/shard_map/inputs/pallas_call | solution.py:43
  126.0 3.8 %weights.1 = (bf16[208,1536]{1,0:T(8,128)(2,1)S(1)}, bf16[192,1536]{1,0:T(8,128)(2,1)S(1)}, bf16[208,1536]{1,0:T(8,128)(2,1)S(1)}, bf16[192,1536]{1,0:T(8,128)(2,1)S(1)}) custom-call(s32[8]{0:T(128)S(1)} %copy-done.7, bf16[512,768]{1,0:T(8,128)(2,1)S(1)} %get-tuple-element.213.x_ref.refs_1_, bf16[512,768]{1,0:T(8,128)(2,1)S(1)} %get-tuple-element.199.x_ref.refs_2_, ...), custom_call_target="tpu_custom_call" | custom-call | flops 1000 | bytes 1000 | tf_op jit(solution)/shard_map/weights/pallas_call | solution.py:43
  140.6 3.1 %output.1 = (f32[512,768]{1,0:T(8,128)S(1)}, bf16[512,384]{1,0:T(8,128)(2,1)S(1)}, bf16[512,384]{1,0:T(8,128)(2,1)S(1)}) custom-call(s32[8]{0:T(128)S(1)} %copy-done.7, bf16[512,1536]{1,0:T(8,128)(2,1)S(1)} %get-tuple-element.235.refs_1_.act_own, bf16[512,1536]{1,0:T(8,128)(2,1)S(1)} %get-tuple-element.236.refs_2_.act_peer, ...), custom_call_target="tpu_custom_call" | custom-call | flops 1000 | bytes 1000 | tf_op jit(solution)/shard_map/output/pallas_call | solution.py:43
  155.0 4.7 %collective-permute-done.51.by_high = bf16[96,768]{1,0:T(8,128)(2,1)S(1)} collective-permute-done((bf16[96,768]{1,0:T(8,128)(2,1)S(1)}, bf16[96,768]{1,0:T(8,128)(2,1)S(1)}, u32[]{:S(2)}, u32[]{:S(2)}) %collective-permute-start.51) | collective-permute-done | bytes 147488 | tf_op jit(solution)/shard_map/ppermute | solution.py:716
  168.7 3.5 %collective-permute-start.57 = (bf16[48,1536]{1,0:T(8,128)(2,1)S(1)}, bf16[48,1536]{1,0:T(8,128)(2,1)S(1)}, u32[]{:S(2)}, u32[]{:S(2)}) collective-permute-start(bf16[48,1536]{1,0:T(8,128)(2,1)S(1)} %add.17.own), channel_id=1, source_target_pairs={{0,2},{1,3},{2,0},{3,1},{4,6},{5,7},{6,4},{7,5},{8,10},{9,11},{10,... | collective-permute-start | bytes 442376 | tf_op jit(solution)/shard_map/ppermute | solution.py:716
  174.3 7.3 %collective-permute-done.55.b = bf16[96,1664]{1,0:T(8,128)(2,1)S(1)} collective-permute-done((bf16[96,1664]{1,0:T(8,128)(2,1)S(1)}, bf16[96,1664]{1,0:T(8,128)(2,1)S(1)}, u32[]{:S(2)}, u32[]{:S(2)}) %collective-permute-start.55) | collective-permute-done | bytes 319520 | tf_op jit(solution)/shard_map/ppermute | solution.py:716
  183.7 2.8 %collective-permute-start.59 = (bf16[48,1664]{1,0:T(8,128)(2,1)S(1)}, bf16[48,1664]{1,0:T(8,128)(2,1)S(1)}, u32[]{:S(2)}, u32[]{:S(2)}) collective-permute-start(bf16[48,1664]{1,0:T(8,128)(2,1)S(1)} %get-tuple-element.362), channel_id=1, source_target_pairs={{0,2},{1,3},{2,0},{3,1},{4,6},{5,7},{6,4},{7,5},{8,10},{9,11},{10,... | collective-permute-start | bytes 479240 | tf_op jit(solution)/shard_map/ppermute | solution.py:716
  186.5 3.4 %collective-permute-done.58.by_both = bf16[48,1536]{1,0:T(8,128)(2,1)S(1)} collective-permute-done((bf16[48,1536]{1,0:T(8,128)(2,1)S(1)}, bf16[48,1536]{1,0:T(8,128)(2,1)S(1)}, u32[]{:S(2)}, u32[]{:S(2)}) %collective-permute-start.58) | collective-permute-done | bytes 147488 | tf_op jit(solution)/shard_map/ppermute | solution.py:716
  197.5 4.2 %collective-permute-done.62.by_high = bf16[48,1536]{1,0:T(8,128)(2,1)S(1)} collective-permute-done((bf16[48,1536]{1,0:T(8,128)(2,1)S(1)}, bf16[48,1536]{1,0:T(8,128)(2,1)S(1)}, u32[]{:S(2)}, u32[]{:S(2)}) %collective-permute-start.62) | collective-permute-done | bytes 147488 | tf_op jit(solution)/shard_map/ppermute | solution.py:716
  203.8 3.1 %collective-permute-done.64.by_both = bf16[48,1536]{1,0:T(8,128)(2,1)S(1)} collective-permute-done((bf16[48,1536]{1,0:T(8,128)(2,1)S(1)}, bf16[48,1536]{1,0:T(8,128)(2,1)S(1)}, u32[]{:S(2)}, u32[]{:S(2)}) %collective-permute-start.64) | collective-permute-done | bytes 147488 | tf_op jit(solution)/shard_map/ppermute | solution.py:716
  (205 shorter events, 106.9 us)
Async XLA Ops:
  0.7 12.3 %collective-permute-start = (bf16[512,768]{1,0:T(8,128)(2,1)}, bf16[512,768]{1,0:T(8,128)(2,1)S(1)}, u32[]{:S(2)}, u32[]{:S(2)}) collective-permute-start(bf16[512,768]{1,0:T(8,128)(2,1)} %hidden.9), channel_id=1, source_target_pairs={{0,4},{4,0},{8,12},{12,8},{16,20},{20,16},{24,28},{28,24},{1,5},{5... | collective-permute-start | bytes 2359304 | tf_op jit(solution)/shard_map/ppermute | solution.py:716
  6.6 11.5 %collective-permute-start.1 = (bf16[96,1664]{1,0:T(8,128)(2,1)}, bf16[96,1664]{1,0:T(8,128)(2,1)}, u32[]{:S(2)}, u32[]{:S(2)}) collective-permute-start(bf16[96,1664]{1,0:T(8,128)(2,1)} %get-tuple-element.195.refs_0_), channel_id=1, source_target_pairs={{0,8},{4,12},{8,0},{12,4},{16,24},{20,28},{24,16},{28,20},{1,9},{5... | collective-permute-start | bytes 958472 | tf_op jit(solution)/shard_map/ppermute | solution.py:716
  11.0 14.9 %collective-permute-start.6 = (bf16[96,1664]{1,0:T(8,128)(2,1)S(1)}, bf16[96,1664]{1,0:T(8,128)(2,1)S(1)}, u32[]{:S(2)}, u32[]{:S(2)}) collective-permute-start(bf16[96,1664]{1,0:T(8,128)(2,1)S(1)} %collective-permute-done.3.refs_4_), channel_id=1, source_target_pairs={{0,8},{4,12},{8,0},{12,4},{16,24},{20,28},{24,16},{28,20},{1,9},{5... | collective-permute-start | bytes 958472 | tf_op jit(solution)/shard_map/ppermute | solution.py:716
  12.5 15.2 %collective-permute-start.2 = (bf16[96,1664]{1,0:T(8,128)(2,1)}, bf16[96,1664]{1,0:T(8,128)(2,1)S(1)}, u32[]{:S(2)}, u32[]{:S(2)}) collective-permute-start(bf16[96,1664]{1,0:T(8,128)(2,1)} %get-tuple-element.195.refs_0_), channel_id=1, source_target_pairs={{0,16},{4,20},{8,24},{12,28},{16,0},{20,4},{24,8},{28,12},{1,17},{... | collective-permute-start | bytes 958472 | tf_op jit(solution)/shard_map/ppermute | solution.py:716
  20.0 13.7 %collective-permute-start.5 = (bf16[96,1664]{1,0:T(8,128)(2,1)}, bf16[96,1664]{1,0:T(8,128)(2,1)}, u32[]{:S(2)}, u32[]{:S(2)}) collective-permute-start(bf16[96,1664]{1,0:T(8,128)(2,1)} %collective-permute-done.1.refs_1_), channel_id=1, source_target_pairs={{0,16},{4,20},{8,24},{12,28},{16,0},{20,4},{24,8},{28,12},{1,17},{... | collective-permute-start | bytes 958472 | tf_op jit(solution)/shard_map/ppermute | solution.py:716
  21.5 12.2 %collective-permute-start.7 = (bf16[96,1664]{1,0:T(8,128)(2,1)}, bf16[96,1664]{1,0:T(8,128)(2,1)}, u32[]{:S(2)}, u32[]{:S(2)}) collective-permute-start(bf16[96,1664]{1,0:T(8,128)(2,1)} %collective-permute-done.4.refs_6_), channel_id=1, source_target_pairs={{0,8},{4,12},{8,0},{12,4},{16,24},{20,28},{24,16},{28,20},{1,9},{5... | collective-permute-start | bytes 958472 | tf_op jit(solution)/shard_map/ppermute | solution.py:716
  26.7 22.2 %collective-permute-start.11 = (bf16[192,1536]{1,0:T(8,128)(2,1)}, bf16[192,1536]{1,0:T(8,128)(2,1)}, u32[]{:S(2)}, u32[]{:S(2)}) collective-permute-start(bf16[192,1536]{1,0:T(8,128)(2,1)} %stack.21.refs_2_), channel_id=1, source_target_pairs={{0,8},{4,12},{8,0},{12,4},{16,24},{20,28},{24,16},{28,20},{1,9},{5... | collective-permute-start | bytes 1769480 | tf_op jit(solution)/shard_map/ppermute | solution.py:716
  28.4 20.5 %collective-permute-start.12 = (bf16[192,1536]{1,0:T(8,128)(2,1)}, bf16[192,1536]{1,0:T(8,128)(2,1)}, u32[]{:S(2)}, u32[]{:S(2)}) collective-permute-start(bf16[192,1536]{1,0:T(8,128)(2,1)} %stack.21.refs_2_), channel_id=1, source_target_pairs={{0,16},{4,20},{8,24},{12,28},{16,0},{20,4},{24,8},{28,12},{1,17},{... | collective-permute-start | bytes 1769480 | tf_op jit(solution)/shard_map/ppermute | solution.py:716
  48.4 13.8 %collective-permute-start.8 = (bf16[512,768]{1,0:T(8,128)(2,1)S(1)}, bf16[512,768]{1,0:T(8,128)(2,1)S(1)}, u32[]{:S(2)}, u32[]{:S(2)}) collective-permute-start(bf16[512,768]{1,0:T(8,128)(2,1)S(1)} %low.1.refs_3_), channel_id=1, source_target_pairs={{0,4},{4,0},{8,12},{12,8},{16,20},{20,16},{24,28},{28,24},{1,5},{5... | collective-permute-start | bytes 2359304 | tf_op jit(solution)/shard_map/ppermute | solution.py:716
  53.3 20.1 %collective-permute-start.17 = (bf16[384,768]{1,0:T(8,128)(2,1)S(1)}, bf16[384,768]{1,0:T(8,128)(2,1)S(1)}, u32[]{:S(2)}, u32[]{:S(2)}) collective-permute-start(bf16[384,768]{1,0:T(8,128)(2,1)S(1)} %copy-done.8), channel_id=1, source_target_pairs={{0,8},{4,12},{8,0},{12,4},{16,24},{20,28},{24,16},{28,20},{1,9},{5... | collective-permute-start | bytes 1769480 | tf_op jit(solution)/shard_map/ppermute | solution.py:716
  53.8 19.6 %collective-permute-start.18 = (bf16[384,768]{1,0:T(8,128)(2,1)S(1)}, bf16[384,768]{1,0:T(8,128)(2,1)S(1)}, u32[]{:S(2)}, u32[]{:S(2)}) collective-permute-start(bf16[384,768]{1,0:T(8,128)(2,1)S(1)} %copy-done.8), channel_id=1, source_target_pairs={{0,16},{4,20},{8,24},{12,28},{16,0},{20,4},{24,8},{28,12},{1,17},{... | collective-permute-start | bytes 1769480 | tf_op jit(solution)/shard_map/ppermute | solution.py:716
  82.7 16.1 %collective-permute-start.27 = (bf16[384,768]{1,0:T(8,128)(2,1)S(1)}, bf16[384,768]{1,0:T(8,128)(2,1)S(1)}, u32[]{:S(2)}, u32[]{:S(2)}) collective-permute-start(bf16[384,768]{1,0:T(8,128)(2,1)S(1)} %get-tuple-element.259), channel_id=1, source_target_pairs={{0,8},{4,12},{8,0},{12,4},{16,24},{20,28},{24,16},{28,20},{1,9},{5... | collective-permute-start | bytes 1769480 | tf_op jit(solution)/shard_map/ppermute | solution.py:716
  84.0 14.8 %collective-permute-start.28 = (bf16[384,768]{1,0:T(8,128)(2,1)S(1)}, bf16[384,768]{1,0:T(8,128)(2,1)S(1)}, u32[]{:S(2)}, u32[]{:S(2)}) collective-permute-start(bf16[384,768]{1,0:T(8,128)(2,1)S(1)} %get-tuple-element.263), channel_id=1, source_target_pairs={{0,16},{4,20},{8,24},{12,28},{16,0},{20,4},{24,8},{28,12},{1,17},{... | collective-permute-start | bytes 1769480 | tf_op jit(solution)/shard_map/ppermute | solution.py:716
  105.9 17.0 %collective-permute-start.33 = (bf16[192,1536]{1,0:T(8,128)(2,1)S(1)}, bf16[192,1536]{1,0:T(8,128)(2,1)S(1)}, u32[]{:S(2)}, u32[]{:S(2)}) collective-permute-start(bf16[192,1536]{1,0:T(8,128)(2,1)S(1)} %get-tuple-element.292), channel_id=1, source_target_pairs={{0,8},{4,12},{8,0},{12,4},{16,24},{20,28},{24,16},{28,20},{1,9},{5... | collective-permute-start | bytes 1769480 | tf_op jit(solution)/shard_map/ppermute | solution.py:716
  107.3 15.7 %collective-permute-start.34 = (bf16[192,1536]{1,0:T(8,128)(2,1)S(1)}, bf16[192,1536]{1,0:T(8,128)(2,1)S(1)}, u32[]{:S(2)}, u32[]{:S(2)}) collective-permute-start(bf16[192,1536]{1,0:T(8,128)(2,1)S(1)} %get-tuple-element.296), channel_id=1, source_target_pairs={{0,16},{4,20},{8,24},{12,28},{16,0},{20,4},{24,8},{28,12},{1,17},{... | collective-permute-start | bytes 1769480 | tf_op jit(solution)/shard_map/ppermute | solution.py:716
  129.8 17.8 %collective-permute-start.44 = (bf16[208,1536]{1,0:T(8,128)(2,1)S(1)}, bf16[208,1536]{1,0:T(8,128)(2,1)S(1)}, u32[]{:S(2)}, u32[]{:S(2)}) collective-permute-start(bf16[208,1536]{1,0:T(8,128)(2,1)S(1)} %get-tuple-element.329), channel_id=1, source_target_pairs={{0,8},{4,12},{8,0},{12,4},{16,24},{20,28},{24,16},{28,20},{1,9},{5... | collective-permute-start | bytes 1916936 | tf_op jit(solution)/shard_map/ppermute | solution.py:716
  131.0 16.0 %collective-permute-start.45 = (bf16[192,1536]{1,0:T(8,128)(2,1)S(1)}, bf16[192,1536]{1,0:T(8,128)(2,1)S(1)}, u32[]{:S(2)}, u32[]{:S(2)}) collective-permute-start(bf16[192,1536]{1,0:T(8,128)(2,1)S(1)} %get-tuple-element.332), channel_id=1, source_target_pairs={{0,16},{4,20},{8,24},{12,28},{16,0},{20,4},{24,8},{28,12},{1,17},{... | collective-permute-start | bytes 1769480 | tf_op jit(solution)/shard_map/ppermute | solution.py:716
  139.0 14.9 %collective-permute-start.46 = (bf16[96,1536]{1,0:T(8,128)(2,1)S(1)}, bf16[96,1536]{1,0:T(8,128)(2,1)S(1)}, u32[]{:S(2)}, u32[]{:S(2)}) collective-permute-start(bf16[96,1536]{1,0:T(8,128)(2,1)S(1)} %get-tuple-element.335), channel_id=1, source_target_pairs={{0,1},{1,0},{2,3},{3,2},{4,5},{5,4},{6,7},{7,6},{8,9},{9,8},{10,11... | collective-permute-start | bytes 884744 | tf_op jit(solution)/shard_map/ppermute | solution.py:716
  148.2 13.2 %collective-permute-start.47 = (bf16[112,1536]{1,0:T(8,128)(2,1)S(1)}, bf16[112,1536]{1,0:T(8,128)(2,1)S(1)}, u32[]{:S(2)}, u32[]{:S(2)}) collective-permute-start(bf16[112,1536]{1,0:T(8,128)(2,1)S(1)} %get-tuple-element.338), channel_id=1, source_target_pairs={{0,16},{4,20},{8,24},{12,28},{16,0},{20,4},{24,8},{28,12},{1,17},{... | collective-permute-start | bytes 1032200 | tf_op jit(solution)/shard_map/ppermute | solution.py:716
  148.9 12.5 %collective-permute-start.48 = (bf16[96,1536]{1,0:T(8,128)(2,1)S(1)}, bf16[96,1536]{1,0:T(8,128)(2,1)S(1)}, u32[]{:S(2)}, u32[]{:S(2)}) collective-permute-start(bf16[96,1536]{1,0:T(8,128)(2,1)S(1)} %get-tuple-element.340), channel_id=1, source_target_pairs={{0,8},{4,12},{8,0},{12,4},{16,24},{20,28},{24,16},{28,20},{1,9},{5... | collective-permute-start | bytes 884744 | tf_op jit(solution)/shard_map/ppermute | solution.py:716
  152.4 12.6 %collective-permute-start.50 = (bf16[96,768]{1,0:T(8,128)(2,1)S(1)}, bf16[96,768]{1,0:T(8,128)(2,1)S(1)}, u32[]{:S(2)}, u32[]{:S(2)}) collective-permute-start(bf16[96,768]{1,0:T(8,128)(2,1)S(1)} %add.16.own), channel_id=1, source_target_pairs={{0,1},{1,0},{2,3},{3,2},{4,5},{5,4},{6,7},{7,6},{8,9},{9,8},{10,11... | collective-permute-start | bytes 442376 | tf_op jit(solution)/shard_map/ppermute | solution.py:716
  168.0 13.6 %collective-permute-start.55 = (bf16[96,1664]{1,0:T(8,128)(2,1)S(1)}, bf16[96,1664]{1,0:T(8,128)(2,1)S(1)}, u32[]{:S(2)}, u32[]{:S(2)}) collective-permute-start(bf16[96,1664]{1,0:T(8,128)(2,1)S(1)} %get-tuple-element.356), channel_id=1, source_target_pairs={{0,1},{1,0},{2,3},{3,2},{4,5},{5,4},{6,7},{7,6},{8,9},{9,8},{10,11... | collective-permute-start | bytes 958472 | tf_op jit(solution)/shard_map/ppermute | solution.py:716
  168.7 13.5 %collective-permute-start.57 = (bf16[48,1536]{1,0:T(8,128)(2,1)S(1)}, bf16[48,1536]{1,0:T(8,128)(2,1)S(1)}, u32[]{:S(2)}, u32[]{:S(2)}) collective-permute-start(bf16[48,1536]{1,0:T(8,128)(2,1)S(1)} %add.17.own), channel_id=1, source_target_pairs={{0,2},{1,3},{2,0},{3,1},{4,6},{5,7},{6,4},{7,5},{8,10},{9,11},{10,... | collective-permute-start | bytes 442376 | tf_op jit(solution)/shard_map/ppermute | solution.py:716
  172.2 14.3 %collective-permute-start.56 = (bf16[48,1536]{1,0:T(8,128)(2,1)S(1)}, bf16[48,1536]{1,0:T(8,128)(2,1)S(1)}, u32[]{:S(2)}, u32[]{:S(2)}) collective-permute-start(bf16[48,1536]{1,0:T(8,128)(2,1)S(1)} %add.17.own), channel_id=1, source_target_pairs={{0,1},{1,0},{2,3},{3,2},{4,5},{5,4},{6,7},{7,6},{8,9},{9,8},{10,11... | collective-permute-start | bytes 442376 | tf_op jit(solution)/shard_map/ppermute | solution.py:716
  (63 other events, 489.3 us)

commit v5 on v4

--- a/solution.py
+++ b/solution.py
@@ -11,7 +11,7 @@
 EPS = 1e-06
 F32 = jnp.float32
 BF16 = jnp.bfloat16
-VMEM_SPARE = 6 * 2**20
+VMEM_SPARE = 3 * 2**20
 WEIGHTS = {"turn": 30.0, "expand_own": 30.0}
 GELU_A = 0.7978845608028654
 GELU_B = 0.044715

time: 214 us -> 213 us (level)
    unnamed x45 -> x33, local copies, waits for them, and re-layouts: 6.85 us -> 6.81 us
  transfers between devices with their start and end apart: 66 -> 66, of which waited for: 27 -> 28; matrix products, arithmetic and copies ran while one was open for 1% -> 1% of each run, Pallas kernels for 40% -> 40%
where the time goes in v5:
time: 213 us; the launch traced here: 211 us
  Pallas kernels  88.7 us (42%)
  starting transfers between devices  60 us (28%)
  waiting for transfers between devices  50.5 us (24%)
  local copies, waits for them, and re-layouts  8.71 us (4%)
  between operations  2.87 us (1%)
    pallas_call x39, Pallas kernels, call(): pl.pallas_call(kernel, name=name, out_shape=[jax.ShapeDtypeStruct(s, d) f...  88.7 us
    ppermute x66, starting transfers between devices, swap(): return lax.ppermute(v, axis, [(i, i ^ far) for i in range(count)])  60 us
    ppermute x66, waiting for transfers between devices, swap(): return lax.ppermute(v, axis, [(i, i ^ far) for i in range(count)])  50.5 us
    unnamed x33, local copies, waits for them, and re-layouts  6.81 us
  transfers between devices with their start and end apart: 66, of which 28 were waited for; matrix products, arithmetic and copies ran while one was open for 1% of the time, Pallas kernels for 40%

profile of v5, /device:TPU:0, one launch (start us, length us, event | category | flops | bytes accessed | tf_op | source)
XLA Modules:
  0.0 210.8 jit_solution(7104810407457361682)
XLA Ops:
  3.1 3.3 %pack.1 = (bf16[96,1664]{1,0:T(8,128)(2,1)}, bf16[96,1664]{1,0:T(8,128)(2,1)}, bf16[96,1536]{1,0:T(8,128)(2,1)}, bf16[96,1536]{1,0:T(8,128)(2,1)}) custom-call(s32[8]{0:T(128)} %stack.20.meta.refs_0_, bf16[96,768]{1,0:T(8,128)(2,1)} %refs_0_.1, bf16[96,768]{1,0:T(8,128)(2,1)} %refs_1_.1, bf16[96,768]{1,0:T(8,128)(2,1)} %refs_2_.1, bf16[96,768]{1,0:T(8,128)(2,1)} %refs_3_.1, ...), custom_call_target="tpu_custom_call" | custom-call | flops 1000 | bytes 1000 | tf_op jit(solution)/shard_map/pack/pallas_call | solution.py:43
  6.6 2.9 %collective-permute-start.1 = (bf16[96,1664]{1,0:T(8,128)(2,1)}, bf16[96,1664]{1,0:T(8,128)(2,1)}, u32[]{:S(2)}, u32[]{:S(2)}) collective-permute-start(bf16[96,1664]{1,0:T(8,128)(2,1)} %get-tuple-element.195.refs_0_), channel_id=1, source_target_pairs={{0,8},{4,12},{8,0},{12,4},{16,24},{20,28},{24,16},{28,20},{1,9},{5... | collective-permute-start | bytes 958472 | tf_op jit(solution)/shard_map/ppermute | solution.py:716
  13.0 5.1 %collective-permute-done.1.refs_1_ = bf16[96,1664]{1,0:T(8,128)(2,1)} collective-permute-done((bf16[96,1664]{1,0:T(8,128)(2,1)}, bf16[96,1664]{1,0:T(8,128)(2,1)}, u32[]{:S(2)}, u32[]{:S(2)}) %collective-permute-start.1) | collective-permute-done | bytes 319520 | tf_op jit(solution)/shard_map/ppermute | solution.py:716
  31.0 2.7 %collective-permute-done.5.refs_3_ = bf16[96,1664]{1,0:T(8,128)(2,1)} collective-permute-done((bf16[96,1664]{1,0:T(8,128)(2,1)}, bf16[96,1664]{1,0:T(8,128)(2,1)}, u32[]{:S(2)}, u32[]{:S(2)}) %collective-permute-start.5) | collective-permute-done | bytes 319520 | tf_op jit(solution)/shard_map/ppermute | solution.py:716
  36.6 6.1 %prepare.1 = (bf16[512,768]{1,0:T(8,128)(2,1)S(1)}, bf16[512,768]{1,0:T(8,128)(2,1)S(1)}, f32[6,128,896]{2,1,0:T(8,128)S(1)}, f32[1,768]{1,0:T(1,128)S(1)}, f32[...) custom-call(s32[8]{0:T(128)S(1)} %copy-done.3, ...), custom_call_target="tpu_custom_call" | custom-call | flops 1000 | bytes 1000 | tf_op jit(solution)/shard_map/prepare/pallas_call | solution.py:43
  42.8 5.6 %attend_peer.1 = (bf16[512,1152]{1,0:T(8,128)(2,1)S(1)}, bf16[512,384]{1,0:T(8,128)(2,1)S(1)}, bf16[256,384]{1,0:T(8,128)(2,1)S(1)}, bf16[256,384]{1,0:T(8,128)(...) custom-call(s32[8]{0:T(128)S(1)} %copy-done.3, ...), custom_call_target="tpu_custom_call" | custom-call | flops 1000 | bytes 1000 | tf_op jit(solution)/shard_map/attend_peer/pallas_call | solution.py:43
  54.4 5.6 %attend_own.1 = (bf16[512,1152]{1,0:T(8,128)(2,1)S(1)}, bf16[512,384]{1,0:T(8,128)(2,1)S(1)}, bf16[256,384]{1,0:T(8,128)(2,1)S(1)}, bf16[256,384]{1,0:T(8,128)(2...) custom-call(s32[8]{0:T(128)S(1)} %copy-done.3, bf16[512,768]{1,0:T(8,128)(2,1)S(1)} %get-tuple-element.213.x_ref.refs_1_, ...), custom_call_target="tpu_custom_call" | custom-call | flops 1000 | bytes 1000 | tf_op jit(solution)/shard_map/attend_own/pallas_call | solution.py:43
  67.7 4.4 %expand_own.1 = (bf16[512,1536]{1,0:T(8,128)(2,1)S(1)}, bf16[512,1536]{1,0:T(8,128)(2,1)S(1)}, bf16[768,1536]{1,0:T(8,128)(2,1)S(1)}) custom-call(s32[8]{0:T(128)S(1)} %copy-done.3, bf16[512,768]{1,0:T(8,128)(2,1)S(1)} %get-tuple-element.225.refs_1_, bf16[192,1536]{1,0:T(8,128)(2,1)} %stack.21.refs_2_, ...), custom_call_target="tpu_custom_call" | custom-call | flops 1000 | bytes 111001000 | tf_op jit(solution)/shard_map/expand_own/pallas_call | solution.py:43
  75.7 3.2 %expand_peer.1 = (bf16[512,1536]{1,0:T(8,128)(2,1)S(1)}, bf16[512,1536]{1,0:T(8,128)(2,1)S(1)}, bf16[512,768]{1,0:T(8,128)(2,1)S(1)}) custom-call(s32[8]{0:T(128)S(1)} %copy-done.3, bf16[512,256]{1,0:T(8,128)(2,1)S(1)} %collective-permute-done.19.refs_1_, bf16[768,1536]{1,0:T(8,128)(2,1)S(1)} %get-tuple-element.233.refs_2_.refs_5_, ...), custom_call_target="tpu_custom_call" | custom-call | flops 1000 | bytes 1000 | tf_op jit(solution)/shard_map/expand_peer/pallas_call | solution.py:43
  78.9 3.4 %product.1 = (bf16[384,768]{1,0:T(8,128)(2,1)S(1)}, bf16[384,768]{1,0:T(8,128)(2,1)S(1)}, bf16[384,768]{1,0:T(8,128)(2,1)S(1)}, bf16[384,768]{1,0:T(8,128)(2,1)S(1)}) custom-call(s32[8]{0:T(128)S(1)} %copy-done.3, bf16[512,1536]{1,0:T(8,128)(2,1)S(1)} %get-tuple-element.235.refs_1_.act_own, bf16[512,1536]{1,0:T(8,128)(2,1)S(1)} %get-tuple-element.236.refs_2_.act_peer, ...), custom_call_target="tpu_custom_call" | custom-call | flops 1000 | bytes 1000 | tf_op jit(solution)/shard_map/product/pallas_call | solution.py:43
  85.1 6.0 %contract.1 = (bf16[512,1536]{1,0:T(8,128)(2,1)S(1)}, bf16[512,1536]{1,0:T(8,128)(2,1)S(1)}, f32[512,768]{1,0:T(8,128)S(1)}, bf16[512,256]{1,0:T(8,128)(2,1)S(1)...) custom-call(s32[8]{0:T(128)S(1)} %copy-done.3, ...), custom_call_target="tpu_custom_call" | custom-call | flops 1000 | bytes 1000 | tf_op jit(solution)/shard_map/contract/pallas_call | solution.py:43
  91.8 3.3 %outer.1 = (bf16[192,1536]{1,0:T(8,128)(2,1)S(1)}, bf16[192,1536]{1,0:T(8,128)(2,1)S(1)}, bf16[192,1536]{1,0:T(8,128)(2,1)S(1)}, bf16[192,1536]{1,0:T(8,128)(2,1)S(1)}) custom-call(s32[8]{0:T(128)S(1)} %copy-done.3, bf16[512,768]{1,0:T(8,128)(2,1)S(1)} %get-tuple-element.225.refs_1_, bf16[512,768]{1,0:T(8,128)(2,1)S(1)} %get-tuple-element.234.refs_2_, ...), custom_call_target="tpu_custom_call" | custom-call | flops 1000 | bytes 1000 | tf_op jit(solution)/shard_map/outer/pallas_call | solution.py:43
  100.5 5.0 %attend_back_own.1 = (bf16[512,1152]{1,0:T(8,128)(2,1)S(1)}, f32[8,1024]{1,0:T(8,128)S(1)}) custom-call(s32[8]{0:T(128)S(1)} %copy-done.3, bf16[512,1152]{1,0:T(8,128)(2,1)S(1)} %get-tuple-element.267.qkv, bf16[6,512,512]{2,1,0:T(8,128)(2,1)S(1)} %get-tuple-element.268.powers, bf16[512,384]{1,0:T(8,128)(2,1)S(1)} %get-tuple-element.269.g_ref, ...), custom_call_target="tpu_custom_call" | custom-call | flops 1000 | bytes 1000 | tf_op jit(solution)/shard_map/attend_back_own/pallas_call | solution.py:43
  111.3 5.0 %attend_back_peer.1 = (bf16[512,1152]{1,0:T(8,128)(2,1)S(1)}, f32[8,1024]{1,0:T(8,128)S(1)}) custom-call(s32[8]{0:T(128)S(1)} %copy-done.3, bf16[512,1152]{1,0:T(8,128)(2,1)S(1)} %get-tuple-element.278.qkv, bf16[6,512,512]{2,1,0:T(8,128)(2,1)S(1)} %get-tuple-element.279.powers, bf16[512,384]{1,0:T(8,128)(2,1)S(1)} %collective-permute-done.29.g_ref, ...), custom_call_target="tpu_custom_call" | custom-call | flops 1000 | bytes 1000 | tf_op jit(solution)/shard_map/attend_back_peer/pallas_call | solution.py:43
  118.4 3.6 %inputs.1 = (f32[512,768]{1,0:T(8,128)S(1)}, bf16[512,384]{1,0:T(8,128)(2,1)S(1)}, bf16[512,384]{1,0:T(8,128)(2,1)S(1)}, f32[16,128]{1,0:T(8,128)S(1)}) custom-call(s32[8]{0:T(128)S(1)} %copy-done.3, bf16[512,1152]{1,0:T(8,128)(2,1)S(1)} %get-tuple-element.271.dqkv_own.refs_3_, bf16[512,1152]{1,0:T(8,128)(2,1)S(1)} %get-tuple-element.287.dqkv_peer.refs_4_, ...), custom_call_target="tpu_custom_call" | custom-call | flops 1000 | bytes 1000 | tf_op jit(solution)/shard_map/inputs/pallas_call | solution.py:43
  125.6 3.8 %weights.1 = (bf16[208,1536]{1,0:T(8,128)(2,1)S(1)}, bf16[192,1536]{1,0:T(8,128)(2,1)S(1)}, bf16[208,1536]{1,0:T(8,128)(2,1)S(1)}, bf16[192,1536]{1,0:T(8,128)(2,1)S(1)}) custom-call(s32[8]{0:T(128)S(1)} %copy-done.3, bf16[512,768]{1,0:T(8,128)(2,1)S(1)} %get-tuple-element.213.x_ref.refs_1_, bf16[512,768]{1,0:T(8,128)(2,1)S(1)} %get-tuple-element.199.x_ref.refs_2_, ...), custom_call_target="tpu_custom_call" | custom-call | flops 1000 | bytes 1000 | tf_op jit(solution)/shard_map/weights/pallas_call | solution.py:43
  140.2 3.1 %output.1 = (f32[512,768]{1,0:T(8,128)S(1)}, bf16[512,384]{1,0:T(8,128)(2,1)S(1)}, bf16[512,384]{1,0:T(8,128)(2,1)S(1)}) custom-call(s32[8]{0:T(128)S(1)} %copy-done.3, bf16[512,1536]{1,0:T(8,128)(2,1)S(1)} %get-tuple-element.235.refs_1_.act_own, bf16[512,1536]{1,0:T(8,128)(2,1)S(1)} %get-tuple-element.236.refs_2_.act_peer, ...), custom_call_target="tpu_custom_call" | custom-call | flops 1000 | bytes 1000 | tf_op jit(solution)/shard_map/output/pallas_call | solution.py:43
  154.6 4.7 %collective-permute-done.51.by_high = bf16[96,768]{1,0:T(8,128)(2,1)S(1)} collective-permute-done((bf16[96,768]{1,0:T(8,128)(2,1)S(1)}, bf16[96,768]{1,0:T(8,128)(2,1)S(1)}, u32[]{:S(2)}, u32[]{:S(2)}) %collective-permute-start.51) | collective-permute-done | bytes 147488 | tf_op jit(solution)/shard_map/ppermute | solution.py:716
  168.3 3.5 %collective-permute-start.57 = (bf16[48,1536]{1,0:T(8,128)(2,1)S(1)}, bf16[48,1536]{1,0:T(8,128)(2,1)S(1)}, u32[]{:S(2)}, u32[]{:S(2)}) collective-permute-start(bf16[48,1536]{1,0:T(8,128)(2,1)S(1)} %add.17.own), channel_id=1, source_target_pairs={{0,2},{1,3},{2,0},{3,1},{4,6},{5,7},{6,4},{7,5},{8,10},{9,11},{10,... | collective-permute-start | bytes 442376 | tf_op jit(solution)/shard_map/ppermute | solution.py:716
  173.9 7.3 %collective-permute-done.55.b = bf16[96,1664]{1,0:T(8,128)(2,1)S(1)} collective-permute-done((bf16[96,1664]{1,0:T(8,128)(2,1)S(1)}, bf16[96,1664]{1,0:T(8,128)(2,1)S(1)}, u32[]{:S(2)}, u32[]{:S(2)}) %collective-permute-start.55) | collective-permute-done | bytes 319520 | tf_op jit(solution)/shard_map/ppermute | solution.py:716
  183.4 2.8 %collective-permute-start.59 = (bf16[48,1664]{1,0:T(8,128)(2,1)S(1)}, bf16[48,1664]{1,0:T(8,128)(2,1)S(1)}, u32[]{:S(2)}, u32[]{:S(2)}) collective-permute-start(bf16[48,1664]{1,0:T(8,128)(2,1)S(1)} %get-tuple-element.362), channel_id=1, source_target_pairs={{0,2},{1,3},{2,0},{3,1},{4,6},{5,7},{6,4},{7,5},{8,10},{9,11},{10,... | collective-permute-start | bytes 479240 | tf_op jit(solution)/shard_map/ppermute | solution.py:716
  186.1 3.4 %collective-permute-done.58.by_both = bf16[48,1536]{1,0:T(8,128)(2,1)S(1)} collective-permute-done((bf16[48,1536]{1,0:T(8,128)(2,1)S(1)}, bf16[48,1536]{1,0:T(8,128)(2,1)S(1)}, u32[]{:S(2)}, u32[]{:S(2)}) %collective-permute-start.58) | collective-permute-done | bytes 147488 | tf_op jit(solution)/shard_map/ppermute | solution.py:716
  197.1 4.2 %collective-permute-done.62.by_high = bf16[48,1536]{1,0:T(8,128)(2,1)S(1)} collective-permute-done((bf16[48,1536]{1,0:T(8,128)(2,1)S(1)}, bf16[48,1536]{1,0:T(8,128)(2,1)S(1)}, u32[]{:S(2)}, u32[]{:S(2)}) %collective-permute-start.62) | collective-permute-done | bytes 147488 | tf_op jit(solution)/shard_map/ppermute | solution.py:716
  203.4 3.1 %collective-permute-done.64.by_both = bf16[48,1536]{1,0:T(8,128)(2,1)S(1)} collective-permute-done((bf16[48,1536]{1,0:T(8,128)(2,1)S(1)}, bf16[48,1536]{1,0:T(8,128)(2,1)S(1)}, u32[]{:S(2)}, u32[]{:S(2)}) %collective-permute-start.64) | collective-permute-done | bytes 147488 | tf_op jit(solution)/shard_map/ppermute | solution.py:716
  (193 shorter events, 106.8 us)
Async XLA Ops:
  0.7 12.3 %collective-permute-start = (bf16[512,768]{1,0:T(8,128)(2,1)}, bf16[512,768]{1,0:T(8,128)(2,1)S(1)}, u32[]{:S(2)}, u32[]{:S(2)}) collective-permute-start(bf16[512,768]{1,0:T(8,128)(2,1)} %hidden.9), channel_id=1, source_target_pairs={{0,4},{4,0},{8,12},{12,8},{16,20},{20,16},{24,28},{28,24},{1,5},{5... | collective-permute-start | bytes 2359304 | tf_op jit(solution)/shard_map/ppermute | solution.py:716
  6.6 11.5 %collective-permute-start.1 = (bf16[96,1664]{1,0:T(8,128)(2,1)}, bf16[96,1664]{1,0:T(8,128)(2,1)}, u32[]{:S(2)}, u32[]{:S(2)}) collective-permute-start(bf16[96,1664]{1,0:T(8,128)(2,1)} %get-tuple-element.195.refs_0_), channel_id=1, source_target_pairs={{0,8},{4,12},{8,0},{12,4},{16,24},{20,28},{24,16},{28,20},{1,9},{5... | collective-permute-start | bytes 958472 | tf_op jit(solution)/shard_map/ppermute | solution.py:716
  11.0 14.9 %collective-permute-start.6 = (bf16[96,1664]{1,0:T(8,128)(2,1)S(1)}, bf16[96,1664]{1,0:T(8,128)(2,1)S(1)}, u32[]{:S(2)}, u32[]{:S(2)}) collective-permute-start(bf16[96,1664]{1,0:T(8,128)(2,1)S(1)} %collective-permute-done.3.refs_4_), channel_id=1, source_target_pairs={{0,8},{4,12},{8,0},{12,4},{16,24},{20,28},{24,16},{28,20},{1,9},{5... | collective-permute-start | bytes 958472 | tf_op jit(solution)/shard_map/ppermute | solution.py:716
  12.5 15.2 %collective-permute-start.2 = (bf16[96,1664]{1,0:T(8,128)(2,1)}, bf16[96,1664]{1,0:T(8,128)(2,1)S(1)}, u32[]{:S(2)}, u32[]{:S(2)}) collective-permute-start(bf16[96,1664]{1,0:T(8,128)(2,1)} %get-tuple-element.195.refs_0_), channel_id=1, source_target_pairs={{0,16},{4,20},{8,24},{12,28},{16,0},{20,4},{24,8},{28,12},{1,17},{... | collective-permute-start | bytes 958472 | tf_op jit(solution)/shard_map/ppermute | solution.py:716
  20.0 13.7 %collective-permute-start.5 = (bf16[96,1664]{1,0:T(8,128)(2,1)}, bf16[96,1664]{1,0:T(8,128)(2,1)}, u32[]{:S(2)}, u32[]{:S(2)}) collective-permute-start(bf16[96,1664]{1,0:T(8,128)(2,1)} %collective-permute-done.1.refs_1_), channel_id=1, source_target_pairs={{0,16},{4,20},{8,24},{12,28},{16,0},{20,4},{24,8},{28,12},{1,17},{... | collective-permute-start | bytes 958472 | tf_op jit(solution)/shard_map/ppermute | solution.py:716
  21.5 12.2 %collective-permute-start.7 = (bf16[96,1664]{1,0:T(8,128)(2,1)}, bf16[96,1664]{1,0:T(8,128)(2,1)}, u32[]{:S(2)}, u32[]{:S(2)}) collective-permute-start(bf16[96,1664]{1,0:T(8,128)(2,1)} %collective-permute-done.4.refs_6_), channel_id=1, source_target_pairs={{0,8},{4,12},{8,0},{12,4},{16,24},{20,28},{24,16},{28,20},{1,9},{5... | collective-permute-start | bytes 958472 | tf_op jit(solution)/shard_map/ppermute | solution.py:716
  26.7 22.2 %collective-permute-start.11 = (bf16[192,1536]{1,0:T(8,128)(2,1)}, bf16[192,1536]{1,0:T(8,128)(2,1)}, u32[]{:S(2)}, u32[]{:S(2)}) collective-permute-start(bf16[192,1536]{1,0:T(8,128)(2,1)} %stack.21.refs_2_), channel_id=1, source_target_pairs={{0,8},{4,12},{8,0},{12,4},{16,24},{20,28},{24,16},{28,20},{1,9},{5... | collective-permute-start | bytes 1769480 | tf_op jit(solution)/shard_map/ppermute | solution.py:716
  28.4 20.5 %collective-permute-start.12 = (bf16[192,1536]{1,0:T(8,128)(2,1)}, bf16[192,1536]{1,0:T(8,128)(2,1)}, u32[]{:S(2)}, u32[]{:S(2)}) collective-permute-start(bf16[192,1536]{1,0:T(8,128)(2,1)} %stack.21.refs_2_), channel_id=1, source_target_pairs={{0,16},{4,20},{8,24},{12,28},{16,0},{20,4},{24,8},{28,12},{1,17},{... | collective-permute-start | bytes 1769480 | tf_op jit(solution)/shard_map/ppermute | solution.py:716
  48.4 13.8 %collective-permute-start.8 = (bf16[512,768]{1,0:T(8,128)(2,1)S(1)}, bf16[512,768]{1,0:T(8,128)(2,1)S(1)}, u32[]{:S(2)}, u32[]{:S(2)}) collective-permute-start(bf16[512,768]{1,0:T(8,128)(2,1)S(1)} %low.1.refs_3_), channel_id=1, source_target_pairs={{0,4},{4,0},{8,12},{12,8},{16,20},{20,16},{24,28},{28,24},{1,5},{5... | collective-permute-start | bytes 2359304 | tf_op jit(solution)/shard_map/ppermute | solution.py:716
  53.2 19.8 %collective-permute-start.17 = (bf16[384,768]{1,0:T(8,128)(2,1)S(1)}, bf16[384,768]{1,0:T(8,128)(2,1)S(1)}, u32[]{:S(2)}, u32[]{:S(2)}) collective-permute-start(bf16[384,768]{1,0:T(8,128)(2,1)S(1)} %copy-done.4), channel_id=1, source_target_pairs={{0,8},{4,12},{8,0},{12,4},{16,24},{20,28},{24,16},{28,20},{1,9},{5... | collective-permute-start | bytes 1769480 | tf_op jit(solution)/shard_map/ppermute | solution.py:716
  53.8 19.3 %collective-permute-start.18 = (bf16[384,768]{1,0:T(8,128)(2,1)S(1)}, bf16[384,768]{1,0:T(8,128)(2,1)S(1)}, u32[]{:S(2)}, u32[]{:S(2)}) collective-permute-start(bf16[384,768]{1,0:T(8,128)(2,1)S(1)} %copy-done.4), channel_id=1, source_target_pairs={{0,16},{4,20},{8,24},{12,28},{16,0},{20,4},{24,8},{28,12},{1,17},{... | collective-permute-start | bytes 1769480 | tf_op jit(solution)/shard_map/ppermute | solution.py:716
  82.3 16.1 %collective-permute-start.27 = (bf16[384,768]{1,0:T(8,128)(2,1)S(1)}, bf16[384,768]{1,0:T(8,128)(2,1)S(1)}, u32[]{:S(2)}, u32[]{:S(2)}) collective-permute-start(bf16[384,768]{1,0:T(8,128)(2,1)S(1)} %get-tuple-element.259), channel_id=1, source_target_pairs={{0,8},{4,12},{8,0},{12,4},{16,24},{20,28},{24,16},{28,20},{1,9},{5... | collective-permute-start | bytes 1769480 | tf_op jit(solution)/shard_map/ppermute | solution.py:716
  83.6 14.8 %collective-permute-start.28 = (bf16[384,768]{1,0:T(8,128)(2,1)S(1)}, bf16[384,768]{1,0:T(8,128)(2,1)S(1)}, u32[]{:S(2)}, u32[]{:S(2)}) collective-permute-start(bf16[384,768]{1,0:T(8,128)(2,1)S(1)} %get-tuple-element.263), channel_id=1, source_target_pairs={{0,16},{4,20},{8,24},{12,28},{16,0},{20,4},{24,8},{28,12},{1,17},{... | collective-permute-start | bytes 1769480 | tf_op jit(solution)/shard_map/ppermute | solution.py:716
  105.6 17.0 %collective-permute-start.33 = (bf16[192,1536]{1,0:T(8,128)(2,1)S(1)}, bf16[192,1536]{1,0:T(8,128)(2,1)S(1)}, u32[]{:S(2)}, u32[]{:S(2)}) collective-permute-start(bf16[192,1536]{1,0:T(8,128)(2,1)S(1)} %get-tuple-element.292), channel_id=1, source_target_pairs={{0,8},{4,12},{8,0},{12,4},{16,24},{20,28},{24,16},{28,20},{1,9},{5... | collective-permute-start | bytes 1769480 | tf_op jit(solution)/shard_map/ppermute | solution.py:716
  106.8 15.8 %collective-permute-start.34 = (bf16[192,1536]{1,0:T(8,128)(2,1)S(1)}, bf16[192,1536]{1,0:T(8,128)(2,1)S(1)}, u32[]{:S(2)}, u32[]{:S(2)}) collective-permute-start(bf16[192,1536]{1,0:T(8,128)(2,1)S(1)} %get-tuple-element.296), channel_id=1, source_target_pairs={{0,16},{4,20},{8,24},{12,28},{16,0},{20,4},{24,8},{28,12},{1,17},{... | collective-permute-start | bytes 1769480 | tf_op jit(solution)/shard_map/ppermute | solution.py:716
  129.4 17.8 %collective-permute-start.44 = (bf16[208,1536]{1,0:T(8,128)(2,1)S(1)}, bf16[208,1536]{1,0:T(8,128)(2,1)S(1)}, u32[]{:S(2)}, u32[]{:S(2)}) collective-permute-start(bf16[208,1536]{1,0:T(8,128)(2,1)S(1)} %get-tuple-element.329), channel_id=1, source_target_pairs={{0,8},{4,12},{8,0},{12,4},{16,24},{20,28},{24,16},{28,20},{1,9},{5... | collective-permute-start | bytes 1916936 | tf_op jit(solution)/shard_map/ppermute | solution.py:716
  130.6 16.0 %collective-permute-start.45 = (bf16[192,1536]{1,0:T(8,128)(2,1)S(1)}, bf16[192,1536]{1,0:T(8,128)(2,1)S(1)}, u32[]{:S(2)}, u32[]{:S(2)}) collective-permute-start(bf16[192,1536]{1,0:T(8,128)(2,1)S(1)} %get-tuple-element.332), channel_id=1, source_target_pairs={{0,16},{4,20},{8,24},{12,28},{16,0},{20,4},{24,8},{28,12},{1,17},{... | collective-permute-start | bytes 1769480 | tf_op jit(solution)/shard_map/ppermute | solution.py:716
  138.7 14.9 %collective-permute-start.46 = (bf16[96,1536]{1,0:T(8,128)(2,1)S(1)}, bf16[96,1536]{1,0:T(8,128)(2,1)S(1)}, u32[]{:S(2)}, u32[]{:S(2)}) collective-permute-start(bf16[96,1536]{1,0:T(8,128)(2,1)S(1)} %get-tuple-element.335), channel_id=1, source_target_pairs={{0,1},{1,0},{2,3},{3,2},{4,5},{5,4},{6,7},{7,6},{8,9},{9,8},{10,11... | collective-permute-start | bytes 884744 | tf_op jit(solution)/shard_map/ppermute | solution.py:716
  147.9 13.2 %collective-permute-start.47 = (bf16[112,1536]{1,0:T(8,128)(2,1)S(1)}, bf16[112,1536]{1,0:T(8,128)(2,1)S(1)}, u32[]{:S(2)}, u32[]{:S(2)}) collective-permute-start(bf16[112,1536]{1,0:T(8,128)(2,1)S(1)} %get-tuple-element.338), channel_id=1, source_target_pairs={{0,16},{4,20},{8,24},{12,28},{16,0},{20,4},{24,8},{28,12},{1,17},{... | collective-permute-start | bytes 1032200 | tf_op jit(solution)/shard_map/ppermute | solution.py:716
  148.5 12.5 %collective-permute-start.48 = (bf16[96,1536]{1,0:T(8,128)(2,1)S(1)}, bf16[96,1536]{1,0:T(8,128)(2,1)S(1)}, u32[]{:S(2)}, u32[]{:S(2)}) collective-permute-start(bf16[96,1536]{1,0:T(8,128)(2,1)S(1)} %get-tuple-element.340), channel_id=1, source_target_pairs={{0,8},{4,12},{8,0},{12,4},{16,24},{20,28},{24,16},{28,20},{1,9},{5... | collective-permute-start | bytes 884744 | tf_op jit(solution)/shard_map/ppermute | solution.py:716
  152.0 12.6 %collective-permute-start.50 = (bf16[96,768]{1,0:T(8,128)(2,1)S(1)}, bf16[96,768]{1,0:T(8,128)(2,1)S(1)}, u32[]{:S(2)}, u32[]{:S(2)}) collective-permute-start(bf16[96,768]{1,0:T(8,128)(2,1)S(1)} %add.16.own), channel_id=1, source_target_pairs={{0,1},{1,0},{2,3},{3,2},{4,5},{5,4},{6,7},{7,6},{8,9},{9,8},{10,11... | collective-permute-start | bytes 442376 | tf_op jit(solution)/shard_map/ppermute | solution.py:716
  167.6 13.6 %collective-permute-start.55 = (bf16[96,1664]{1,0:T(8,128)(2,1)S(1)}, bf16[96,1664]{1,0:T(8,128)(2,1)S(1)}, u32[]{:S(2)}, u32[]{:S(2)}) collective-permute-start(bf16[96,1664]{1,0:T(8,128)(2,1)S(1)} %get-tuple-element.356), channel_id=1, source_target_pairs={{0,1},{1,0},{2,3},{3,2},{4,5},{5,4},{6,7},{7,6},{8,9},{9,8},{10,11... | collective-permute-start | bytes 958472 | tf_op jit(solution)/shard_map/ppermute | solution.py:716
  168.3 13.5 %collective-permute-start.57 = (bf16[48,1536]{1,0:T(8,128)(2,1)S(1)}, bf16[48,1536]{1,0:T(8,128)(2,1)S(1)}, u32[]{:S(2)}, u32[]{:S(2)}) collective-permute-start(bf16[48,1536]{1,0:T(8,128)(2,1)S(1)} %add.17.own), channel_id=1, source_target_pairs={{0,2},{1,3},{2,0},{3,1},{4,6},{5,7},{6,4},{7,5},{8,10},{9,11},{10,... | collective-permute-start | bytes 442376 | tf_op jit(solution)/shard_map/ppermute | solution.py:716
  171.9 14.3 %collective-permute-start.56 = (bf16[48,1536]{1,0:T(8,128)(2,1)S(1)}, bf16[48,1536]{1,0:T(8,128)(2,1)S(1)}, u32[]{:S(2)}, u32[]{:S(2)}) collective-permute-start(bf16[48,1536]{1,0:T(8,128)(2,1)S(1)} %add.17.own), channel_id=1, source_target_pairs={{0,1},{1,0},{2,3},{3,2},{4,5},{5,4},{6,7},{7,6},{8,9},{9,8},{10,11... | collective-permute-start | bytes 442376 | tf_op jit(solution)/shard_map/ppermute | solution.py:716
  (57 other events, 443.2 us)
